TPU v7x, 32 devices: a whole 2x2x4 slice. The times are simulated.
32 devices in a mesh: fsdp: 4 (over y, x), blk: 8 (over z, core).
Axes of the slice: x: 2, y: 2, z: 4, core: 2. Of those that a mesh axis runs over, the one named last changes fastest.
Arguments:
- inputs: bfloat16 [8192, 1152], P(('fsdp', 'blk')), may hold values from -6 to 6
- segments: int32 [4, 2048], P('fsdp'), may hold values from 0 to 2, as said below
- cotangent: bfloat16 [8192, 1152], P(('fsdp', 'blk')), may hold values from -6 to 6
- norm_gain_rows: bfloat16 [2, 1152], P(None, ('fsdp', 'blk')), may hold values from 0.5 to 1.5
- query_key_value_weight: bfloat16 [1152, 1536], P(('fsdp', 'blk')), may hold values from -0.1875 to 0.1875
- output_weight: bfloat16 [1024, 1152], P(('fsdp', 'blk')), may hold values from -1.5 to 1.5
- gate_up_weight: bfloat16 [1152, 13824], P(('fsdp', 'blk')), may hold values from -0.1875 to 0.1875
- down_weight: bfloat16 [6912, 1152], P(('fsdp', 'blk')), may hold values from -0.078125 to 0.078125
- adapter_query_down: bfloat16 [2, 1152, 256], P(None, ('fsdp', 'blk')), may hold values from -0.1875 to 0.1875
- adapter_query_lift: bfloat16 [2, 256, 1536], P(None, ('fsdp', 'blk')), may hold values from -0.1875 to 0.1875
- adapter_output_down: bfloat16 [2, 1024, 256], P(None, ('fsdp', 'blk')), may hold values from -1.5 to 1.5
- adapter_output_lift: bfloat16 [2, 256, 1152], P(None, ('fsdp', 'blk')), may hold values from -0.1875 to 0.1875
Outputs:
- result: bfloat16 [8192, 1152], P(('fsdp', 'blk'))
- d_inputs: float32 [8192, 1152], P(('fsdp', 'blk'))
- d_norm_gains: float32 [2, 1152], P(None, ('fsdp', 'blk'))
- d_w_qkv: float32 [1152, 1536], P(('fsdp', 'blk'))
- d_w_out: float32 [1024, 1152], P(('fsdp', 'blk'))
- d_w_gate_up: float32 [1152, 13824], P(('fsdp', 'blk'))
- d_w_down: float32 [6912, 1152], P(('fsdp', 'blk'))
- d_lora_qkv_in: float32 [2, 1152, 256], P(None, ('fsdp', 'blk'))
- d_lora_qkv_up: float32 [2, 256, 1536], P(None, ('fsdp', 'blk'))
- d_lora_out_in: float32 [2, 1024, 256], P(None, ('fsdp', 'blk'))
- d_lora_out_up: float32 [2, 256, 1152], P(None, ('fsdp', 'blk'))
Inputs may be any that keep to these rules, and one draw needn't show every extreme that they name: `segments`: each row holds document numbers 0, 1, 2 in order, each document nonempty; document 1 begins within the first 256 tokens of the row and ends within its last 256 tokens.
All inputs are finite; a program needn't handle non-finite values.
Results may differ from a plain program's by a relative error of at most 0.038.
Values may be sent and summed in bfloat16 or wider, within the bound.
No kernel may reach another device: no remote copies, remote signals or barrier semaphores. Data moves between devices by JAX's collectives and lax.ppermute only.
A program may use at most 448 MiB of HBM per device.

v0:
```python
import math

import jax
import jax.numpy as jnp
from jax import lax
from jax.sharding import PartitionSpec as P

H = 4
HD = 256


EPS = 1e-06
NEG = -1e30
ROPE_BASE = 10000.0


def matmul(left_side, right_side):
    return jnp.dot(left_side, right_side, preferred_element_type=jnp.float32)


def matmul_nt(left_side, right_side):
    return lax.dot_general(
        left_side, right_side, (((1,), (1,)), ((), ())), preferred_element_type=jnp.float32
    )


def matmul_tn(left_side, right_side):
    return lax.dot_general(
        left_side, right_side, (((0,), (0,)), ((), ())), preferred_element_type=jnp.float32
    )


def rounded(values):
    return values.astype(jnp.bfloat16)


def norm_rows(values, gain_row):
    return values * lax.rsqrt(jnp.mean(values * values, axis=-1, keepdims=True) + EPS) * gain_row


def rotate(values, cosine_table, sine_table):
    halfway = values.shape[-1] // 2
    first_half = values[..., :halfway]
    second_half = values[..., halfway:]
    return jnp.concatenate(
        [
            first_half * cosine_table - second_half * sine_table,
            second_half * cosine_table + first_half * sine_table,
        ],
        axis=-1,
    )


def angles_of(segrow):
    places = jnp.arange(segrow.shape[0], dtype=jnp.int32)
    previous = jnp.concatenate([segrow[:1] - 1, segrow[:-1]])
    starts = lax.cummax(jnp.where(segrow != previous, places, 0), axis=0)
    offsets = (places - starts).astype(jnp.float32)
    frequency = jnp.exp(jnp.arange(HD // 2, dtype=jnp.float32) * (-2.0 * math.log(ROPE_BASE) / HD))
    turned = offsets[:, None] * frequency[None, :]
    return (jnp.cos(turned), jnp.sin(turned))


def allowed_pairs(segrow, query_segs, query_places, key_count):
    key_places = jnp.arange(key_count, dtype=jnp.int32)
    return (query_segs[:, None] == segrow[None, :]) & (key_places[None, :] <= query_places[:, None])


def attention_forward(queries, key_rows, value_rows, segrow, query_places):
    query_segs = jnp.take(segrow, query_places)
    row_count = queries.shape[0]

    def fold_step(carried, pieces, first_row):
        running_max, running_sum, weighted = carried
        key_piece, value_piece = pieces
        allowed = allowed_pairs(segrow, query_segs, query_places, key_piece.shape[0])
        scores = matmul_nt(queries, key_piece)
        new_max = jnp.maximum(
            running_max, jnp.max(jnp.where(allowed, scores, NEG), axis=1, keepdims=True)
        )
        probabilities = jnp.where(allowed, jnp.exp(scores - new_max), 0.0)
        running_sum = jnp.sum(probabilities, axis=1, keepdims=True)
        weighted = matmul(rounded(probabilities), value_piece)
        return (new_max, running_sum, weighted)

    initial = (
        jnp.full((row_count, 1), NEG, jnp.float32),
        jnp.zeros((row_count, 1), jnp.float32),
        jnp.zeros((row_count, HD), jnp.float32),
    )
    running_max, running_sum, weighted = fold_step(
        initial,
        (
            lax.all_gather(key_rows, "blk", axis=0, tiled=True),
            lax.all_gather(value_rows, "blk", axis=0, tiled=True),
        ),
        jnp.int32(0),
    )
    return (weighted / running_sum, running_max + jnp.log(running_sum))


def attention_backward(
    queries, key_rows, value_rows, segrow, query_places, grad_rows, log_total, delta
):
    query_segs = jnp.take(segrow, query_places)
    row_count = queries.shape[0]
    seq_len = segrow.shape[0]

    def fold_step(carried, pieces, first_row):
        key_piece, value_piece = pieces
        allowed = allowed_pairs(segrow, query_segs, query_places, key_piece.shape[0])
        scores = matmul_nt(queries, key_piece)
        probabilities = jnp.where(allowed, jnp.exp(scores - log_total), 0.0)
        grad_probs = matmul_nt(grad_rows, value_piece)
        grad_scores = rounded(probabilities * (grad_probs - delta))
        grad_q = matmul(grad_scores, key_piece)
        grad_k_all = matmul_tn(grad_scores, queries)
        grad_v_all = matmul_tn(rounded(probabilities), grad_rows)
        return (grad_q, grad_k_all, grad_v_all)

    initial = (
        jnp.zeros((row_count, HD), jnp.float32),
        jnp.zeros((seq_len, HD), jnp.float32),
        jnp.zeros((seq_len, HD), jnp.float32),
    )
    grad_q, grad_k_all, grad_v_all = fold_step(
        initial,
        (
            lax.all_gather(key_rows, "blk", axis=0, tiled=True),
            lax.all_gather(value_rows, "blk", axis=0, tiled=True),
        ),
        jnp.int32(0),
    )
    grad_k, grad_v = (
        lax.psum_scatter(
            grad_k_all.astype(jnp.bfloat16), "blk", scatter_dimension=0, tiled=True
        ).astype(jnp.float32),
        lax.psum_scatter(
            grad_v_all.astype(jnp.bfloat16), "blk", scatter_dimension=0, tiled=True
        ).astype(jnp.float32),
    )
    return (grad_q, grad_k, grad_v)


def forward_loop(residual, loop_index, weights, context, finish):
    segrow, query_places, cosine_table, sine_table = context
    (
        gain_rows,
        query_key_value_weight,
        output_weight,
        gate_up_weight,
        down_weight,
        qkv_in_all,
        qkv_up_all,
        out_in_all,
        out_up_all,
    ) = weights
    qkv_in = qkv_in_all[loop_index]
    qkv_up = qkv_up_all[loop_index]
    out_in = out_in_all[loop_index]
    out_up = out_up_all[loop_index]
    gain_rows = gain_rows.astype(jnp.float32)
    tokens = residual.shape[0]
    width_q = H * HD
    normed_b = rounded(norm_rows(residual, gain_rows[0]))
    low_rank_b = rounded(matmul(normed_b, qkv_in))
    joined = matmul(normed_b, query_key_value_weight) + matmul(low_rank_b, qkv_up)
    query_heads = joined[:, :width_q].reshape(tokens, H, HD).transpose(1, 0, 2)
    queries = rounded(rotate(query_heads, cosine_table, sine_table) * HD ** (-0.5)).reshape(
        H * tokens, HD
    )
    key_rows = rounded(rotate(joined[:, width_q : width_q + HD], cosine_table, sine_table))
    value_rows = rounded(joined[:, width_q + HD :])
    mixed_rows, log_total = attention_forward(queries, key_rows, value_rows, segrow, query_places)
    mixed_b = rounded(mixed_rows.reshape(H, tokens, HD).transpose(1, 0, 2).reshape(tokens, width_q))
    side_b = rounded(matmul(mixed_b, out_in))
    middle = residual + (matmul(mixed_b, output_weight) + matmul(side_b, out_up))
    normed_ff_b = rounded(norm_rows(middle, gain_rows[1]))
    gate_up = matmul(normed_ff_b, gate_up_weight)
    ff_width = gate_up_weight.shape[1] // 2
    hidden_b = rounded(jax.nn.gelu(gate_up[:, :ff_width], approximate=True) * gate_up[:, ff_width:])
    cache = (
        residual,
        normed_b,
        low_rank_b,
        queries,
        key_rows,
        value_rows,
        mixed_rows,
        log_total,
        mixed_b,
        side_b,
        middle,
        normed_ff_b,
        gate_up,
        hidden_b,
    )
    if not finish:
        return (middle, cache)
    return (middle + matmul(hidden_b, down_weight), cache)


def accumulate(totals, index, term):
    if totals is None:
        return term
    return totals[index] + term


def accumulate_adapter(totals, index, term):
    if totals is None:
        return term[:, None]
    return jnp.concatenate([term[:, None], totals[index]], axis=1)


def backward_loop(cache, grad_result, loop_index, weights, context, totals):
    segrow, query_places, cosine_table, sine_table = context
    (
        residual,
        normed_b,
        low_rank_b,
        queries,
        key_rows,
        value_rows,
        mixed_rows,
        log_total,
        mixed_b,
        side_b,
        middle,
        normed_ff_b,
        gate_up,
        hidden_b,
    ) = cache
    (
        gain_rows,
        query_key_value_weight,
        output_weight,
        gate_up_weight,
        down_weight,
        qkv_in_all,
        qkv_up_all,
        out_in_all,
        out_up_all,
    ) = weights
    qkv_in = qkv_in_all[loop_index]
    qkv_up = qkv_up_all[loop_index]
    out_in = out_in_all[loop_index]
    out_up = out_up_all[loop_index]
    gain_rows = gain_rows.astype(jnp.float32)
    tokens = residual.shape[0]
    width_q = H * HD
    ff_width = gate_up_weight.shape[1] // 2
    grad_ff_b = rounded(grad_result)
    grad_hidden = matmul_nt(grad_ff_b, down_weight)
    down_term = accumulate(totals, 4, matmul_tn(hidden_b, grad_ff_b))

    def activate(gate_in, up_in):
        return jax.nn.gelu(gate_in, approximate=True) * up_in

    unused, pullback = jax.vjp(activate, gate_up[:, :ff_width], gate_up[:, ff_width:])
    grad_gate, grad_up = pullback(grad_hidden)
    grad_gate_up_b = rounded(jnp.concatenate([grad_gate, grad_up], axis=1))
    gate_up_term = accumulate(totals, 3, matmul_tn(normed_ff_b, grad_gate_up_b))
    grad_normed_ff = matmul_nt(grad_gate_up_b, gate_up_weight)
    unused, norm_pull = jax.vjp(norm_rows, middle, gain_rows[1])
    grad_middle_norm, gain_grad_ff = norm_pull(grad_normed_ff)
    grad_middle = grad_result + grad_middle_norm
    grad_branch_b = rounded(grad_middle)
    grad_side_b = rounded(matmul_nt(grad_branch_b, out_up))
    grad_mixed_b = rounded(matmul_nt(grad_branch_b, output_weight) + matmul_nt(grad_side_b, out_in))
    out_term = accumulate(totals, 2, matmul_tn(mixed_b, grad_branch_b))
    grad_rows = grad_mixed_b.reshape(tokens, H, HD).transpose(1, 0, 2).reshape(H * tokens, HD)
    delta = jnp.sum(grad_rows.astype(jnp.float32) * mixed_rows, axis=1, keepdims=True)
    grad_q, grad_k, grad_v = attention_backward(
        queries, key_rows, value_rows, segrow, query_places, grad_rows, log_total, delta
    )
    grad_query_heads = rotate(grad_q.reshape(H, tokens, HD), cosine_table, -sine_table) * HD ** (
        -0.5
    )
    grad_joined_b = rounded(
        jnp.concatenate(
            [
                grad_query_heads.transpose(1, 0, 2).reshape(tokens, width_q),
                rotate(grad_k, cosine_table, -sine_table),
                grad_v,
            ],
            axis=1,
        )
    )
    grad_low_rank_b = rounded(matmul_nt(grad_joined_b, qkv_up))
    grad_normed = matmul_nt(grad_joined_b, query_key_value_weight) + matmul_nt(
        grad_low_rank_b, qkv_in
    )
    unused, norm_pull = jax.vjp(norm_rows, residual, gain_rows[0])
    grad_state_norm, gain_grad_attn = norm_pull(grad_normed)
    grad_residual = grad_middle + grad_state_norm
    terms = (
        accumulate(totals, 0, jnp.stack([gain_grad_attn, gain_grad_ff], axis=1)),
        accumulate(totals, 1, matmul_tn(normed_b, grad_joined_b)),
        out_term,
        gate_up_term,
        down_term,
        accumulate_adapter(totals, 5, matmul_tn(normed_b, grad_low_rank_b)),
        accumulate_adapter(totals, 6, matmul_tn(low_rank_b, grad_joined_b)),
        accumulate_adapter(totals, 7, matmul_tn(mixed_b, grad_side_b)),
        accumulate_adapter(totals, 8, matmul_tn(side_b, grad_branch_b)),
    )
    return (grad_residual, terms)


def finish_layout(reduced):
    return (
        (jnp.transpose(reduced[0]),)
        + tuple(reduced[1:5])
        + tuple((jnp.transpose(reduced[index], (1, 0, 2)) for index in range(5, 9)))
    )


def per_device(
    inputs,
    segments,
    cotangent,
    norm_gain_rows,
    query_key_value_weight,
    output_weight,
    gate_up_weight,
    down_weight,
    adapter_query_down,
    adapter_query_lift,
    adapter_output_down,
    adapter_output_lift,
):
    weights = (
        lax.all_gather(norm_gain_rows, ("fsdp", "blk"), axis=1, tiled=True),
        lax.all_gather(query_key_value_weight, ("fsdp", "blk"), axis=0, tiled=True),
        lax.all_gather(output_weight, ("fsdp", "blk"), axis=0, tiled=True),
        lax.all_gather(gate_up_weight, ("fsdp", "blk"), axis=0, tiled=True),
        lax.all_gather(down_weight, ("fsdp", "blk"), axis=0, tiled=True),
        lax.all_gather(adapter_query_down, ("fsdp", "blk"), axis=1, tiled=True),
        lax.all_gather(adapter_query_lift, ("fsdp", "blk"), axis=1, tiled=True),
        lax.all_gather(adapter_output_down, ("fsdp", "blk"), axis=1, tiled=True),
        lax.all_gather(adapter_output_lift, ("fsdp", "blk"), axis=1, tiled=True),
    )
    tokens = inputs.shape[0]
    segrow = segments[0]
    position = lax.axis_index("blk")
    cosine_all, sine_all = angles_of(segrow)
    cosine_table = lax.dynamic_slice_in_dim(cosine_all, position * tokens, tokens, 0)
    sine_table = lax.dynamic_slice_in_dim(sine_all, position * tokens, tokens, 0)
    query_places = jnp.tile(position * tokens + jnp.arange(tokens, dtype=jnp.int32), H)
    context = (segrow, query_places, cosine_table, sine_table)
    residual_zero = inputs.astype(jnp.float32)
    residual_one, unused = forward_loop(residual_zero, 0, weights, context, True)
    result, cache_two = forward_loop(residual_one, 1, weights, context, True)
    grad_one, terms_two = backward_loop(
        cache_two, cotangent.astype(jnp.float32), 1, weights, context, None
    )
    unused, cache_one = forward_loop(residual_zero, 0, weights, context, False)
    grad_inputs, merged = backward_loop(cache_one, grad_one, 0, weights, context, terms_two)
    reduced = (
        lax.psum_scatter(merged[0], ("fsdp", "blk"), scatter_dimension=0, tiled=True),
        lax.psum_scatter(merged[1], ("fsdp", "blk"), scatter_dimension=0, tiled=True),
        lax.psum_scatter(merged[2], ("fsdp", "blk"), scatter_dimension=0, tiled=True),
        lax.psum_scatter(merged[3], ("fsdp", "blk"), scatter_dimension=0, tiled=True),
        lax.psum_scatter(merged[4], ("fsdp", "blk"), scatter_dimension=0, tiled=True),
        lax.psum_scatter(merged[5], ("fsdp", "blk"), scatter_dimension=0, tiled=True),
        lax.psum_scatter(merged[6], ("fsdp", "blk"), scatter_dimension=0, tiled=True),
        lax.psum_scatter(merged[7], ("fsdp", "blk"), scatter_dimension=0, tiled=True),
        lax.psum_scatter(merged[8], ("fsdp", "blk"), scatter_dimension=0, tiled=True),
    )
    reduced = finish_layout(reduced)
    return (
        rounded(result),
        grad_inputs,
        reduced[0],
        reduced[1],
        reduced[2],
        reduced[3],
        reduced[4],
        reduced[5],
        reduced[6],
        reduced[7],
        reduced[8],
    )


def solution(mesh):
    in_specs = (
        P(("fsdp", "blk"), None),
        P("fsdp", None),
        P(("fsdp", "blk"), None),
        P(None, ("fsdp", "blk")),
        P(("fsdp", "blk"), None),
        P(("fsdp", "blk"), None),
        P(("fsdp", "blk"), None),
        P(("fsdp", "blk"), None),
        P(None, ("fsdp", "blk"), None),
        P(None, ("fsdp", "blk"), None),
        P(None, ("fsdp", "blk"), None),
        P(None, ("fsdp", "blk"), None),
    )
    out_specs = (
        P(("fsdp", "blk"), None),
        P(("fsdp", "blk"), None),
        P(None, ("fsdp", "blk")),
        P(("fsdp", "blk"), None),
        P(("fsdp", "blk"), None),
        P(("fsdp", "blk"), None),
        P(("fsdp", "blk"), None),
        P(None, ("fsdp", "blk"), None),
        P(None, ("fsdp", "blk"), None),
        P(None, ("fsdp", "blk"), None),
        P(None, ("fsdp", "blk"), None),
    )
    return jax.shard_map(
        per_device, mesh=mesh, in_specs=in_specs, out_specs=out_specs, check_vma=False
    )
```

profile of v0, /device:TPU:0, one launch (start us, length us, event | category | flops | bytes accessed | tf_op | source)
XLA Modules:
  0.0 3058.8 jit_solution(4677318907398191048)
XLA Ops:
  9.4 43.2 %all-gather = bf16[32,36,2]{1,2,0:T(2,128)(2,1)S(1)} all-gather(bf16[1,36,2]{1,2,0:T(2,128)(2,1)} %bitcast.283), channel_id=1, replica_groups=mesh['fsdp'=4,'blk'=8] {'fsdp','blk'}, dimensions={0}, use_global_device_ids=true | all-gather | bytes 4752 | tf_op jit(solution)/shard_map/all_gather | solution.py:333
  58.9 9.0 all-gather.16.cloned.1.call-done
  72.8 58.5 %all-gather.36.cloned.1.call-done = bf16[32,36,1536]{2,1,0:T(8,128)(2,1)} async-done(((bf16[1,36,1536]{2,1,0:T(8,128)(2,1)}), bf16[32,36,1536]{2,1,0:T(8,128)(2,1)}) %all-gather.36.cloned.1.call-update) | async-done | bytes 3538960 | tf_op jit(solution)/shard_map/all_gather | solution.py:334
  141.3 46.8 %all-gather.18.cloned.1.call-done = bf16[2,256,1536]{2,1,0:T(8,128)(2,1)} async-done(((bf16[2,8,1536]{2,1,0:T(8,128)(2,1)}), bf16[2,256,1536]{2,1,0:T(8,128)(2,1)}) %all-gather.18.cloned.1.call-update) | async-done | bytes 1572880 | tf_op jit(solution)/shard_map/all_gather | solution.py:339
  197.5 6.2 gather_fusion
  204.0 9.3 all-gather.20.cloned.1.call-done
  223.3 13.7 all-gather.22.cloned.1.call-done
  237.0 5.9 fusion.126
  243.1 50.2 %all-gather.26.cloned.1.call-done = bf16[2,1024,256]{2,1,0:T(8,128)(2,1)} async-done(((bf16[2,32,256]{2,1,0:T(8,128)(2,1)}), bf16[2,1024,256]{2,1,0:T(8,128)(2,1)}) %all-gather.26.cloned.1.call-update) | async-done | bytes 1048592 | tf_op jit(solution)/shard_map/all_gather | solution.py:340
  294.7 58.0 %all-gather.24.cloned.1.call-done = bf16[1024,1152]{1,0:T(8,128)(2,1)} async-done(((bf16[32,1152]{1,0:T(8,128)(2,1)}), bf16[1024,1152]{1,0:T(8,128)(2,1)}) %all-gather.24.cloned.1.call-update) | async-done | bytes 2359312 | tf_op jit(solution)/shard_map/all_gather | solution.py:335
  355.3 53.5 %all-gather.28.cloned.1.call-done = bf16[2,256,1152]{2,1,0:T(8,128)(2,1)} async-done(((bf16[2,8,1152]{2,1,0:T(8,128)(2,1)}), bf16[2,256,1152]{2,1,0:T(8,128)(2,1)}) %all-gather.28.cloned.1.call-update) | async-done | bytes 1179664 | tf_op jit(solution)/shard_map/all_gather | solution.py:341
  410.3 204.1 %all-gather.38.cloned.1.call-done = bf16[32,36,13824]{2,1,0:T(8,128)(2,1)} async-done(((bf16[1,36,13824]{2,1,0:T(8,128)(2,1)}), bf16[32,36,13824]{2,1,0:T(8,128)(2,1)}) %all-gather.38.cloned.1.call-update) | async-done | bytes 31850512 | tf_op jit(solution)/shard_map/all_gather | solution.py:336
  614.5 29.2 reshape.262
  643.7 18.4 fusion.107
  662.0 7.8 multiply_convert_fusion.5
  669.9 56.6 %all-gather.30.cloned.1.call-done = bf16[6912,1152]{1,0:T(8,128)(2,1)} async-done(((bf16[216,1152]{1,0:T(8,128)(2,1)}), bf16[6912,1152]{1,0:T(8,128)(2,1)}) %all-gather.30.cloned.1.call-update) | async-done | bytes 15925264 | tf_op jit(solution)/shard_map/all_gather | solution.py:337
  726.4 10.5 multiply_reduce_fusion.7
  745.6 16.2 all-gather.32.cloned.1.call-done
  769.8 15.9 all-gather.34.cloned.1.call-done
  785.7 6.1 fusion.127
  798.1 18.1 fusion.108
  816.2 18.0 fusion.16
  834.3 19.3 multiply_reduce_fusion.1
  860.3 5.8 multiply_convert_fusion.1
  870.7 7.5 fusion.45
  886.4 16.1 reduce-scatter.17.cloned.1.call-done
  908.2 27.0 reduce-scatter.19.cloned.1.call-done
  945.4 17.6 fusion.9
  963.0 19.4 multiply_reduce_fusion
  989.4 5.8 multiply_convert_fusion
  999.7 7.0 fusion.48
  1012.8 17.6 reduce-scatter.21.cloned.1.call-done
  1031.7 31.6 %reduce-scatter.23.cloned.1.call-done = bf16[256,256]{1,0:T(8,128)(2,1)} async-done(((bf16[2048,256]{1,0:T(8,128)(2,1)}), bf16[256,256]{1,0:T(8,128)(2,1)}) %reduce-scatter.23.cloned.1.call-update) | async-done | bytes 131088 | tf_op jit(solution)/shard_map/reduce_scatter | solution.py:138
  1067.2 7.6 copy.91
  1093.0 14.7 fusion.136
  1107.7 26.3 fusion.24
  1134.1 25.0 convolution_add_fusion.1
  1160.4 43.7 %convolution_add_fusion = f32[1152,13824]{1,0:T(8,128)} fusion(f32[1152,13824]{1,0:T(8,128)} %fusion.24, bf16[256,6912]{1,0:T(8,128)(2,1)} %get-tuple-element.62, bf16[256,6912]{1,0:T(8,128)(2,1)} %get-tuple-element.61, f32[256,1152]{1,0:T(8,128)S(1)} %copy-done.14, f32[1152]{0:T(1024)S(1)} %get-tuple-element.53, f32[256]{0:T(256)S(1)} %copy-done.108), kind=kOutput, calls=%fused_computation.1 | convolution fusion | flops 8184692736 | bytes 135665152 | tf_op jit(solution)/shard_map/dot_general | solution.py:28
  1204.1 1114.0 %fusion.1 = f32[48,13824]{1,0:T(8,128)S(1)} fusion(f32[1152,13824]{1,0:T(8,128)} %convolution_add_fusion), kind=kCustom, calls=%all-reduce-scatter.1 | all-reduce-scatter fusion | flops 21233664 | bytes 66355200
  2322.6 9.3 collective-permute-start.4
  2340.3 130.7 %fusion = f32[40,1536]{1,0:T(8,128)S(1)} fusion(f32[1152,1536]{1,0:T(8,128)} %convolution_add_fusion.2), kind=kCustom, calls=%all-reduce-scatter | all-reduce-scatter fusion | flops 1966081 | bytes 7323648
  2484.9 35.9 %collective-permute-start.6 = (f32[48,13824]{1,0:T(8,128)S(1)}, f32[48,13824]{1,0:T(8,128)}, u32[]{:S(2)}, u32[]{:S(2)}) collective-permute-start(f32[48,13824]{1,0:T(8,128)S(1)} %fusion.1), channel_id=1, source_target_pairs={{0,3},{1,4},{2,5},{3,6},{4,7},{5,8},{6,9},{7,10},{8,11},{9,12},{10... | collective-permute-start | bytes 7962632
  2520.9 6.7 collective-permute-start.7
  2527.6 7.1 collective-permute-start.8
  2537.5 12.4 fusion.44
  2553.5 384.7 %all-reduce = f32[1152,2]{0,1:T(2,128)S(1)} all-reduce(f32[1152,2]{0,1:T(2,128)S(1)} %maximum_add_fusion), channel_id=6, replica_groups=mesh['fsdp'=4,'blk'=8] {'fsdp','blk'}, use_global_device_ids=true, to_apply=%region_24.26.clone | all-reduce | flops 2304 | bytes 18432
  2942.5 7.4 concatenate.85
  2951.6 95.1 %concatenate.86 = f32[420,13824]{1,0:T(8,128)} concatenate(f32[36,13824]{1,0:T(8,128)} %collective-permute-done.11, f32[48,13824]{1,0:T(8,128)} %collective-permute-done.10, f32[48,13824]{1,0:T(8,128)} %collective-permute-done.9, f32[48,13824]{1,0:T(8,128)} %collective-permute-done.8, f32[48,13824]{1,0:T(8,128)} %collective-permute-done.7, f32[48,13824]{1,0:T(8,128)} %collective-permute-done.6, ...), dimensions={0} | concatenate | bytes 46448640
  (492 shorter events, 190.6 us)
Async XLA Ops:
  7.2 60.7 %all-gather.16.cloned.1.call-start = ((), (), s32[]{:S(2)}) async-start(), calls=%async_computation.9 | async-start | bytes 1216512 | tf_op jit(solution)/shard_map/all_gather | solution.py:338
  7.9 123.4 %all-gather.36.cloned.1.call-start = ((), (), s32[]{:S(2)}) async-start(), calls=%async_computation.27 | async-start | bytes 4055040 | tf_op jit(solution)/shard_map/all_gather | solution.py:334
  8.7 179.5 %all-gather.18.cloned.1.call-start = ((), (), s32[]{:S(2)}) async-start(), calls=%async_computation.10 | async-start | bytes 1622016 | tf_op jit(solution)/shard_map/all_gather | solution.py:339
  9.4 203.9 %all-gather.20.cloned.1.call-start = ((), (), s32[]{:S(2)}) async-start(), calls=%async_computation.11 | async-start | bytes 1179648 | tf_op jit(solution)/shard_map/all_gather | solution.py:94
  56.0 80.9 %copy-start.59 = (f32[1152]{0:T(1024)}, f32[1152]{0:T(1024)S(1)}, u32[]{:S(2)}) copy-start(f32[1152]{0:T(1024)S(1)} %get-tuple-element.54) | copy-start | bytes 13828
  57.6 686.7 %copy-start.19 = (f32[256,128]{1,0:T(8,128)}, f32[256,128]{1,0:T(8,128)S(1)}, u32[]{:S(2)}) copy-start(f32[256,128]{1,0:T(8,128)S(1)} %get-tuple-element.58) | copy-start | bytes 393220
  58.9 78.1 %copy-start.117 = (f32[256]{0:T(256)}, f32[256]{0:T(256)S(1)}, u32[]{:S(2)}) copy-start(f32[256]{0:T(256)S(1)} %fusion.87) | copy-start | bytes 3076
  72.8 115.4 %copy-start.104 = (bf16[256,256]{1,0:T(8,128)(2,1)}, bf16[256,256]{1,0:T(8,128)(2,1)S(1)}, u32[]{:S(2)}) copy-start(bf16[256,256]{1,0:T(8,128)(2,1)S(1)} %convolution_convert_fusion.7) | copy-start | bytes 393220
  190.7 553.6 %copy-start.9 = (f32[256,128]{1,0:T(8,128)}, f32[256,128]{1,0:T(8,128)S(1)}, u32[]{:S(2)}) copy-start(f32[256,128]{1,0:T(8,128)S(1)} %get-tuple-element.60) | copy-start | bytes 393220
  192.1 44.9 %all-gather.22.cloned.1.call-start = ((), (), s32[]{:S(2)}) async-start(), calls=%async_computation.12 | async-start | bytes 1179648 | tf_op jit(solution)/shard_map/all_gather | solution.py:95
  193.8 99.5 %all-gather.26.cloned.1.call-start = ((), (), s32[]{:S(2)}) async-start(), calls=%async_computation.14 | async-start | bytes 1081344 | tf_op jit(solution)/shard_map/all_gather | solution.py:340
  194.4 158.4 %all-gather.24.cloned.1.call-start = ((), (), s32[]{:S(2)}) async-start(), calls=%async_computation.13 | async-start | bytes 2433024 | tf_op jit(solution)/shard_map/all_gather | solution.py:335
  195.1 213.7 %all-gather.28.cloned.1.call-start = ((), (), s32[]{:S(2)}) async-start(), calls=%async_computation.15 | async-start | bytes 1216512 | tf_op jit(solution)/shard_map/all_gather | solution.py:341
  195.9 418.6 %all-gather.38.cloned.1.call-start = ((), (), s32[]{:S(2)}) async-start(), calls=%async_computation.28 | async-start | bytes 36495360 | tf_op jit(solution)/shard_map/all_gather | solution.py:336
  196.6 529.8 %all-gather.30.cloned.1.call-start = ((), (), s32[]{:S(2)}) async-start(), calls=%async_computation.16 | async-start | bytes 16422912 | tf_op jit(solution)/shard_map/all_gather | solution.py:337
  197.2 564.7 %all-gather.32.cloned.1.call-start = ((), (), s32[]{:S(2)}) async-start(), calls=%async_computation.17 | async-start | bytes 1179648 | tf_op jit(solution)/shard_map/all_gather | solution.py:94
  243.1 112.2 %copy-start.23 = (bf16[4,256,256]{1,2,0:T(8,128)(2,1)}, bf16[4,256,256]{1,2,0:T(8,128)(2,1)S(1)}, u32[]{:S(2)}) copy-start(bf16[4,256,256]{1,2,0:T(8,128)(2,1)S(1)} %copy.77) | copy-start | bytes 1572868
  294.7 115.6 %copy-start.82 = (bf16[256,256]{1,0:T(8,128)(2,1)}, bf16[256,256]{1,0:T(8,128)(2,1)S(1)}, u32[]{:S(2)}) copy-start(bf16[256,256]{1,0:T(8,128)(2,1)S(1)} %convolution_convert_fusion.3) | copy-start | bytes 393220
  410.3 233.4 %copy-start.132 = (f32[256]{0:T(256)}, f32[256]{0:T(256)S(1)}, u32[]{:S(2)}) copy-start(f32[256]{0:T(256)S(1)} %get-tuple-element.86) | copy-start | bytes 3076
  410.3 316.1 %copy-start.13 = (f32[256,1152]{1,0:T(8,128)}, f32[256,1152]{1,0:T(8,128)S(1)}, u32[]{:S(2)}) copy-start(f32[256,1152]{1,0:T(8,128)S(1)} %get-tuple-element.87) | copy-start | bytes 3538948
  410.3 233.3 %copy-start.107 = (f32[256]{0:T(256)}, f32[256]{0:T(256)S(1)}, u32[]{:S(2)}) copy-start(f32[256]{0:T(256)S(1)} %fusion.88) | copy-start | bytes 3076
  741.4 44.3 %all-gather.34.cloned.1.call-start = ((), (), s32[]{:S(2)}) async-start(), calls=%async_computation.18 | async-start | bytes 1179648 | tf_op jit(solution)/shard_map/all_gather | solution.py:95
  744.2 158.3 %reduce-scatter.17.cloned.1.call-start = ((), (), s32[]{:S(2)}) async-start(), calls=%async_computation.19 | async-start | bytes 1179648 | tf_op jit(solution)/shard_map/reduce_scatter | solution.py:135
  870.4 64.8 %reduce-scatter.19.cloned.1.call-start = ((), (), s32[]{:S(2)}) async-start(), calls=%async_computation.20 | async-start | bytes 1179648 | tf_op jit(solution)/shard_map/reduce_scatter | solution.py:138
  878.2 152.2 %reduce-scatter.21.cloned.1.call-start = ((), (), s32[]{:S(2)}) async-start(), calls=%async_computation.21 | async-start | bytes 1179648 | tf_op jit(solution)/shard_map/reduce_scatter | solution.py:135
  999.7 63.5 %reduce-scatter.23.cloned.1.call-start = ((), (), s32[]{:S(2)}) async-start(), calls=%async_computation.22 | async-start | bytes 1179648 | tf_op jit(solution)/shard_map/reduce_scatter | solution.py:138
  1006.8 2043.2 %all-reduce.9.cloned.1.call-start = ((), (), s32[]{:S(2)}) async-start(), calls=%async_computation.29 | async-start | bytes 4718592
  1074.9 1976.6 %reduce-scatter.31.cloned.1.call-start = ((), (), s32[]{:S(2)}) async-start(), calls=%async_computation.26 | async-start | bytes 2433024 | tf_op jit(solution)/shard_map/reduce_scatter | solution.py:368
  1078.3 1973.2 %reduce-scatter.29.cloned.1.call-start = ((), (), s32[]{:S(2)}) async-start(), calls=%async_computation.25 | async-start | bytes 2162688 | tf_op jit(solution)/shard_map/reduce_scatter | solution.py:367
  1083.5 1968.0 %reduce-scatter.27.cloned.1.call-start = ((), (), s32[]{:S(2)}) async-start(), calls=%async_computation.24 | async-start | bytes 3244032 | tf_op jit(solution)/shard_map/reduce_scatter | solution.py:366
  1087.7 1963.9 %reduce-scatter.25.cloned.1.call-start = ((), (), s32[]{:S(2)}) async-start(), calls=%async_computation.23 | async-start | bytes 4866048 | tf_op jit(solution)/shard_map/reduce_scatter | solution.py:362
  1092.0 1959.6 %reduce-scatter.33.cloned.1.call-start = ((), (), s32[]{:S(2)}) async-start(), calls=%async_computation.30 | async-start | bytes 32845824
  2319.7 207.9 %collective-permute-start.10 = (f32[48,13824]{1,0:T(8,128)S(1)}, f32[48,13824]{1,0:T(8,128)}, u32[]{:S(2)}, u32[]{:S(2)}) collective-permute-start(f32[48,13824]{1,0:T(8,128)S(1)} %fusion.1), channel_id=1, source_target_pairs={{0,7},{1,8},{2,9},{3,10},{4,11},{5,12},{6,13},{7,14},{8,15},{9,16}... | collective-permute-start | bytes 7962632
  2322.6 212.0 %collective-permute-start.4 = (f32[48,13824]{1,0:T(8,128)S(1)}, f32[48,13824]{1,0:T(8,128)}, u32[]{:S(2)}, u32[]{:S(2)}) collective-permute-start(f32[48,13824]{1,0:T(8,128)S(1)} %fusion.1), channel_id=1, source_target_pairs={{0,1},{1,2},{2,3},{3,4},{4,5},{5,6},{6,7},{7,8},{8,9},{9,10},{10,1... | collective-permute-start | bytes 7962632
  2332.0 143.4 %collective-permute-start.11 = (f32[36,13824]{1,0:T(8,128)}, f32[36,13824]{1,0:T(8,128)}, u32[]{:S(2)}, u32[]{:S(2)}) collective-permute-start(f32[36,13824]{1,0:T(8,128)} %slice.238), channel_id=1, source_target_pairs={{0,8},{1,9},{2,10},{3,11},{4,12},{5,13},{6,14},{7,15},{8,16},{9,17... | collective-permute-start | bytes 5971976
  2471.0 6.4 collective-permute-start.3
  2472.3 8.6 collective-permute-start
  2475.4 9.6 collective-permute-start.1
  2477.4 43.5 %collective-permute-start.2 = (f32[40,1536]{1,0:T(8,128)S(1)}, f32[40,1536]{1,0:T(8,128)}, u32[]{:S(2)}, u32[]{:S(2)}) collective-permute-start(f32[40,1536]{1,0:T(8,128)S(1)} %fusion), channel_id=1, source_target_pairs={{0,3},{1,4},{2,5},{3,6},{4,7},{5,8},{6,9},{7,10},{8,11},{9,12},{10... | collective-permute-start | bytes 737288
  2480.9 69.2 %copy-start.69 = (bf16[256,256]{0,1:T(8,128)(2,1)S(1)}, bf16[256,256]{0,1:T(8,128)(2,1)}, u32[]{:S(2)}) copy-start(bf16[256,256]{0,1:T(8,128)(2,1)} %copy-done.66) | copy-start | bytes 393220
  2480.9 69.2 %copy-start.96 = (bf16[256,128]{0,1:T(8,128)(2,1)S(1)}, bf16[256,128]{0,1:T(8,128)(2,1)}, u32[]{:S(2)}) copy-start(bf16[256,128]{0,1:T(8,128)(2,1)} %copy-done.93) | copy-start | bytes 196612
  2480.9 69.2 %copy-start.100 = (bf16[256,128]{0,1:T(8,128)(2,1)S(1)}, bf16[256,128]{0,1:T(8,128)(2,1)}, u32[]{:S(2)}) copy-start(bf16[256,128]{0,1:T(8,128)(2,1)} %copy-done.97) | copy-start | bytes 196612
  2480.9 470.7 %collective-permute-start.5 = (f32[48,13824]{1,0:T(8,128)S(1)}, f32[48,13824]{1,0:T(8,128)}, u32[]{:S(2)}, u32[]{:S(2)}) collective-permute-start(f32[48,13824]{1,0:T(8,128)S(1)} %fusion.1), channel_id=1, source_target_pairs={{0,2},{1,3},{2,4},{3,5},{4,6},{5,7},{6,8},{7,9},{8,10},{9,11},{10,... | collective-permute-start | bytes 7962632
  2484.9 466.6 %collective-permute-start.6 = (f32[48,13824]{1,0:T(8,128)S(1)}, f32[48,13824]{1,0:T(8,128)}, u32[]{:S(2)}, u32[]{:S(2)}) collective-permute-start(f32[48,13824]{1,0:T(8,128)S(1)} %fusion.1), channel_id=1, source_target_pairs={{0,3},{1,4},{2,5},{3,6},{4,7},{5,8},{6,9},{7,10},{8,11},{9,12},{10... | collective-permute-start | bytes 7962632
  2520.9 430.7 %collective-permute-start.7 = (f32[48,13824]{1,0:T(8,128)S(1)}, f32[48,13824]{1,0:T(8,128)}, u32[]{:S(2)}, u32[]{:S(2)}) collective-permute-start(f32[48,13824]{1,0:T(8,128)S(1)} %fusion.1), channel_id=1, source_target_pairs={{0,4},{1,5},{2,6},{3,7},{4,8},{5,9},{6,10},{7,11},{8,12},{9,13},{1... | collective-permute-start | bytes 7962632
  2527.6 424.0 %collective-permute-start.8 = (f32[48,13824]{1,0:T(8,128)S(1)}, f32[48,13824]{1,0:T(8,128)}, u32[]{:S(2)}, u32[]{:S(2)}) collective-permute-start(f32[48,13824]{1,0:T(8,128)S(1)} %fusion.1), channel_id=1, source_target_pairs={{0,5},{1,6},{2,7},{3,8},{4,9},{5,10},{6,11},{7,12},{8,13},{9,14},{... | collective-permute-start | bytes 7962632
  2534.7 416.9 %collective-permute-start.9 = (f32[48,13824]{1,0:T(8,128)S(1)}, f32[48,13824]{1,0:T(8,128)}, u32[]{:S(2)}, u32[]{:S(2)}) collective-permute-start(f32[48,13824]{1,0:T(8,128)S(1)} %fusion.1), channel_id=1, source_target_pairs={{0,6},{1,7},{2,8},{3,9},{4,10},{5,11},{6,12},{7,13},{8,14},{9,15},... | collective-permute-start | bytes 7962632
  2551.3 387.5 %copy-start.128 = (f32[256]{0:T(256)S(1)}, f32[256]{0:T(256)}, u32[]{:S(2)}) copy-start(f32[256]{0:T(256)} %copy-done.127) | copy-start | bytes 3076
  (132 other events, 1396.1 us)
Sparse Core Ops, SparseCore 0:
  11.0 56.8 all-gather.15
  70.9 60.3 all-gather.35
  134.3 53.7 all-gather.17
  192.2 21.0 all-gather.19
  215.3 21.6 all-gather.21
  239.9 53.3 all-gather.25
  296.3 56.3 all-gather.23
  355.6 53.0 all-gather.27
  411.8 202.6 all-gather.37
  617.2 109.1 all-gather.29
  741.6 20.2 all-gather.31
  763.9 21.8 all-gather.33
  870.6 31.8 reduce-scatter.16
  904.6 30.5 reduce-scatter.18
  999.8 30.5 reduce-scatter.20
  1032.5 30.6 reduce-scatter.22
  1075.0 133.3 all-reduce.8
  1215.0 102.0 reduce-scatter.30
  1320.0 145.3 reduce-scatter.28
  1472.1 104.4 reduce-scatter.26
  1583.5 118.1 reduce-scatter.24
  1708.7 491.1 reduce-scatter.32
where the time goes:
time: 3070 us; the launch traced here: 3060 us
  blocking collectives  1670 us (54%)
  waiting for transfers between devices  691 us (23%)
  matrix products  348 us (11%)
  local copies, waits for them, and re-layouts  202 us (7%)
  starting transfers between devices  82.1 us (3%)
  other arithmetic  46.1 us (2%)
    unnamed x3, blocking collectives  1630 us
    all_gather x1, waiting for transfers between devices, per_device(): lax.all_gather(gate_up_weight, ('fsdp', 'blk'), axis=0, tiled=True)  204 us
    unnamed x298, local copies, waits for them, and re-layouts  165 us
    dot_general x20, matrix products, matmul_tn(): lax.dot_general(left_side, right_side, (((0,), (0,)), ((), ())), preferre...  145 us
    dot_general x20, matrix products, matmul_nt(): lax.dot_general(left_side, right_side, (((1,), (1,)), ((), ())), preferre...  107 us
    dot_general x20, matrix products, matmul(): return jnp.dot(left_side, right_side, preferred_element_type=jnp.float32)  95.8 us
    unnamed x14, starting transfers between devices  80.7 us
  transfers between devices with their start and end apart: 34, of which 17 were waited for; matrix products, arithmetic and copies ran while one was open for 54% of the time, Pallas kernels for 0%

commit v1 on v0

v1 whole, which is shorter than its diff:
```python
import math

import jax
import jax.numpy as jnp
from jax import lax
from jax.sharding import PartitionSpec as P

H = 4
HD = 256
EPS = 1e-06
NEG = -1e30
ROPE_BASE = 10000.0
AXES = ("fsdp", "blk")
BF = jnp.bfloat16
F32 = jnp.float32


def matmul(left_side, right_side):
    return jnp.dot(left_side, right_side, preferred_element_type=F32)


def matmul_nt(left_side, right_side):
    return lax.dot_general(
        left_side, right_side, (((1,), (1,)), ((), ())), preferred_element_type=F32
    )


def matmul_tn(left_side, right_side):
    return lax.dot_general(
        left_side, right_side, (((0,), (0,)), ((), ())), preferred_element_type=F32
    )


def rounded(values):
    return values.astype(BF)


class Grid:
    def __init__(self, mesh):
        self.fsdp = mesh.shape["fsdp"]
        self.blk = mesh.shape["blk"]
        self.sizes = {"y": self.fsdp // 2, "x": 2, "p": self.blk // 4, "h": 2, "c": 2}
        self.devices = self.fsdp * self.blk
        self.groups = self.devices // 4

    def place(self, name):
        f = lax.axis_index("fsdp")
        b = lax.axis_index("blk")
        return {"y": f // 2, "x": f % 2, "p": b // 4, "h": (b // 2) % 2, "c": b % 2}[name]

    def permute(self, values, shifts):
        pairs = []
        for f in range(self.fsdp):
            for b in range(self.blk):
                at = {"y": f // 2, "x": f % 2, "p": b // 4, "h": (b // 2) % 2, "c": b % 2}
                for name, shift in shifts.items():
                    at[name] = (at[name] + shift) % self.sizes[name]
                pairs.append(
                    (
                        f * self.blk + b,
                        (at["y"] * 2 + at["x"]) * self.blk + at["p"] * 4 + at["h"] * 2 + at["c"],
                    )
                )
        return lax.ppermute(values, AXES, pairs)

    def gather(self, values, name, axis):
        size = self.sizes[name]
        if size == 1:
            return jnp.expand_dims(values, axis)
        place = self.place(name)
        if size == 2:
            other = self.permute(values, {name: 1})
            first = place == 0
            return jnp.stack(
                [jnp.where(first, values, other), jnp.where(first, other, values)], axis=axis
            )
        parts = [values] + [self.permute(values, {name: shift}) for shift in range(1, size)]
        stacked = jnp.stack(parts, axis=axis)
        order = (place - jnp.arange(size)) % size
        return jnp.take(stacked, order, axis=axis)

    def scatter(self, values, name, axis):
        size = self.sizes[name]
        place = self.place(name)
        total = lax.dynamic_index_in_dim(values, place, axis, keepdims=False).astype(F32)
        for shift in range(1, size):
            sent = lax.dynamic_index_in_dim(values, (place + shift) % size, axis, keepdims=False)
            total = total + self.permute(sent.astype(BF), {name: shift}).astype(F32)
        return total

    def gather_all(self, values, turn, with_core):
        out = self.gather(values, "p", 0)
        out = self.gather(out, "h", 1)
        if turn:
            out = self.gather(out, "y", 0)
            out = self.gather(out, "x", 1)
        else:
            out = self.gather(out, "x", 0)
            out = self.gather(out, "y", 0)
        if with_core:
            out = self.gather(out, "c", 4)
        return out

    def gather_groups(self, values, turn):
        out = self.gather(values, "p", 0)
        if turn:
            out = self.gather(out, "y", 0)
            out = self.gather(out, "x", 1)
        else:
            out = self.gather(out, "x", 0)
            out = self.gather(out, "y", 0)
        return out.reshape(self.groups * values.shape[0], values.shape[1])

    def scatter_groups(self, values, turn):
        sizes = self.sizes
        out = values.reshape(
            sizes["y"], 2, sizes["p"], values.shape[0] // self.groups, values.shape[1]
        )
        if turn:
            out = self.scatter(out, "y", 0)
            out = self.scatter(out, "x", 0)
        else:
            out = self.scatter(out, "x", 1)
            out = self.scatter(out, "y", 0)
        return self.scatter(out, "p", 0)

    def scatter_all(self, values, turn):
        sizes = self.sizes
        out = values.reshape((sizes["y"], 2, sizes["p"], 2, 2) + values.shape[1:])
        out = self.scatter(out, "c", 4)
        if turn:
            out = self.scatter(out, "y", 0)
            out = self.scatter(out, "x", 0)
        else:
            out = self.scatter(out, "x", 1)
            out = self.scatter(out, "y", 0)
        out = self.scatter(out, "h", 1)
        return self.scatter(out, "p", 0)

    def tokens_in(self, rows):
        both = jnp.concatenate([rows, self.permute(rows, {"h": 1})], axis=0)
        return jnp.concatenate([both, self.permute(both, {"c": 1})], axis=0)

    def tokens_out(self, sums):
        count = sums.shape[0] // 4
        both = sums[: 2 * count] + self.permute(rounded(sums[2 * count :]), {"c": 1}).astype(F32)
        return both[:count] + self.permute(rounded(both[count:]), {"h": 1}).astype(F32)


def pad_rows(values, rows, axis):
    if values.shape[axis] == rows:
        return values
    widths = [(0, 0)] * values.ndim
    widths[axis] = (0, rows - values.shape[axis])
    return jnp.pad(values, widths)


def up8(rows):
    return -(-rows // 8) * 8


def pack(parts):
    axis = parts[0].ndim - 2
    return jnp.concatenate([pad_rows(part, up8(part.shape[axis]), axis) for part in parts], axis=axis)


def unpack(packed, counts):
    out = []
    at = 0
    for count in counts:
        piece = packed[:, at : at + count]
        out.append(piece.reshape(packed.shape[0] * count, packed.shape[2]))
        at += up8(count)
    return out


def unpack_own(packed, counts):
    out = []
    at = 0
    for count in counts:
        out.append(packed[at : at + count])
        at += up8(count)
    return out


def norm_rows(values, gain_row):
    return values * lax.rsqrt(jnp.mean(values * values, axis=-1, keepdims=True) + EPS) * gain_row


def norm_back(values, gain_row, grad):
    inverse = lax.rsqrt(jnp.mean(values * values, axis=-1, keepdims=True) + EPS)
    weighted = grad * gain_row
    inner = jnp.mean(weighted * values, axis=-1, keepdims=True)
    gain_grad = jnp.sum(grad * values * inverse, axis=0)
    return inverse * weighted - values * (inverse * inverse * inverse) * inner, gain_grad


def rotate(values, cosine_table, sine_table):
    halfway = values.shape[-1] // 2
    first_half = values[..., :halfway]
    second_half = values[..., halfway:]
    return jnp.concatenate(
        [
            first_half * cosine_table - second_half * sine_table,
            second_half * cosine_table + first_half * sine_table,
        ],
        axis=-1,
    )


def activate(gate, up):
    return jax.nn.gelu(gate, approximate=True) * up


def per_device(
    grid,
    inputs,
    segments,
    cotangent,
    norm_gain_rows,
    query_key_value_weight,
    output_weight,
    gate_up_weight,
    down_weight,
    adapter_query_down,
    adapter_query_lift,
    adapter_output_down,
    adapter_output_lift,
):
    tokens = inputs.shape[0]
    width = inputs.shape[1]
    groups = grid.groups
    gain_cols = norm_gain_rows.shape[1]
    qkv_rows = query_key_value_weight.shape[0]
    out_rows = output_weight.shape[0]
    qd_rows = adapter_query_down.shape[1]
    ql_rows = adapter_query_lift.shape[1]
    od_rows = adapter_output_down.shape[1]
    ol_rows = adapter_output_lift.shape[1]
    rank = adapter_query_down.shape[2]
    hidden_block = down_weight.shape[0]

    gains_part = jnp.pad(norm_gain_rows, ((0, 0), (0, rank - gain_cols)))
    packed_qkv = pack([query_key_value_weight, adapter_query_lift[0], adapter_query_lift[1]])
    packed_narrow = pack(
        [
            adapter_query_down[0],
            adapter_query_down[1],
            adapter_output_down[0],
            adapter_output_down[1],
            gains_part,
        ]
    )
    packed_out = pack([output_weight, adapter_output_lift[0], adapter_output_lift[1]])

    def whole(packed, turn):
        return grid.gather_all(packed, turn, True).reshape((grid.devices,) + packed.shape)

    all_qkv = whole(packed_qkv, False)
    all_narrow = whole(packed_narrow, True)
    all_out = whole(packed_out, True)
    qkv_counts = [qkv_rows, ql_rows, ql_rows]
    out_counts = [out_rows, ol_rows, ol_rows]
    narrow_counts = [qd_rows, qd_rows, od_rows, od_rows]
    w_qkv, ql_0, ql_1 = unpack(all_qkv, qkv_counts)
    qd_0, qd_1, od_0, od_1 = unpack(all_narrow, narrow_counts)
    w_out, ol_0, ol_1 = unpack(all_out, out_counts)
    gains = (
        all_narrow[:, -8:-6, :gain_cols].transpose(1, 0, 2).reshape(2, width).astype(F32)
    )
    adapters = ((qd_0, ql_0, od_0, ol_0), (qd_1, ql_1, od_1, ol_1))

    place_h = grid.place("h")
    place_c = grid.place("c")
    quarter = place_h * 2 + place_c
    cut = (
        gate_up_weight.reshape(qkv_rows, 2, groups, 4, hidden_block)
        .transpose(3, 1, 0, 2, 4)
        .reshape(2, 2, 2, qkv_rows, groups * hidden_block)
    )

    def cut_for(h, c):
        part = lax.dynamic_index_in_dim(cut, h, 0, keepdims=False)
        return lax.dynamic_index_in_dim(part, c, 0, keepdims=False)

    own = cut_for(place_h, place_c)
    from_c = grid.permute(cut_for(place_h, 1 - place_c), {"c": 1})
    from_h = grid.permute(cut_for(1 - place_h, place_c), {"h": 1})
    from_hc = grid.permute(cut_for(1 - place_h, 1 - place_c), {"h": 1, "c": 1})
    relative = jnp.stack([own, from_c, from_h, from_hc])
    pieces = jnp.stack(
        [
            lax.dynamic_index_in_dim(relative, quarter ^ index, 0, keepdims=False)
            for index in range(4)
        ],
        axis=1,
    )
    pieces = pieces.reshape(2, 4 * qkv_rows, groups * hidden_block)
    w_gate = grid.gather_groups(pieces[0], False)
    w_up = grid.gather_groups(pieces[1], True)
    half_cols = (width // 256) * 128 + 128
    w_down = jnp.concatenate(
        [
            grid.gather_groups(down_weight[:, :half_cols], False),
            grid.gather_groups(down_weight[:, half_cols:], True),
        ],
        axis=1,
    )

    segrow = segments[0]
    seq_len = segrow.shape[0]
    position = lax.axis_index("blk")
    places = position * tokens + jnp.arange(tokens, dtype=jnp.int32)
    own_segs = lax.dynamic_slice_in_dim(segrow, position * tokens, tokens, 0)
    below_one = jnp.sum((segrow < 1).astype(jnp.int32))
    below_two = jnp.sum((segrow < 2).astype(jnp.int32))
    starts = jnp.where(own_segs == 0, 0, jnp.where(own_segs == 1, below_one, below_two))
    offsets = (places - starts).astype(F32)
    frequency = jnp.exp(jnp.arange(HD // 2, dtype=F32) * (-2.0 * math.log(ROPE_BASE) / HD))
    turned = offsets[:, None] * frequency[None, :]
    cosine_table = jnp.cos(turned)
    sine_table = jnp.sin(turned)
    width_q = H * HD
    row_places = jnp.tile(places, H)
    row_segs = jnp.tile(own_segs, H)
    key_places = jnp.arange(seq_len, dtype=jnp.int32)
    allowed = (row_segs[:, None] == segrow[None, :]) & (key_places[None, :] <= row_places[:, None])

    def forward_loop(residual, loop):
        qd, ql, od, ol = adapters[loop]
        normed_b = rounded(norm_rows(residual, gains[0]))
        low_rank_b = rounded(matmul(normed_b, qd))
        joined = matmul(normed_b, w_qkv) + matmul(low_rank_b, ql)
        query_heads = joined[:, :width_q].reshape(tokens, H, HD).transpose(1, 0, 2)
        queries = rounded(rotate(query_heads, cosine_table, sine_table) * HD ** (-0.5)).reshape(
            H * tokens, HD
        )
        key_rows = rounded(rotate(joined[:, width_q : width_q + HD], cosine_table, sine_table))
        value_rows = rounded(joined[:, width_q + HD :])
        both = lax.all_gather(
            jnp.concatenate([key_rows, value_rows], axis=1), "blk", axis=0, tiled=True
        )
        keys, values = both[:, :HD], both[:, HD:]
        scores = matmul_nt(queries, keys)
        top = jnp.max(jnp.where(allowed, scores, NEG), axis=1, keepdims=True)
        probabilities = jnp.where(allowed, jnp.exp(scores - top), 0.0)
        total = jnp.sum(probabilities, axis=1, keepdims=True)
        mixed_rows = matmul(rounded(probabilities), values) / total
        log_total = top + jnp.log(total)
        mixed_b = rounded(
            mixed_rows.reshape(H, tokens, HD).transpose(1, 0, 2).reshape(tokens, width_q)
        )
        side_b = rounded(matmul(mixed_b, od))
        middle = residual + (matmul(mixed_b, w_out) + matmul(side_b, ol))
        normed_ff_b = rounded(norm_rows(middle, gains[1]))
        ff_in = grid.tokens_in(normed_ff_b)
        gate = matmul(ff_in, w_gate)
        up = matmul(ff_in, w_up)
        hidden_b = rounded(activate(gate, up))
        following = middle + grid.tokens_out(matmul(hidden_b, w_down))
        cache = (
            residual, normed_b, low_rank_b, queries, keys, values, mixed_rows, log_total,
            mixed_b, side_b, middle, ff_in, rounded(gate), rounded(up), hidden_b,
        )
        return following, cache

    def backward_loop(cache, grad_result, loop):
        (
            residual, normed_b, low_rank_b, queries, keys, values, mixed_rows, log_total,
            mixed_b, side_b, middle, ff_in, gate_b, up_b, hidden_b,
        ) = cache
        qd, ql, od, ol = adapters[loop]
        ff_grad = grid.tokens_in(rounded(grad_result))
        grad_hidden = matmul_nt(ff_grad, w_down)
        unused, pullback = jax.vjp(activate, gate_b.astype(F32), up_b.astype(F32))
        grad_gate, grad_up = pullback(grad_hidden)
        grad_gate_b = rounded(grad_gate)
        grad_up_b = rounded(grad_up)
        d_down = matmul_tn(hidden_b, ff_grad)
        grad_normed_ff = grid.tokens_out(
            matmul_nt(grad_gate_b, w_gate) + matmul_nt(grad_up_b, w_up)
        )
        d_gate = matmul_tn(ff_in, grad_gate_b)
        d_up = matmul_tn(ff_in, grad_up_b)
        grad_middle_norm, gain_grad_ff = norm_back(middle, gains[1], grad_normed_ff)
        grad_middle = grad_result + grad_middle_norm
        grad_branch_b = rounded(grad_middle)
        grad_side_b = rounded(matmul_nt(grad_branch_b, ol))
        grad_mixed_b = rounded(matmul_nt(grad_branch_b, w_out) + matmul_nt(grad_side_b, od))
        d_out = matmul_tn(mixed_b, grad_branch_b)
        d_ol = matmul_tn(side_b, grad_branch_b)
        d_od = matmul_tn(mixed_b, grad_side_b)
        grad_rows = grad_mixed_b.reshape(tokens, H, HD).transpose(1, 0, 2).reshape(H * tokens, HD)
        delta = jnp.sum(grad_rows.astype(F32) * mixed_rows, axis=1, keepdims=True)
        scores = matmul_nt(queries, keys)
        probabilities = jnp.where(allowed, jnp.exp(scores - log_total), 0.0)
        grad_probs = matmul_nt(grad_rows, values)
        grad_scores = rounded(probabilities * (grad_probs - delta))
        grad_q = matmul(grad_scores, keys)
        grad_k_all = matmul_tn(grad_scores, queries)
        grad_v_all = matmul_tn(rounded(probabilities), grad_rows)
        grad_kv = lax.psum_scatter(
            jnp.concatenate([rounded(grad_k_all), rounded(grad_v_all)], axis=1),
            "blk",
            scatter_dimension=0,
            tiled=True,
        ).astype(F32)
        grad_query_heads = rotate(
            grad_q.reshape(H, tokens, HD), cosine_table, -sine_table
        ) * HD ** (-0.5)
        grad_joined_b = rounded(
            jnp.concatenate(
                [
                    grad_query_heads.transpose(1, 0, 2).reshape(tokens, width_q),
                    rotate(grad_kv[:, :HD], cosine_table, -sine_table),
                    grad_kv[:, HD:],
                ],
                axis=1,
            )
        )
        grad_low_rank_b = rounded(matmul_nt(grad_joined_b, ql))
        grad_normed = matmul_nt(grad_joined_b, w_qkv) + matmul_nt(grad_low_rank_b, qd)
        grad_state_norm, gain_grad_attn = norm_back(residual, gains[0], grad_normed)
        shared = (
            jnp.stack([gain_grad_attn, gain_grad_ff]),
            matmul_tn(normed_b, grad_joined_b),
            d_out,
            d_gate,
            d_up,
            d_down,
        )
        single = (
            matmul_tn(normed_b, grad_low_rank_b),
            matmul_tn(low_rank_b, grad_joined_b),
            d_od,
            d_ol,
        )
        return grad_middle + grad_state_norm, shared, single

    residual_zero = inputs.astype(F32)
    residual_one, cache_one = forward_loop(residual_zero, 0)
    result, cache_two = forward_loop(residual_one, 1)
    grad_one, shared_two, single_two = backward_loop(cache_two, cotangent.astype(F32), 1)
    grad_inputs, shared_one, single_one = backward_loop(cache_one, grad_one, 0)
    g_gains, g_qkv, g_out, g_gate, g_up, g_down = [
        first + second for first, second in zip(shared_two, shared_one)
    ]

    def blocks(values):
        return values.reshape(grid.devices, values.shape[0] // grid.devices, values.shape[1])

    d_down = jnp.concatenate(
        [
            grid.scatter_groups(g_down[:, :half_cols], False),
            grid.scatter_groups(g_down[:, half_cols:], True),
        ],
        axis=1,
    )
    d_pieces = jnp.stack(
        [grid.scatter_groups(g_gate, False), grid.scatter_groups(g_up, True)]
    ).reshape(2, 4, qkv_rows, groups * hidden_block)
    d_pieces = rounded(d_pieces)

    def member(index):
        return lax.dynamic_index_in_dim(d_pieces, index, 1, keepdims=False)

    back = jnp.stack(
        [
            member(quarter),
            grid.permute(member(quarter ^ 1), {"c": 1}),
            grid.permute(member(quarter ^ 2), {"h": 1}),
            grid.permute(member(quarter ^ 3), {"h": 1, "c": 1}),
        ]
    )
    back = jnp.stack(
        [lax.dynamic_index_in_dim(back, quarter ^ index, 0, keepdims=False) for index in range(4)]
    )
    d_gate_up = (
        back.reshape(4, 2, qkv_rows, groups, hidden_block)
        .transpose(2, 1, 3, 0, 4)
        .reshape(qkv_rows, 8 * groups * hidden_block)
        .astype(F32)
    )

    got_out = grid.scatter_all(
        pack([blocks(g_out), blocks(single_one[3]), blocks(single_two[3])]), True
    )
    d_out, d_ol_0, d_ol_1 = unpack_own(got_out, out_counts)
    gain_blocks = jnp.pad(
        g_gains.reshape(2, grid.devices, gain_cols).transpose(1, 0, 2),
        ((0, 0), (0, 0), (0, rank - gain_cols)),
    )
    got_narrow = grid.scatter_all(
        pack(
            [
                blocks(single_one[0]),
                blocks(single_two[0]),
                blocks(single_one[2]),
                blocks(single_two[2]),
                gain_blocks,
            ]
        ),
        True,
    )
    d_qd_0, d_qd_1, d_od_0, d_od_1 = unpack_own(got_narrow, narrow_counts)
    d_gains = got_narrow[-8:-6, :gain_cols]
    got_qkv = grid.scatter_all(
        pack([blocks(g_qkv), blocks(single_one[1]), blocks(single_two[1])]), False
    )
    d_qkv, d_ql_0, d_ql_1 = unpack_own(got_qkv, qkv_counts)
    return (
        rounded(result),
        grad_inputs,
        d_gains,
        d_qkv,
        d_out,
        d_gate_up,
        d_down,
        jnp.stack([d_qd_0, d_qd_1]),
        jnp.stack([d_ql_0, d_ql_1]),
        jnp.stack([d_od_0, d_od_1]),
        jnp.stack([d_ol_0, d_ol_1]),
    )


def solution(mesh):
    grid = Grid(mesh)
    rows = P(AXES, None)
    deep = P(None, AXES, None)
    in_specs = (
        rows, P("fsdp", None), rows, P(None, AXES), rows, rows, rows, rows, deep, deep, deep, deep,
    )
    out_specs = (
        rows, rows, P(None, AXES), rows, rows, rows, rows, deep, deep, deep, deep,
    )

    def run(*arguments):
        return per_device(grid, *arguments)

    return jax.shard_map(
        run, mesh=mesh, in_specs=in_specs, out_specs=out_specs, check_vma=False
    )
```

time: 3070 us -> 1060 us (0.35)
  blocking collectives: 1670 us -> 0 us
  waiting for transfers between devices: 691 us -> 419 us
  matrix products: 348 us -> 252 us
  other arithmetic: 46.1 us -> 128 us
  local copies, waits for them, and re-layouts: 202 us -> 158 us
    unnamed x3 -> x0, blocking collectives: 1630 us -> none
    all_gather x12 -> x2, waiting for transfers between devices: 592 us -> 40.2 us  [forward_loop(): lax.all_gather(jnp.concatenate([key_rows, value_rows], axis=1), 'blk', ax...]
    ppermute x0 -> x76, waiting for transfers between devices: none -> 348 us  [permute(): return lax.ppermute(values, AXES, pairs)]
    unnamed x298 -> x484, local copies, waits for them, and re-layouts: 165 us -> 34.1 us
    unnamed x14 -> x0, starting transfers between devices: 80.7 us -> none
    ppermute x0 -> x76, starting transfers between devices: none -> 80.4 us  [permute(): return lax.ppermute(values, AXES, pairs)]
    dot_general x20 -> x22, matrix products: 145 us -> 75.2 us  [matmul_tn(): lax.dot_general(left_side, right_side, (((0,), (0,)), ((), ())), preferre...]
    reduce_scatter x8 -> x2, waiting for transfers between devices: 92.3 us -> 30.7 us  [backward_loop(): lax.psum_scatter(jnp.concatenate([rounded(grad_k_all), rounded(grad_v_all...]
  transfers between devices with their start and end apart: 34 -> 80, of which waited for: 17 -> 39; matrix products, arithmetic and copies ran while one was open for 54% -> 31% of each run, Pallas kernels for 0% -> 0%
where the time goes in v1:
time: 1060 us
  waiting for transfers between devices  419 us (40%)
  matrix products  252 us (24%)
  local copies, waits for them, and re-layouts  158 us (15%)
  other arithmetic  128 us (12%)
  starting transfers between devices  81 us (8%)
  between operations  18.1 us (2%)
    ppermute x76, waiting for transfers between devices, permute(): return lax.ppermute(values, AXES, pairs)  348 us
    dot_general x22, matrix products, matmul_nt(): lax.dot_general(left_side, right_side, (((1,), (1,)), ((), ())), preferre...  101 us
    ppermute x76, starting transfers between devices, permute(): return lax.ppermute(values, AXES, pairs)  80.4 us
    dot_general x22, matrix products, matmul(): return jnp.dot(left_side, right_side, preferred_element_type=F32)  75.7 us
    dot_general x22, matrix products, matmul_tn(): lax.dot_general(left_side, right_side, (((0,), (0,)), ((), ())), preferre...  75.2 us
    another operation x53, other arithmetic, gather(): jnp.stack([jnp.where(first, values, other), jnp.where(first, other, value...  41.1 us
    all_gather x2, waiting for transfers between devices, forward_loop(): lax.all_gather(jnp.concatenate([key_rows, value_rows], axis=1), 'blk', ax...  40.2 us
    unnamed x484, local copies, waits for them, and re-layouts  34.1 us
  transfers between devices with their start and end apart: 80, of which 39 were waited for; matrix products, arithmetic and copies ran while one was open for 31% of the time, Pallas kernels for 0%

profile of v1, /device:TPU:0, one launch (start us, length us, event | category | flops | bytes accessed | tf_op | source)
XLA Modules:
  0.0 1056.7 jit_solution(1132102398795833535)
XLA Ops:
  53.6 17.2 %collective-permute-done.1 = bf16[2,152,256]{2,1,0:T(8,128)(2,1)S(1)} collective-permute-done((bf16[2,152,256]{2,1,0:T(8,128)(2,1)S(1)}, bf16[2,152,256]{2,1,0:T(8,128)(2,1)S(1)}, u32[]{:S(2)}, u32[]{:S(2)}) %collective-permute-start.1) | collective-permute-done | bytes 155680 | tf_op jit(solution)/shard_map/ppermute | solution.py:64
  84.6 5.8 collective-permute-done.6
  97.6 19.4 %collective-permute-done.23 = bf16[144,1728]{1,0:T(8,128)(2,1)S(1)} collective-permute-done((bf16[144,1728]{1,0:T(8,128)(2,1)S(1)}, bf16[144,1728]{1,0:T(8,128)(2,1)S(1)}, u32[]{:S(2)}, u32[]{:S(2)}) %collective-permute-start.23) | collective-permute-done | bytes 497696 | tf_op jit(solution)/shard_map/ppermute | solution.py:64
  118.5 7.6 collective-permute-done.20
  136.2 27.8 %collective-permute-done.8 = bf16[2,2,2,56,1536]{4,3,2,1,0:T(8,128)(2,1)S(1)} collective-permute-done((bf16[2,2,2,56,1536]{4,3,2,1,0:T(8,128)(2,1)S(1)}, bf16[2,2,2,56,1536]{4,3,2,1,0:T(8,128)(2,1)S(1)}, u32[]{:S(2)}, u32[]{:S(2)}) %collective-permute-start.8) | collective-permute-done | bytes 1376288 | tf_op jit(solution)/shard_map/ppermute | solution.py:64
  168.3 23.9 %collective-permute-done.13 = bf16[2,2,2,48,1152]{4,3,2,1,0:T(8,128)(2,1)S(1)} collective-permute-done((bf16[2,2,2,48,1152]{4,3,2,1,0:T(8,128)(2,1)S(1)}, bf16[2,2,2,48,1152]{4,3,2,1,0:T(8,128)(2,1)S(1)}, u32[]{:S(2)}, u32[]{:S(2)}) %collective-permute-start.13) | collective-permute-done | bytes 884768 | tf_op jit(solution)/shard_map/ppermute | solution.py:64
  211.9 5.6 reshape.457
  243.8 8.6 all-gather.3.cloned.1.call-done
  270.6 8.0 collective-permute-done.25
  289.7 8.5 fusion.219
  298.2 11.9 %fusion.17 = (bf16[1024,1728]{0,1:T(8,128)(2,1)S(1)}, bf16[1024,1728]{0,1:T(8,128)(2,1)}) fusion(f32[1024,1728]{0,1:T(8,128)} %fusion.219, bf16[1152,1728]{1,0:T(8,128)(2,1)S(1)} %bitcast.570, bf16[512,1152]{1,0:T(8,128)(2,1)S(1)} %collective-permute-done.16, bf16[256,1152]{1,0:T(8,128)(2,1)S(1)} %collective-permute-done.15, ...), kind=kOutput, calls=%fused_computation.43 | convolution fusion | flops 4103405568 | bytes 20496384 | tf_op jit(solution)/shard_map/dot_general | solution.py:19
  310.2 5.3 fusion.202
  324.8 12.2 %collective-permute-done.33 = bf16[256,1152]{1,0:T(8,128)(2,1)} collective-permute-done((bf16[256,1152]{1,0:T(8,128)(2,1)}, bf16[256,1152]{1,0:T(8,128)(2,1)}, u32[]{:S(2)}, u32[]{:S(2)}) %collective-permute-start.33) | collective-permute-done | bytes 589856 | tf_op jit(solution)/shard_map/ppermute | solution.py:64
  347.7 31.7 %all-gather.5.cloned.1.call-done = bf16[2048,512]{1,0:T(8,128)(2,1)} async-done(((bf16[256,512]{1,0:T(8,128)(2,1)}), bf16[2048,512]{1,0:T(8,128)(2,1)}) %all-gather.5.cloned.1.call-update) | async-done | bytes 2097168 | tf_op jit(solution)/shard_map/all_gather | solution.py:340
  398.0 12.8 %collective-permute-done.34 = bf16[256,1152]{1,0:T(8,128)(2,1)S(1)} collective-permute-done((bf16[256,1152]{1,0:T(8,128)(2,1)S(1)}, bf16[256,1152]{1,0:T(8,128)(2,1)S(1)}, u32[]{:S(2)}, u32[]{:S(2)}) %collective-permute-start.34) | collective-permute-done | bytes 589856 | tf_op jit(solution)/shard_map/ppermute | solution.py:64
  413.8 8.2 fusion.214
  422.0 8.8 fusion.215
  430.8 23.1 %fusion.33 = (bf16[1024,1728]{0,1:T(8,128)(2,1)}, bf16[1024,1728]{0,1:T(8,128)(2,1)}, bf16[1024,1728]{0,1:T(8,128)(2,1)}) fusion(f32[1024,1728]{0,1:T(8,128)} %fusion.215, f32[1024,1728]{0,1:T(8,128)} %fusion.214, bf16[1024,1152]{1,0:T(8,128)(2,1)} %copy-done.157, bf16[1728,512]{1,0:T(8,128)(2,1)} %bitcast.604, bf16[1728,640]{1,0:T(8,128)(2,1)S(1)} %bitcast.581), kind=kOutput, calls=%fused_computation.59 | convolution fusion | flops 4152066048 | bytes 31113216 | tf_op jit(solution)/shard_map/dot_general | solution.py:23
  453.9 10.5 fusion.237
  464.4 7.4 convolution_add_fusion.6
  473.3 5.2 fusion.201
  483.4 12.0 %collective-permute-done.41 = bf16[256,1152]{1,0:T(8,128)(2,1)S(1)} collective-permute-done((bf16[256,1152]{1,0:T(8,128)(2,1)S(1)}, bf16[256,1152]{1,0:T(8,128)(2,1)S(1)}, u32[]{:S(2)}, u32[]{:S(2)}) %collective-permute-start.41) | collective-permute-done | bytes 589856 | tf_op jit(solution)/shard_map/ppermute | solution.py:64
  496.6 11.0 %collective-permute-done.37 = bf16[256,1152]{1,0:T(8,128)(2,1)S(1)} collective-permute-done((bf16[256,1152]{1,0:T(8,128)(2,1)S(1)}, bf16[256,1152]{1,0:T(8,128)(2,1)S(1)}, u32[]{:S(2)}, u32[]{:S(2)}) %collective-permute-start.37) | collective-permute-done | bytes 589856 | tf_op jit(solution)/shard_map/ppermute | solution.py:64
  529.3 30.7 %reduce-scatter.3.cloned.1.call-done = bf16[256,512]{1,0:T(8,128)(2,1)} async-done(((bf16[2048,512]{1,0:T(8,128)(2,1)}), bf16[256,512]{1,0:T(8,128)(2,1)}) %reduce-scatter.3.cloned.1.call-update) | async-done | bytes 262160 | tf_op jit(solution)/shard_map/reduce_scatter | solution.py:402
  573.8 8.1 collective-permute-done.42
  593.8 6.6 fusion.101
  600.4 4.9 convolution_add_fusion.3
  608.3 14.2 %fusion.40 = (bf16[1024,1728]{0,1:T(8,128)(2,1)}, bf16[1024,1728]{0,1:T(8,128)(2,1)S(1)}) fusion(f32[1024,1728]{0,1:T(8,128)} %fusion.219, bf16[1024,1728]{0,1:T(8,128)(2,1)} %get-tuple-element.196, bf16[1728,512]{1,0:T(8,128)(2,1)} %bitcast.605, bf16[1728,640]{1,0:T(8,128)(2,1)S(1)} %bitcast.583, bf16[512,1152]{1,0:T(8,128)(2,1)} %collective-permute-done.43, ...), kind=kOutput, calls=%fused_computation.66 | convolution fusion | flops 4139679744 | bytes 24035328 | tf_op jit(solution)/shard_map/dot_general | solution.py:23
  622.5 6.7 fusion.239
  629.2 7.5 convolution_add_fusion.5
  653.1 10.6 %convolution_add_fusion.1 = f32[1152,1728]{0,1:T(8,128)} fusion(f32[1152,1728]{0,1:T(8,128)S(1)} %fusion.217, bf16[1024,1728]{0,1:T(8,128)(2,1)} %get-tuple-element.66, bf16[512,1152]{1,0:T(8,128)(2,1)S(1)} %copy-done.211, bf16[256,1152]{1,0:T(8,128)(2,1)S(1)} %copy-done.119, bf16[256,1152]{1,0:T(8,128)(2,1)S(1)} %copy-done.84), kind=kOutput, calls=%fused_computation.16 | convolution fusion | flops 4085932032 | bytes 21823488 | tf_op jit(solution)/shard_map/dot_general | solution.py:29
  663.7 6.9 convolution_add_fusion.2
  670.6 8.9 copy.114
  679.5 8.9 copy.113
  712.2 5.3 collective-permute-done.75
  718.3 39.5 %collective-permute-done.71 = bf16[2,216,640]{2,1,0:T(8,128)(2,1)S(1)} collective-permute-done((bf16[2,216,640]{2,1,0:T(8,128)(2,1)S(1)}, bf16[2,216,640]{2,1,0:T(8,128)(2,1)S(1)}, u32[]{:S(2)}, u32[]{:S(2)}) %collective-permute-start.71) | collective-permute-done | bytes 552992 | tf_op jit(solution)/shard_map/ppermute | solution.py:64
  767.6 6.6 fusion.70
  774.2 6.0 multiply_convert_fusion
  803.8 17.8 %collective-permute-done.62 = bf16[2,144,1728]{2,1,0:T(8,128)(2,1)S(1)} collective-permute-done((bf16[2,144,1728]{2,1,0:T(8,128)(2,1)S(1)}, bf16[2,144,1728]{2,1,0:T(8,128)(2,1)S(1)}, u32[]{:S(2)}, u32[]{:S(2)}) %collective-permute-start.62) | collective-permute-done | bytes 995360 | tf_op jit(solution)/shard_map/ppermute | solution.py:64
  826.7 31.0 %collective-permute-done.63 = bf16[144,1728]{1,0:T(8,128)(2,1)S(1)} collective-permute-done((bf16[144,1728]{1,0:T(8,128)(2,1)S(1)}, bf16[144,1728]{1,0:T(8,128)(2,1)S(1)}, u32[]{:S(2)}, u32[]{:S(2)}) %collective-permute-start.63) | collective-permute-done | bytes 497696 | tf_op jit(solution)/shard_map/ppermute | solution.py:64
  861.1 6.3 collective-permute-done.66
  922.9 7.9 reshape.487
  930.8 7.3 pad.47
  938.1 5.9 pad_maximum_fusion
  947.6 6.3 collective-permute-done.59
  994.7 20.1 %collective-permute-done.52 = bf16[2,2,2,56,1536]{4,3,2,1,0:T(8,128)(2,1)S(1)} collective-permute-done((bf16[2,2,2,56,1536]{4,3,2,1,0:T(8,128)(2,1)S(1)}, bf16[2,2,2,56,1536]{4,3,2,1,0:T(8,128)(2,1)S(1)}, u32[]{:S(2)}, u32[]{:S(2)}) %collective-permute-start.52) | collective-permute-done | bytes 1376288 | tf_op jit(solution)/shard_map/ppermute | solution.py:64
  1018.3 13.2 %collective-permute-done.53 = bf16[2,2,56,1536]{3,2,1,0:T(8,128)(2,1)S(1)} collective-permute-done((bf16[2,2,56,1536]{3,2,1,0:T(8,128)(2,1)S(1)}, bf16[2,2,56,1536]{3,2,1,0:T(8,128)(2,1)S(1)}, u32[]{:S(2)}, u32[]{:S(2)}) %collective-permute-start.53) | collective-permute-done | bytes 688160 | tf_op jit(solution)/shard_map/ppermute | solution.py:64
  1033.9 6.3 collective-permute-done.54
  (941 shorter events, 452.8 us)
Async XLA Ops:
  7.2 245.1 %all-gather.3.cloned.1.call-start = ((), (), s32[]{:S(2)}) async-start(), calls=%async_computation.2 | async-start | bytes 2359296 | tf_op jit(solution)/shard_map/all_gather | solution.py:340
  13.4 27.9 %collective-permute-start = (bf16[152,256]{1,0:T(8,128)(2,1)}, bf16[152,256]{1,0:T(8,128)(2,1)}, u32[]{:S(2)}, u32[]{:S(2)}) collective-permute-start(bf16[152,256]{1,0:T(8,128)(2,1)} %constant_dynamic-update-slice_fusion), channel_id=1, source_target_pairs={{0,4},{1,5},{2,6},{3,7},{4,0},{5,1},{6,2},{7,3},{8,12},{9,13},{10,... | collective-permute-start | bytes 233480 | tf_op jit(solution)/shard_map/ppermute | solution.py:64
  19.7 23.6 %collective-permute-start.10 = (bf16[48,1152]{1,0:T(8,128)(2,1)}, bf16[48,1152]{1,0:T(8,128)(2,1)}, u32[]{:S(2)}, u32[]{:S(2)}) collective-permute-start(bf16[48,1152]{1,0:T(8,128)(2,1)} %pad_maximum_fusion.49), channel_id=1, source_target_pairs={{0,4},{1,5},{2,6},{3,7},{4,0},{5,1},{6,2},{7,3},{8,12},{9,13},{10,... | collective-permute-start | bytes 331784 | tf_op jit(solution)/shard_map/ppermute | solution.py:64
  22.0 25.1 %collective-permute-start.5 = (bf16[56,1536]{1,0:T(8,128)(2,1)}, bf16[56,1536]{1,0:T(8,128)(2,1)}, u32[]{:S(2)}, u32[]{:S(2)}) collective-permute-start(bf16[56,1536]{1,0:T(8,128)(2,1)} %fusion.152), channel_id=1, source_target_pairs={{0,4},{1,5},{2,6},{3,7},{4,0},{5,1},{6,2},{7,3},{8,12},{9,13},{10,... | collective-permute-start | bytes 516104 | tf_op jit(solution)/shard_map/ppermute | solution.py:64
  26.6 25.2 %collective-permute-start.29 = (bf16[216,512]{1,0:T(8,128)(2,1)}, bf16[216,512]{1,0:T(8,128)(2,1)}, u32[]{:S(2)}, u32[]{:S(2)}) collective-permute-start(bf16[216,512]{1,0:T(8,128)(2,1)} %slice.302), channel_id=1, source_target_pairs={{0,4},{1,5},{2,6},{3,7},{4,0},{5,1},{6,2},{7,3},{8,12},{9,13},{10,... | collective-permute-start | bytes 663560 | tf_op jit(solution)/shard_map/ppermute | solution.py:64
  28.3 50.9 %collective-permute-start.26 = (bf16[216,640]{1,0:T(8,128)(2,1)}, bf16[216,640]{1,0:T(8,128)(2,1)}, u32[]{:S(2)}, u32[]{:S(2)}) collective-permute-start(bf16[216,640]{1,0:T(8,128)(2,1)} %slice.301), channel_id=1, source_target_pairs={{0,4},{1,5},{2,6},{3,7},{4,0},{5,1},{6,2},{7,3},{8,12},{9,13},{10,... | collective-permute-start | bytes 829448 | tf_op jit(solution)/shard_map/ppermute | solution.py:64
  41.3 30.3 %collective-permute-start.19 = (bf16[2,36,1728]{2,0,1:T(2,128)(2,1)S(1)}, bf16[2,36,1728]{2,0,1:T(2,128)(2,1)S(1)}, u32[]{:S(2)}, u32[]{:S(2)}) collective-permute-start(bf16[2,36,1728]{2,0,1:T(2,128)(2,1)S(1)} %get-tuple-element.133), channel_id=1, source_target_pairs={{0,3},{1,2},{2,1},{3,0},{4,7},{5,6},{6,5},{7,4},{8,11},{9,10},{10,... | collective-permute-start | bytes 746504 | tf_op jit(solution)/shard_map/ppermute | solution.py:64
  43.3 30.4 %collective-permute-start.18 = (bf16[2,36,1728]{2,0,1:T(2,128)(2,1)S(1)}, bf16[2,36,1728]{2,0,1:T(2,128)(2,1)S(1)}, u32[]{:S(2)}, u32[]{:S(2)}) collective-permute-start(bf16[2,36,1728]{2,0,1:T(2,128)(2,1)S(1)} %get-tuple-element.134), channel_id=1, source_target_pairs={{0,2},{1,3},{2,0},{3,1},{4,6},{5,7},{6,4},{7,5},{8,10},{9,11},{10,... | collective-permute-start | bytes 746504 | tf_op jit(solution)/shard_map/ppermute | solution.py:64
  47.1 28.1 %collective-permute-start.17 = (bf16[2,36,1728]{2,0,1:T(2,128)(2,1)S(1)}, bf16[2,36,1728]{2,0,1:T(2,128)(2,1)S(1)}, u32[]{:S(2)}, u32[]{:S(2)}) collective-permute-start(bf16[2,36,1728]{2,0,1:T(2,128)(2,1)S(1)} %get-tuple-element.135), channel_id=1, source_target_pairs={{0,1},{1,0},{2,3},{3,2},{4,5},{5,4},{6,7},{7,6},{8,9},{9,8},{10,11... | collective-permute-start | bytes 746504 | tf_op jit(solution)/shard_map/ppermute | solution.py:64
  73.7 22.0 %collective-permute-start.30 = (bf16[2,216,512]{2,1,0:T(8,128)(2,1)}, bf16[2,216,512]{2,1,0:T(8,128)(2,1)}, u32[]{:S(2)}, u32[]{:S(2)}) collective-permute-start(bf16[2,216,512]{2,1,0:T(8,128)(2,1)} %pad_maximum_fusion.42), channel_id=1, source_target_pairs={{0,16},{1,17},{2,18},{3,19},{4,20},{5,21},{6,22},{7,23},{8,24},{9,... | collective-permute-start | bytes 1327112 | tf_op jit(solution)/shard_map/ppermute | solution.py:64
  79.2 37.8 %collective-permute-start.23 = (bf16[144,1728]{1,0:T(8,128)(2,1)S(1)}, bf16[144,1728]{1,0:T(8,128)(2,1)S(1)}, u32[]{:S(2)}, u32[]{:S(2)}) collective-permute-start(bf16[144,1728]{1,0:T(8,128)(2,1)S(1)} %squeeze.212), channel_id=1, source_target_pairs={{0,4},{1,5},{2,6},{3,7},{4,0},{5,1},{6,2},{7,3},{8,12},{9,13},{10,... | collective-permute-start | bytes 1493000 | tf_op jit(solution)/shard_map/ppermute | solution.py:64
  81.1 44.9 %collective-permute-start.20 = (bf16[144,1728]{1,0:T(8,128)(2,1)S(1)}, bf16[144,1728]{1,0:T(8,128)(2,1)S(1)}, u32[]{:S(2)}, u32[]{:S(2)}) collective-permute-start(bf16[144,1728]{1,0:T(8,128)(2,1)S(1)} %squeeze.211), channel_id=1, source_target_pairs={{0,4},{1,5},{2,6},{3,7},{4,0},{5,1},{6,2},{7,3},{8,12},{9,13},{10,... | collective-permute-start | bytes 1493000 | tf_op jit(solution)/shard_map/ppermute | solution.py:64
  90.4 42.2 %collective-permute-start.27 = (bf16[2,216,640]{2,1,0:T(8,128)(2,1)S(1)}, bf16[2,216,640]{2,1,0:T(8,128)(2,1)S(1)}, u32[]{:S(2)}, u32[]{:S(2)}) collective-permute-start(bf16[2,216,640]{2,1,0:T(8,128)(2,1)S(1)} %pad_maximum_fusion.40), channel_id=1, source_target_pairs={{0,8},{1,9},{2,10},{3,11},{4,12},{5,13},{6,14},{7,15},{8,0},{9,1},... | collective-permute-start | bytes 1658888 | tf_op jit(solution)/shard_map/ppermute | solution.py:64
  93.0 37.8 %collective-permute-start.12 = (bf16[2,2,48,1152]{3,2,1,0:T(8,128)(2,1)S(1)}, bf16[2,2,48,1152]{3,2,1,0:T(8,128)(2,1)S(1)}, u32[]{:S(2)}, u32[]{:S(2)}) collective-permute-start(bf16[2,2,48,1152]{3,2,1,0:T(8,128)(2,1)S(1)} %pad_maximum_fusion.41), channel_id=1, source_target_pairs={{0,16},{1,17},{2,18},{3,19},{4,20},{5,21},{6,22},{7,23},{8,24},{9,... | collective-permute-start | bytes 1327112 | tf_op jit(solution)/shard_map/ppermute | solution.py:64
  95.7 34.3 %collective-permute-start.7 = (bf16[2,2,56,1536]{3,2,1,0:T(8,128)(2,1)S(1)}, bf16[2,2,56,1536]{3,2,1,0:T(8,128)(2,1)S(1)}, u32[]{:S(2)}, u32[]{:S(2)}) collective-permute-start(bf16[2,2,56,1536]{3,2,1,0:T(8,128)(2,1)S(1)} %pad_maximum_fusion.38), channel_id=1, source_target_pairs={{0,8},{1,9},{2,10},{3,11},{4,12},{5,13},{6,14},{7,15},{8,0},{9,1},... | collective-permute-start | bytes 2064392 | tf_op jit(solution)/shard_map/ppermute | solution.py:64
  126.1 40.1 %collective-permute-start.31 = (bf16[2,2,216,512]{3,2,1,0:T(8,128)(2,1)S(1)}, bf16[2,2,216,512]{3,2,1,0:T(8,128)(2,1)S(1)}, u32[]{:S(2)}, u32[]{:S(2)}) collective-permute-start(bf16[2,2,216,512]{3,2,1,0:T(8,128)(2,1)S(1)} %pad_maximum_fusion.35), channel_id=1, source_target_pairs={{0,8},{1,9},{2,10},{3,11},{4,12},{5,13},{6,14},{7,15},{8,0},{9,1},... | collective-permute-start | bytes 2654216 | tf_op jit(solution)/shard_map/ppermute | solution.py:64
  130.0 94.6 %collective-permute-start.21 = (bf16[2,144,1728]{2,1,0:T(8,128)(2,1)}, bf16[2,144,1728]{2,1,0:T(8,128)(2,1)}, u32[]{:S(2)}, u32[]{:S(2)}) collective-permute-start(bf16[2,144,1728]{2,1,0:T(8,128)(2,1)} %pad_maximum_fusion.28), channel_id=1, source_target_pairs={{0,8},{1,9},{2,10},{3,11},{4,12},{5,13},{6,14},{7,15},{8,0},{9,1},... | collective-permute-start | bytes 2985992 | tf_op jit(solution)/shard_map/ppermute | solution.py:64
  130.8 33.2 %collective-permute-start.8 = (bf16[2,2,2,56,1536]{4,3,2,1,0:T(8,128)(2,1)S(1)}, bf16[2,2,2,56,1536]{4,3,2,1,0:T(8,128)(2,1)S(1)}, u32[]{:S(2)}, u32[]{:S(2)}) collective-permute-start(bf16[2,2,2,56,1536]{4,3,2,1,0:T(8,128)(2,1)S(1)} %pad_maximum_fusion.19), channel_id=1, source_target_pairs={{0,16},{1,17},{2,18},{3,19},{4,20},{5,21},{6,22},{7,23},{8,24},{9,... | collective-permute-start | bytes 4128776 | tf_op jit(solution)/shard_map/ppermute | solution.py:64
  132.6 95.4 %collective-permute-start.24 = (bf16[2,144,1728]{2,1,0:T(8,128)(2,1)}, bf16[2,144,1728]{2,1,0:T(8,128)(2,1)}, u32[]{:S(2)}, u32[]{:S(2)}) collective-permute-start(bf16[2,144,1728]{2,1,0:T(8,128)(2,1)} %pad_maximum_fusion.29), channel_id=1, source_target_pairs={{0,16},{1,17},{2,18},{3,19},{4,20},{5,21},{6,22},{7,23},{8,24},{9,... | collective-permute-start | bytes 2985992 | tf_op jit(solution)/shard_map/ppermute | solution.py:64
  134.6 57.6 %collective-permute-start.13 = (bf16[2,2,2,48,1152]{4,3,2,1,0:T(8,128)(2,1)S(1)}, bf16[2,2,2,48,1152]{4,3,2,1,0:T(8,128)(2,1)S(1)}, u32[]{:S(2)}, u32[]{:S(2)}) collective-permute-start(bf16[2,2,2,48,1152]{4,3,2,1,0:T(8,128)(2,1)S(1)} %pad_maximum_fusion.34), channel_id=1, source_target_pairs={{0,8},{1,9},{2,10},{3,11},{4,12},{5,13},{6,14},{7,15},{8,0},{9,1},... | collective-permute-start | bytes 2654216 | tf_op jit(solution)/shard_map/ppermute | solution.py:64
  166.0 38.5 %collective-permute-start.9 = (bf16[2,2,2,2,56,1536]{5,4,3,2,1,0:T(8,128)(2,1)}, bf16[2,2,2,2,56,1536]{5,4,3,2,1,0:T(8,128)(2,1)}, u32[]{:S(2)}, u32[]{:S(2)}) collective-permute-start(bf16[2,2,2,2,56,1536]{5,4,3,2,1,0:T(8,128)(2,1)} %pad_maximum_fusion.7), channel_id=1, source_target_pairs={{0,1},{1,0},{2,3},{3,2},{4,5},{5,4},{6,7},{7,6},{8,9},{9,8},{10,11... | collective-permute-start | bytes 8257544 | tf_op jit(solution)/shard_map/ppermute | solution.py:64
  166.1 30.2 %collective-permute-start.4 = (bf16[2,2,2,2,152,256]{5,4,2,3,0,1:T(8,128)(2,1)S(1)}, bf16[2,2,2,2,152,256]{5,4,2,3,0,1:T(8,128)(2,1)S(1)}, u32[]{:S(2)}, u32[]{:S(2)}) collective-permute-start(bf16[2,2,2,2,152,256]{5,4,2,3,0,1:T(8,128)(2,1)S(1)} %pad_maximum_fusion.20), channel_id=1, source_target_pairs={{0,1},{1,0},{2,3},{3,2},{4,5},{5,4},{6,7},{7,6},{8,9},{9,8},{10,11... | collective-permute-start | bytes 3735560 | tf_op jit(solution)/shard_map/ppermute | solution.py:64
  192.2 40.2 %collective-permute-start.28 = (bf16[2,2,216,640]{3,2,1,0:T(8,128)(2,1)}, bf16[2,2,216,640]{3,2,1,0:T(8,128)(2,1)}, u32[]{:S(2)}, u32[]{:S(2)}) collective-permute-start(bf16[2,2,216,640]{3,2,1,0:T(8,128)(2,1)} %pad_maximum_fusion.26), channel_id=1, source_target_pairs={{0,16},{1,17},{2,18},{3,19},{4,20},{5,21},{6,22},{7,23},{8,24},{9,... | collective-permute-start | bytes 3317768 | tf_op jit(solution)/shard_map/ppermute | solution.py:64
  196.3 41.5 %collective-permute-start.14 = (bf16[2,2,2,2,48,1152]{5,4,3,2,1,0:T(8,128)(2,1)}, bf16[2,2,2,2,48,1152]{5,4,3,2,1,0:T(8,128)(2,1)}, u32[]{:S(2)}, u32[]{:S(2)}) collective-permute-start(bf16[2,2,2,2,48,1152]{5,4,3,2,1,0:T(8,128)(2,1)} %pad_maximum_fusion.17), channel_id=1, source_target_pairs={{0,1},{1,0},{2,3},{3,2},{4,5},{5,4},{6,7},{7,6},{8,9},{9,8},{10,11... | collective-permute-start | bytes 5308424 | tf_op jit(solution)/shard_map/ppermute | solution.py:64
  224.5 154.8 %all-gather.5.cloned.1.call-start = ((), (), s32[]{:S(2)}) async-start(), calls=%async_computation.3 | async-start | bytes 2359296 | tf_op jit(solution)/shard_map/all_gather | solution.py:340
  227.5 57.9 %collective-permute-start.22 = (bf16[2,2,144,1728]{3,2,1,0:T(8,128)(2,1)}, bf16[2,2,144,1728]{3,2,1,0:T(8,128)(2,1)}, u32[]{:S(2)}, u32[]{:S(2)}) collective-permute-start(bf16[2,2,144,1728]{3,2,1,0:T(8,128)(2,1)} %pad_maximum_fusion.15), channel_id=1, source_target_pairs={{0,16},{1,17},{2,18},{3,19},{4,20},{5,21},{6,22},{7,23},{8,24},{9,... | collective-permute-start | bytes 5971976 | tf_op jit(solution)/shard_map/ppermute | solution.py:64
  231.0 47.6 %collective-permute-start.25 = (bf16[2,2,144,1728]{3,2,1,0:T(8,128)(2,1)}, bf16[2,2,144,1728]{3,2,1,0:T(8,128)(2,1)}, u32[]{:S(2)}, u32[]{:S(2)}) collective-permute-start(bf16[2,2,144,1728]{3,2,1,0:T(8,128)(2,1)} %pad_maximum_fusion.16), channel_id=1, source_target_pairs={{0,8},{1,9},{2,10},{3,11},{4,12},{5,13},{6,14},{7,15},{8,0},{9,1},... | collective-permute-start | bytes 5971976 | tf_op jit(solution)/shard_map/ppermute | solution.py:64
  345.8 214.2 %reduce-scatter.3.cloned.1.call-start = ((), (), s32[]{:S(2)}) async-start(), calls=%async_computation.4 | async-start | bytes 2359296 | tf_op jit(solution)/shard_map/reduce_scatter | solution.py:402
  345.9 50.9 %collective-permute-start.38 = (bf16[256,1152]{1,0:T(8,128)(2,1)}, bf16[256,1152]{1,0:T(8,128)(2,1)}, u32[]{:S(2)}, u32[]{:S(2)}) collective-permute-start(bf16[256,1152]{1,0:T(8,128)(2,1)} %param.14), channel_id=1, source_target_pairs={{0,2},{1,3},{2,0},{3,1},{4,6},{5,7},{6,4},{7,5},{8,10},{9,11},{10,... | collective-permute-start | bytes 1769480 | tf_op jit(solution)/shard_map/ppermute | solution.py:64
  481.9 25.6 %collective-permute-start.37 = (bf16[256,1152]{1,0:T(8,128)(2,1)S(1)}, bf16[256,1152]{1,0:T(8,128)(2,1)S(1)}, u32[]{:S(2)}, u32[]{:S(2)}) collective-permute-start(bf16[256,1152]{1,0:T(8,128)(2,1)S(1)} %slice.547), channel_id=1, source_target_pairs={{0,2},{1,3},{2,0},{3,1},{4,6},{5,7},{6,4},{7,5},{8,10},{9,11},{10,... | collective-permute-start | bytes 1769480 | tf_op jit(solution)/shard_map/ppermute | solution.py:64
  524.6 368.4 %reduce-scatter.5.cloned.1.call-start = ((), (), s32[]{:S(2)}) async-start(), calls=%async_computation.5 | async-start | bytes 2359296 | tf_op jit(solution)/shard_map/reduce_scatter | solution.py:402
  637.9 70.7 %collective-permute-start.44 = (bf16[512,1152]{1,0:T(8,128)(2,1)}, bf16[512,1152]{1,0:T(8,128)(2,1)}, u32[]{:S(2)}, u32[]{:S(2)}) collective-permute-start(bf16[512,1152]{1,0:T(8,128)(2,1)} %slice.541), channel_id=1, source_target_pairs={{0,1},{1,0},{2,3},{3,2},{4,5},{5,4},{6,7},{7,6},{8,9},{9,8},{10,11... | collective-permute-start | bytes 3538952 | tf_op jit(solution)/shard_map/ppermute | solution.py:64
  639.4 52.9 %collective-permute-start.73 = (bf16[2,2,216,512]{3,2,1,0:T(8,128)(2,1)}, bf16[2,2,216,512]{3,2,1,0:T(8,128)(2,1)}, u32[]{:S(2)}, u32[]{:S(2)}) collective-permute-start(bf16[2,2,216,512]{3,2,1,0:T(8,128)(2,1)} %fusion.122), channel_id=1, source_target_pairs={{0,16},{1,17},{2,18},{3,19},{4,20},{5,21},{6,22},{7,23},{8,24},{9,... | collective-permute-start | bytes 2654216 | tf_op jit(solution)/shard_map/ppermute | solution.py:64
  641.9 58.6 %collective-permute-start.70 = (bf16[2,2,216,640]{3,2,1,0:T(8,128)(2,1)}, bf16[2,2,216,640]{3,2,1,0:T(8,128)(2,1)}, u32[]{:S(2)}, u32[]{:S(2)}) collective-permute-start(bf16[2,2,216,640]{3,2,1,0:T(8,128)(2,1)} %fusion.92), channel_id=1, source_target_pairs={{0,8},{1,9},{2,10},{3,11},{4,12},{5,13},{6,14},{7,15},{8,0},{9,1},... | collective-permute-start | bytes 3317768 | tf_op jit(solution)/shard_map/ppermute | solution.py:64
  698.5 94.9 %collective-permute-start.61 = (bf16[2,2,144,1728]{3,2,1,0:T(8,128)(2,1)}, bf16[2,2,144,1728]{3,2,1,0:T(8,128)(2,1)}, u32[]{:S(2)}, u32[]{:S(2)}) collective-permute-start(bf16[2,2,144,1728]{3,2,1,0:T(8,128)(2,1)} %fusion.73), channel_id=1, source_target_pairs={{0,8},{1,9},{2,10},{3,11},{4,12},{5,13},{6,14},{7,15},{8,0},{9,1},... | collective-permute-start | bytes 5971976 | tf_op jit(solution)/shard_map/ppermute | solution.py:64
  699.9 99.2 %collective-permute-start.64 = (bf16[2,2,144,1728]{3,2,1,0:T(8,128)(2,1)}, bf16[2,2,144,1728]{3,2,1,0:T(8,128)(2,1)}, u32[]{:S(2)}, u32[]{:S(2)}) collective-permute-start(bf16[2,2,144,1728]{3,2,1,0:T(8,128)(2,1)} %fusion.74), channel_id=1, source_target_pairs={{0,16},{1,17},{2,18},{3,19},{4,20},{5,21},{6,22},{7,23},{8,24},{9,... | collective-permute-start | bytes 5971976 | tf_op jit(solution)/shard_map/ppermute | solution.py:64
  702.0 55.7 %collective-permute-start.71 = (bf16[2,216,640]{2,1,0:T(8,128)(2,1)S(1)}, bf16[2,216,640]{2,1,0:T(8,128)(2,1)S(1)}, u32[]{:S(2)}, u32[]{:S(2)}) collective-permute-start(bf16[2,216,640]{2,1,0:T(8,128)(2,1)S(1)} %fusion.125), channel_id=1, source_target_pairs={{0,16},{1,17},{2,18},{3,19},{4,20},{5,21},{6,22},{7,23},{8,24},{9,... | collective-permute-start | bytes 1658888 | tf_op jit(solution)/shard_map/ppermute | solution.py:64
  710.1 50.2 %collective-permute-start.45 = (bf16[256,1152]{1,0:T(8,128)(2,1)S(1)}, bf16[256,1152]{1,0:T(8,128)(2,1)S(1)}, u32[]{:S(2)}, u32[]{:S(2)}) collective-permute-start(bf16[256,1152]{1,0:T(8,128)(2,1)S(1)} %slice.545), channel_id=1, source_target_pairs={{0,2},{1,3},{2,0},{3,1},{4,6},{5,7},{6,4},{7,5},{8,10},{9,11},{10,... | collective-permute-start | bytes 1769480 | tf_op jit(solution)/shard_map/ppermute | solution.py:64
  758.6 44.3 %collective-permute-start.72 = (bf16[216,640]{1,0:T(8,128)(2,1)}, bf16[216,640]{1,0:T(8,128)(2,1)S(1)}, u32[]{:S(2)}, u32[]{:S(2)}) collective-permute-start(bf16[216,640]{1,0:T(8,128)(2,1)} %fusion.135), channel_id=1, source_target_pairs={{0,4},{1,5},{2,6},{3,7},{4,0},{5,1},{6,2},{7,3},{8,12},{9,13},{10,... | collective-permute-start | bytes 829448 | tf_op jit(solution)/shard_map/ppermute | solution.py:64
  793.3 65.3 %collective-permute-start.56 = (bf16[2,2,2,2,48,1152]{5,4,2,3,1,0:T(8,128)(2,1)S(1)}, bf16[2,2,2,2,48,1152]{5,4,2,3,1,0:T(8,128)(2,1)S(1)}, u32[]{:S(2)}, u32[]{:S(2)}) collective-permute-start(bf16[2,2,2,2,48,1152]{5,4,2,3,1,0:T(8,128)(2,1)S(1)} %fusion.75), channel_id=1, source_target_pairs={{0,1},{1,0},{2,3},{3,2},{4,5},{5,4},{6,7},{7,6},{8,9},{9,8},{10,11... | collective-permute-start | bytes 5308424 | tf_op jit(solution)/shard_map/ppermute | solution.py:64
  798.2 23.3 %collective-permute-start.62 = (bf16[2,144,1728]{2,1,0:T(8,128)(2,1)S(1)}, bf16[2,144,1728]{2,1,0:T(8,128)(2,1)S(1)}, u32[]{:S(2)}, u32[]{:S(2)}) collective-permute-start(bf16[2,144,1728]{2,1,0:T(8,128)(2,1)S(1)} %fusion.97), channel_id=1, source_target_pairs={{0,16},{1,17},{2,18},{3,19},{4,20},{5,21},{6,22},{7,23},{8,24},{9,... | collective-permute-start | bytes 2985992 | tf_op jit(solution)/shard_map/ppermute | solution.py:64
  801.4 23.2 %collective-permute-start.65 = (bf16[2,144,1728]{2,1,0:T(8,128)(2,1)S(1)}, bf16[2,144,1728]{2,1,0:T(8,128)(2,1)S(1)}, u32[]{:S(2)}, u32[]{:S(2)}) collective-permute-start(bf16[2,144,1728]{2,1,0:T(8,128)(2,1)S(1)} %fusion.98), channel_id=1, source_target_pairs={{0,8},{1,9},{2,10},{3,11},{4,12},{5,13},{6,14},{7,15},{8,0},{9,1},... | collective-permute-start | bytes 2985992 | tf_op jit(solution)/shard_map/ppermute | solution.py:64
  821.8 35.9 %collective-permute-start.63 = (bf16[144,1728]{1,0:T(8,128)(2,1)S(1)}, bf16[144,1728]{1,0:T(8,128)(2,1)S(1)}, u32[]{:S(2)}, u32[]{:S(2)}) collective-permute-start(bf16[144,1728]{1,0:T(8,128)(2,1)S(1)} %fusion.128), channel_id=1, source_target_pairs={{0,4},{1,5},{2,6},{3,7},{4,0},{5,1},{6,2},{7,3},{8,12},{9,13},{10,... | collective-permute-start | bytes 1493000 | tf_op jit(solution)/shard_map/ppermute | solution.py:64
  824.9 42.5 %collective-permute-start.66 = (bf16[144,1728]{1,0:T(8,128)(2,1)S(1)}, bf16[144,1728]{1,0:T(8,128)(2,1)S(1)}, u32[]{:S(2)}, u32[]{:S(2)}) collective-permute-start(bf16[144,1728]{1,0:T(8,128)(2,1)S(1)} %fusion.129), channel_id=1, source_target_pairs={{0,4},{1,5},{2,6},{3,7},{4,0},{5,1},{6,2},{7,3},{8,12},{9,13},{10,... | collective-permute-start | bytes 1493000 | tf_op jit(solution)/shard_map/ppermute | solution.py:64
  918.1 37.2 %collective-permute-start.46 = (bf16[2,2,2,2,152,256]{5,4,3,2,1,0:T(8,128)(2,1)}, bf16[2,2,2,2,152,256]{5,4,3,2,1,0:T(8,128)(2,1)}, u32[]{:S(2)}, u32[]{:S(2)}) collective-permute-start(bf16[2,2,2,2,152,256]{5,4,3,2,1,0:T(8,128)(2,1)} %fusion.79), channel_id=1, source_target_pairs={{0,1},{1,0},{2,3},{3,2},{4,5},{5,4},{6,7},{7,6},{8,9},{9,8},{10,11... | collective-permute-start | bytes 3735560 | tf_op jit(solution)/shard_map/ppermute | solution.py:64
  946.0 32.3 %collective-permute-start.51 = (bf16[2,2,2,2,56,1536]{5,4,3,2,1,0:T(8,128)(2,1)}, bf16[2,2,2,2,56,1536]{5,4,3,2,1,0:T(8,128)(2,1)}, u32[]{:S(2)}, u32[]{:S(2)}) collective-permute-start(bf16[2,2,2,2,56,1536]{5,4,3,2,1,0:T(8,128)(2,1)} %fusion.66), channel_id=1, source_target_pairs={{0,1},{1,0},{2,3},{3,2},{4,5},{5,4},{6,7},{7,6},{8,9},{9,8},{10,11... | collective-permute-start | bytes 8257544 | tf_op jit(solution)/shard_map/ppermute | solution.py:64
  982.8 31.9 %collective-permute-start.52 = (bf16[2,2,2,56,1536]{4,3,2,1,0:T(8,128)(2,1)S(1)}, bf16[2,2,2,56,1536]{4,3,2,1,0:T(8,128)(2,1)S(1)}, u32[]{:S(2)}, u32[]{:S(2)}) collective-permute-start(bf16[2,2,2,56,1536]{4,3,2,1,0:T(8,128)(2,1)S(1)} %fusion.76), channel_id=1, source_target_pairs={{0,8},{1,9},{2,10},{3,11},{4,12},{5,13},{6,14},{7,15},{8,0},{9,1},... | collective-permute-start | bytes 4128776 | tf_op jit(solution)/shard_map/ppermute | solution.py:64
  991.7 26.1 %collective-permute-start.50 = (bf16[152,256]{1,0:T(8,128)(2,1)S(1)}, bf16[152,256]{1,0:T(8,128)(2,1)S(1)}, u32[]{:S(2)}, u32[]{:S(2)}) collective-permute-start(bf16[152,256]{1,0:T(8,128)(2,1)S(1)} %fusion.178), channel_id=1, source_target_pairs={{0,4},{1,5},{2,6},{3,7},{4,0},{5,1},{6,2},{7,3},{8,12},{9,13},{10,... | collective-permute-start | bytes 233480 | tf_op jit(solution)/shard_map/ppermute | solution.py:64
  (269 other events, 3793.7 us)
Sparse Core Ops, SparseCore 0:
  224.6 27.6 all-gather.2
  345.9 33.4 all-gather.4
  524.7 35.2 reduce-scatter.2
  788.0 34.7 reduce-scatter.4

commit v2 on v1

v2 whole, which is shorter than its diff:
```python
import functools
import itertools
import math

import jax
import jax.numpy as jnp
from jax import lax
from jax.experimental import pallas as pl
from jax.experimental.pallas import tpu as pltpu
from jax.sharding import PartitionSpec as P

H = 4
HD = 256
EPS = 1e-06
NEG = -1e30
ROPE_BASE = 10000.0
AXES = ("fsdp", "blk")
BF = jnp.bfloat16
F32 = jnp.float32


def matmul(left_side, right_side):
    return jnp.dot(left_side, right_side, preferred_element_type=F32)


def matmul_nt(left_side, right_side):
    return lax.dot_general(
        left_side, right_side, (((1,), (1,)), ((), ())), preferred_element_type=F32
    )


def matmul_tn(left_side, right_side):
    return lax.dot_general(
        left_side, right_side, (((0,), (0,)), ((), ())), preferred_element_type=F32
    )


def rounded(values):
    return values.astype(BF)


NAMES = ("y", "x", "p", "h", "c")


class Grid:
    def __init__(self, mesh):
        self.fsdp = mesh.shape["fsdp"]
        self.blk = mesh.shape["blk"]
        self.sizes = {"y": self.fsdp // 2, "x": 2, "p": self.blk // 4, "h": 2, "c": 2}
        self.devices = self.fsdp * self.blk
        self.groups = self.devices // 4

    def places(self):
        f = lax.axis_index("fsdp")
        b = lax.axis_index("blk")
        return {"y": f // 2, "x": f % 2, "p": b // 4, "h": (b // 2) % 2, "c": b % 2}

    def coordinates(self):
        places = self.places()
        return jnp.stack([places[name] for name in NAMES]).astype(jnp.int32)

    def permute(self, values, masks):
        pairs = []
        for f in range(self.fsdp):
            for b in range(self.blk):
                at = {"y": f // 2, "x": f % 2, "p": b // 4, "h": (b // 2) % 2, "c": b % 2}
                for name, mask in masks.items():
                    at[name] = at[name] ^ mask
                pairs.append(
                    (
                        f * self.blk + b,
                        (at["y"] * 2 + at["x"]) * self.blk + at["p"] * 4 + at["h"] * 2 + at["c"],
                    )
                )
        return lax.ppermute(values, AXES, pairs)

    def parts(self, values, name):
        return [values] + [
            self.permute(values, {name: mask}) for mask in range(1, self.sizes[name])
        ]

    def order(self, names):
        out = []
        stride = 1
        for name in names:
            out.append((NAMES.index(name), stride))
            stride *= self.sizes[name]
        return tuple(out)

    def blocks_of(self, names):
        out = []
        for y in range(self.sizes["y"]):
            for x in range(2):
                for p in range(self.sizes["p"]):
                    for h in range(2 if "h" in names else 1):
                        for c in range(2 if "c" in names else 1):
                            out.append((y, x, p, h, c))
        return tuple(out)

    def tokens_in(self, rows):
        other = self.permute(rows, {"h": 1})
        return [rows, other, self.permute(rows, {"c": 1}), self.permute(other, {"c": 1})]

    def extent(self, names):
        return tuple(self.sizes[name] for name in names)


def up8(rows):
    return -(-rows // 8) * 8


TILE = 256
INNER = math.sqrt(2.0 / math.pi)
CUBIC = 0.044715


def chunk_of(rows):
    return min(rows, 256)


LIGHT = pl.CostEstimate(flops=0, bytes_accessed=0, transcendentals=0)


def full(extent):
    return pl.BlockSpec(extent, lambda j: tuple([0] * len(extent)))


ANY = pl.BlockSpec(memory_space=pl.ANY)


def tied(body, operands, ties):
    if not ties:
        return body

    def run(*refs):
        body(*refs[:operands], *refs[operands + len(ties) :])

    return run


def kernel_call(body, grid, in_specs, out_specs, out_shape, scratch, ties=()):
    return pl.pallas_call(
        tied(body, len(in_specs), ties),
        grid=grid,
        in_specs=in_specs + [ANY] * len(ties),
        out_specs=out_specs,
        out_shape=out_shape,
        scratch_shapes=scratch,
        cost_estimate=LIGHT,
        compiler_params=pltpu.CompilerParams(
            dimension_semantics=("arbitrary",), vmem_limit_bytes=48 * 1024 * 1024
        ),
    )


def whole_call(body, out_shape, coordinates, operands, ties=(), scratch=()):
    count = len(operands)
    specs = [pl.BlockSpec(memory_space=pltpu.VMEM)] * count
    if coordinates is not None:
        operands = [coordinates, *operands]
        specs = [pl.BlockSpec(memory_space=pltpu.SMEM)] + specs
    return pl.pallas_call(
        tied(body, len(specs), ties),
        out_shape=out_shape,
        in_specs=specs + [ANY] * len(ties),
        scratch_shapes=list(scratch),
        cost_estimate=LIGHT,
        compiler_params=pltpu.CompilerParams(vmem_limit_bytes=48 * 1024 * 1024),
    )(*operands, *ties)


def left_columns(width):
    return (width // 256) * 128 + 128


def add_rows(start, size, value, own_ref, other_ref):
    half = own_ref.shape[0]
    if start < half:
        own_ref[start : start + size] += value
    else:
        other_ref[start - half : start - half + size] += value


CHUNKS = 4


def send_rows(other_ref, sent_refs):
    count = sent_refs[0].shape[0]
    for number, sent_ref in enumerate(sent_refs):
        sent_ref[...] = rounded(other_ref[number * count : (number + 1) * count])


def sent_chunks(rows, width):
    count = rows // 2 // CHUNKS
    return [full((count, width))] * CHUNKS, [shape(count, width)] * CHUNKS


def ff_forward_body(
    x0_ref, x1_ref, x2_ref, x3_ref, wg_ref, wu_ref, wd_ref, own_ref, g_ref, u_ref, *sent_refs
):
    *sent_refs, other_ref = sent_refs
    size = x0_ref.shape[0]

    @pl.when(pl.program_id(0) == 0)
    def _():
        own_ref[...] = jnp.zeros_like(own_ref)
        other_ref[...] = jnp.zeros_like(other_ref)

    wg, wu, wd = wg_ref[...], wu_ref[...], wd_ref[...]
    for number, x_ref in enumerate((x0_ref, x1_ref, x2_ref, x3_ref)):
        start = number * size
        part = slice(start, start + size)
        x = x_ref[...]
        gate = matmul(x, wg)
        up = matmul(x, wu)
        g_ref[part] = rounded(gate)
        u_ref[part] = rounded(up)
        bent = jnp.tanh(INNER * (gate + CUBIC * (gate * gate * gate)))
        hidden = rounded(0.5 * gate * (1.0 + bent) * up)
        add_rows(start, size, matmul(hidden, wd), own_ref, other_ref)

    @pl.when(pl.program_id(0) == pl.num_programs(0) - 1)
    def _():
        send_rows(other_ref, sent_refs)


def ff_forward(blocks, w_gate, w_up, w_down, ties=()):
    size, width = blocks[0].shape
    rows = 4 * size
    wide = w_gate.shape[1]
    column = pl.BlockSpec((rows, TILE), lambda j: (0, j))
    return kernel_call(
        ff_forward_body,
        (wide // TILE,),
        [full((size, width))] * 4
        + [
            pl.BlockSpec((width, TILE), lambda j: (0, j)),
            pl.BlockSpec((width, TILE), lambda j: (0, j)),
            pl.BlockSpec((TILE, width), lambda j: (j, 0)),
        ],
        [full((rows // 2, width)), column, column] + sent_chunks(rows, width)[0],
        [
            jax.ShapeDtypeStruct((rows // 2, width), F32),
            jax.ShapeDtypeStruct((rows, wide), BF),
            jax.ShapeDtypeStruct((rows, wide), BF),
        ]
        + sent_chunks(rows, width)[1],
        [pltpu.VMEM((rows // 2, width), F32)],
        ties,
    )(*blocks, w_gate, w_up, w_down, *ties)


def ff_backward_body(with_old, *refs):
    block_refs = refs[:4]
    g_ref, u_ref, wg_ref, wu_ref, wd_ref = refs[4:9]
    old_refs = refs[9:11] if with_old else None
    (
        own_ref, dg_ref, du_ref, dl_ref, dr_ref, *sent_refs, hidden_ref, other_ref, gg_ref,
    ) = refs[11 if with_old else 9 :]
    size = block_refs[0].shape[0]
    rows = 4 * size

    @pl.when(pl.program_id(0) == 0)
    def _():
        own_ref[...] = jnp.zeros_like(own_ref)
        other_ref[...] = jnp.zeros_like(other_ref)
        for number, block_ref in enumerate(block_refs):
            gg_ref[number * size : (number + 1) * size] = block_ref[...]

    wg, wu, wd = wg_ref[...], wu_ref[...], wd_ref[...]
    for start in range(0, rows, size):
        part = slice(start, start + size)
        grad = matmul_nt(gg_ref[part], wd)
        gate = g_ref[part].astype(F32)
        up = u_ref[part].astype(F32)
        square = gate * gate
        bent = jnp.tanh(INNER * (gate + CUBIC * (square * gate)))
        half = 0.5 * (1.0 + bent)
        gelu = gate * half
        slope = half + (0.5 * INNER) * gate * (1.0 - bent * bent) * (1.0 + (3.0 * CUBIC) * square)
        hidden_ref[part] = rounded(gelu * up)
        grad_gate = rounded(grad * up * slope)
        grad_up = rounded(grad * gelu)
        dg_ref[part] = grad_gate
        du_ref[part] = grad_up
        add_rows(
            start, size, matmul_nt(grad_gate, wg) + matmul_nt(grad_up, wu), own_ref, other_ref
        )
    total = matmul_tn(hidden_ref[...], gg_ref[...])
    left = dl_ref.shape[1]
    for number, (out_ref, part) in enumerate(((dl_ref, total[:, :left]), (dr_ref, total[:, left:]))):
        if old_refs is not None:
            part = part + old_refs[number][...].astype(F32)
        out_ref[...] = rounded(part)

    @pl.when(pl.program_id(0) == pl.num_programs(0) - 1)
    def _():
        send_rows(other_ref, sent_refs)


def ff_backward(blocks, gate, up, w_gate, w_up, w_down, old, ties=()):
    size, width = blocks[0].shape
    rows = 4 * size
    wide = w_gate.shape[1]
    left = left_columns(width)
    column = pl.BlockSpec((rows, TILE), lambda j: (0, j))
    halves = [pl.BlockSpec((TILE, cols), lambda j: (j, 0)) for cols in (left, width - left)]
    in_specs = [full((size, width))] * 4 + [
        column,
        column,
        pl.BlockSpec((width, TILE), lambda j: (0, j)),
        pl.BlockSpec((width, TILE), lambda j: (0, j)),
        pl.BlockSpec((TILE, width), lambda j: (j, 0)),
    ]
    operands = [*blocks, gate, up, w_gate, w_up, w_down]
    if old is not None:
        in_specs += halves
        operands += list(old)
    return kernel_call(
        functools.partial(ff_backward_body, old is not None),
        (wide // TILE,),
        in_specs,
        [full((rows // 2, width)), column, column] + halves + sent_chunks(rows, width)[0],
        [
            jax.ShapeDtypeStruct((rows // 2, width), F32),
            jax.ShapeDtypeStruct((rows, wide), BF),
            jax.ShapeDtypeStruct((rows, wide), BF),
            jax.ShapeDtypeStruct((wide, left), BF),
            jax.ShapeDtypeStruct((wide, width - left), BF),
        ]
        + sent_chunks(rows, width)[1],
        [
            pltpu.VMEM((rows, TILE), BF),
            pltpu.VMEM((rows // 2, width), F32),
            pltpu.VMEM((rows, width), BF),
        ],
        ties,
    )(*operands, *ties)


def ff_weights_body(with_old, *refs):
    x_refs = refs[:4]
    dg_ref, du_ref = refs[4:6]
    old_refs = refs[6:8] if with_old else (None, None)
    wg_ref, wu_ref, turned_ref = refs[8 if with_old else 6 :]
    size = x_refs[0].shape[0]

    @pl.when(pl.program_id(0) == 0)
    def _():
        for number, x_ref in enumerate(x_refs):
            turned_ref[:, number * size : (number + 1) * size] = x_ref[...].T

    for grad_ref, old_ref, out_ref in (
        (dg_ref, old_refs[0], wg_ref),
        (du_ref, old_refs[1], wu_ref),
    ):
        total = matmul(turned_ref[...], grad_ref[...])
        if old_ref is not None:
            total = total + old_ref[...].astype(F32)
        out_ref[...] = rounded(total)


def ff_weights(blocks, grad_gate, grad_up, old, ties=()):
    size, width = blocks[0].shape
    rows = 4 * size
    wide = grad_gate.shape[1]
    column = pl.BlockSpec((rows, TILE), lambda j: (0, j))
    block = pl.BlockSpec((width, TILE), lambda j: (0, j))
    operands = [*blocks, grad_gate, grad_up] + (list(old) if old is not None else [])
    return kernel_call(
        functools.partial(ff_weights_body, old is not None),
        (wide // TILE,),
        [full((size, width))] * 4
        + [column, column]
        + ([block, block] if old is not None else []),
        [block, block],
        [jax.ShapeDtypeStruct((width, wide), BF)] * 2,
        [pltpu.VMEM((width, rows), BF)],
        ties,
    )(*operands, *ties)


def stack_body(plan, *refs):
    out_at = sum(count for count, pick, columns in plan)
    at = 0
    for count, pick, columns in plan:
        group = refs[at : at + count]
        at += count
        for column in columns:
            out_ref = refs[out_at]
            out_at += 1
            for index, ref in enumerate(group):
                place = () if pick is None else (pick,)
                value = ref[place + (Ellipsis, column)]
                if count == 1:
                    out_ref[...] = value
                else:
                    out_ref[index] = value


def stack(items, ties=()):
    plan = []
    outs = []
    operands = []
    for parts, pick, widths in items:
        extent = parts[0].shape if pick is None else parts[0].shape[1:]
        widths = widths or [extent[-1]]
        if len(parts) > 1:
            extent = (len(parts),) + extent
        columns = []
        start = 0
        for columns_wide in widths:
            columns.append(slice(start, start + columns_wide))
            start += columns_wide
            outs.append(jax.ShapeDtypeStruct(extent[:-1] + (columns_wide,), parts[0].dtype))
        plan.append((len(parts), pick, columns))
        operands += parts
    return whole_call(functools.partial(stack_body, plan), outs, None, operands, ties)


def fold_body(plan, coords_ref, *refs):
    at = 0
    out_at = sum(count for item in plan for count in item["counts"])
    for item in plan:
        names, stage, size = item["names"], item["stage"], item["size"]
        outs = refs[out_at : out_at + size]
        out_at += size
        position = names.index(stage)
        own = coords_ref[NAMES.index(stage)]
        rest = [range(extent) for number, extent in enumerate(item["extent"]) if number != position]
        column = 0
        for count in item["counts"]:
            group = refs[at : at + count]
            at += count
            rows, cols = group[0].shape[-2:]
            for mask in range(size):
                for index in itertools.product(*rest):
                    source = index[:position] + (own ^ mask,) + index[position:]
                    if count == 1:
                        value = group[0][source]
                    else:
                        value = group[0][source].astype(F32)
                        for other in group[1:]:
                            value = value + other[source].astype(F32)
                        value = rounded(value)
                    out = outs[mask]
                    out[index + (slice(0, rows), slice(column, column + cols))] = value
                    if rows < out.shape[-2]:
                        out[index + (slice(rows, None), slice(column, column + cols))] = jnp.zeros(
                            (out.shape[-2] - rows, cols), out.dtype
                        )
            column += cols


def fold(grid, coordinates, items, ties=()):
    plan = []
    outs = []
    operands = []
    for names, stage, groups in items:
        rows = max(group[0].shape[-2] for group in groups)
        cols = sum(group[0].shape[-1] for group in groups)
        left = tuple(name for name in names if name != stage)
        size = grid.sizes[stage]
        plan.append(
            {
                "names": names,
                "stage": stage,
                "size": size,
                "extent": grid.extent(names),
                "counts": [len(group) for group in groups],
            }
        )
        outs += [jax.ShapeDtypeStruct(grid.extent(left) + (rows, cols), BF)] * size
        for group in groups:
            operands += [
                value.reshape(grid.extent(names) + value.shape[-2:]) for value in group
            ]
    results = whole_call(
        functools.partial(fold_body, plan), outs, coordinates, operands, ties
    )
    folded = []
    at = 0
    for names, stage, groups in items:
        size = grid.sizes[stage]
        kept = [results[at]] + [
            grid.permute(results[at + mask], {stage: mask}) for mask in range(1, size)
        ]
        folded.append((tuple(name for name in names if name != stage), kept))
        at += size
    return folded


def pair_body(own_ref, *refs):
    came_refs, (own_out, sent_out) = refs[:-2], refs[-2:]
    count = own_out.shape[0]
    step = came_refs[0].shape[0]
    for number, came_ref in enumerate(came_refs):
        start = number * step
        total = own_ref[start : start + step] + came_ref[...].astype(F32)
        if start < count:
            own_out[start : start + step] = total
        else:
            sent_out[start - count : start - count + step] = rounded(total)


def tokens_out(grid, own, sent, ties=()):
    came = [grid.permute(part, {"c": 1}) for part in sent]
    count, width = own.shape[0] // 2, own.shape[1]
    own, sent = whole_call(
        pair_body, [shape(count, width, F32), shape(count, width)], None, [own, *came], ties
    )
    return own, grid.permute(sent, {"h": 1})


def fetch(coords_ref, refs, order, block, place):
    index = 0
    for number, stride in order[:-1]:
        index = index + (coords_ref[number] ^ block[number]) * stride
    last = order[-1][0]
    side = coords_ref[last] ^ block[last]
    value = refs[-1][(index,) + place]
    for number in range(len(refs) - 1):
        value = jnp.where(side == number, refs[number][(index,) + place], value)
    return value


def quarter_of(coords_ref):
    return coords_ref[3] * 2 + coords_ref[4]


def cut_body(groups, block, block_up, coords_ref, w_ref, *refs):
    out_refs, held_ref = refs[:-1], refs[-1]
    own = quarter_of(coords_ref)
    held_ref[...] = jnp.zeros_like(held_ref)
    for quarter in range(4):
        slot = own ^ quarter
        for kind in range(2):
            for group in range(groups):
                at = kind * groups * 4 * block + (group * 4 + quarter) * block
                held_ref[slot, kind, :, group * block_up : group * block_up + block] = w_ref[
                    :, at : at + block
                ]
    for mask, out_ref in enumerate(out_refs):
        out_ref[...] = held_ref[mask]


def pick_of(own, refs, quarter):
    value = refs[3]
    for mask in range(3):
        value = jnp.where(own == quarter ^ mask, refs[mask], value)
    return value


def pieces_body(coords_ref, p0_ref, p1_ref, p2_ref, p3_ref, out_ref):
    own = quarter_of(coords_ref)
    rows = p0_ref.shape[1]
    for kind in range(2):
        refs = [ref[kind] for ref in (p0_ref, p1_ref, p2_ref, p3_ref)]
        for quarter in range(4):
            out_ref[kind, quarter * rows : (quarter + 1) * rows] = pick_of(own, refs, quarter)


def split_body(count, coords_ref, *refs):
    own = quarter_of(coords_ref)
    outs = refs[2 * count :]
    rows = outs[0].shape[1]
    for kind in range(2):
        total = refs[kind * count][...].astype(F32)
        for ref in refs[kind * count + 1 : (kind + 1) * count]:
            total = total + ref[...].astype(F32)
        total = rounded(total)
        for mask, out_ref in enumerate(outs):
            value = total[3 * rows :]
            for quarter in range(3):
                value = jnp.where(
                    own == quarter ^ mask, total[quarter * rows : (quarter + 1) * rows], value
                )
            out_ref[kind] = value


def join_body(groups, block, block_up, coords_ref, p0_ref, p1_ref, p2_ref, p3_ref, out_ref):
    own = quarter_of(coords_ref)
    for kind in range(2):
        refs = [ref[kind] for ref in (p0_ref, p1_ref, p2_ref, p3_ref)]
        for quarter in range(4):
            piece = pick_of(own, refs, quarter).astype(F32)
            for group in range(groups):
                at = kind * groups * 4 * block + (group * 4 + quarter) * block
                out_ref[:, at : at + block] = piece[
                    :, group * block_up : group * block_up + block
                ]


def order_body(blocks, orders, coords_ref, *refs):
    out_ref = refs[-1]
    count = (len(refs) - 1) // len(orders)
    at = 0
    for group, order in enumerate(orders):
        group_refs = refs[group * count : (group + 1) * count]
        rows, cols = group_refs[0].shape[1:]
        for number, block in enumerate(blocks):
            out_ref[number * rows : (number + 1) * rows, at : at + cols] = fetch(
                coords_ref, group_refs, order, block, (slice(None), slice(None))
            )
        at += cols


def in_order(grid, coordinates, *columns, ties=()):
    blocks = grid.blocks_of("pxy")
    orders = []
    flat = []
    count = max(len(parts) for parts, names in columns)
    for parts, names in columns:
        parts = [part.reshape((-1,) + part.shape[-2:]) for part in parts]
        order = grid.order(names)
        if len(parts) < count:
            parts = [jnp.concatenate(parts)]
            parts += parts * (count - 1)
            order = order + ((order[-1][0], -1),)
        flat += parts
        orders.append(order)
    rows = flat[0].shape[1]
    cols = sum(parts[0].shape[-1] for parts, names in columns)
    return whole_call(
        functools.partial(order_body, blocks, tuple(orders)),
        jax.ShapeDtypeStruct((grid.groups * rows, cols), flat[0].dtype),
        coordinates,
        flat,
        ties,
    )


def spread_body(sizes, coords_ref, normed_ref, low_ref, mixed_ref, side_ref, *refs):
    own_ref, sent_ref, held_ref = refs
    devices, qkv, joined, lift, lift_at, out, mixed, last, last_at = sizes
    held_ref[...] = jnp.zeros_like(held_ref)
    second = devices // 2 * joined
    for number in range(devices):
        core, place = number % 2, number // 2
        at = place * joined
        held_ref[core, :, at : at + qkv] = normed_ref[:, number * qkv : (number + 1) * qkv]
        at = at + lift_at
        held_ref[core, :, at : at + lift] = low_ref[:, number * lift : (number + 1) * lift]
        at = second + place * mixed
        held_ref[core, :, at : at + out] = mixed_ref[:, number * out : (number + 1) * out]
        at = at + last_at
        held_ref[core, :, at : at + last] = side_ref[:, number * last : (number + 1) * last]
    own_ref[...] = held_ref[coords_ref[4]]
    sent_ref[...] = held_ref[1 - coords_ref[4]]


def unpack_first_body(blocks, order, sizes, count, coords_ref, *refs):
    chunks = [refs[at : at + count] for at in range(0, len(refs) - 4, count)]
    w_ref, lift_ref, down_ref, gain_ref = refs[-4:]
    rows, rows_up, lift_rows, gain_cols = sizes
    gain_ref[...] = jnp.zeros_like(gain_ref)
    main = slice(0, rows)
    lift = slice(rows_up, rows_up + lift_rows)
    every = slice(None)
    for number, block in enumerate(blocks):
        place = slice(number * rows, (number + 1) * rows)
        lift_place = slice(number * lift_rows, (number + 1) * lift_rows)
        at = 0
        for chunk in chunks[:-1]:
            columns = slice(at, at + chunk[0].shape[-1])
            w_ref[place, columns] = fetch(coords_ref, chunk, order, block, (main, every))
            lift_ref[lift_place, columns] = fetch(coords_ref, chunk, order, block, (lift, every))
            at = columns.stop
        down_ref[place, :] = fetch(coords_ref, chunks[-1], order, block, (main, every))
        gain_ref[0:2, number * gain_cols : (number + 1) * gain_cols] = fetch(
            coords_ref,
            chunks[-1],
            order,
            block,
            (slice(rows_up, rows_up + 2), slice(0, gain_cols)),
        ).astype(F32)


def unpack_second_body(blocks, order, sizes, count, coords_ref, *refs):
    chunks = [refs[at : at + count] for at in range(0, len(refs) - 5, count)]
    out_ref, lift0_ref, lift1_ref, down_ref, late_ref = refs[-5:]
    rows, rows_up, lift_rows, lift_up, late_rows, late_up = sizes
    every = slice(None)
    main = slice(0, rows)
    fold_cols = chunks[-1][0].shape[-1]
    for number, block in enumerate(blocks):

        def get(chunk, start, size):
            return fetch(coords_ref, chunk, order, block, (slice(start, start + size), every))

        place = slice(number * rows, (number + 1) * rows)
        lift_place = slice(number * lift_rows, (number + 1) * lift_rows)
        at = 0
        for chunk in chunks[:-2]:
            columns = slice(at, at + chunk[0].shape[-1])
            out_ref[place, columns] = get(chunk, 0, rows)
            lift0_ref[lift_place, columns] = get(chunk, rows_up, lift_rows)
            lift1_ref[lift_place, columns] = get(chunk, rows_up + lift_up, lift_rows)
            at = columns.stop
        down_ref[place, :] = get(chunks[-2], 0, rows)
        late_place = slice(number * late_rows, (number + 1) * late_rows)
        for part in range(late_ref.shape[1] // fold_cols):
            late_ref[late_place, part * fold_cols : (part + 1) * fold_cols] = get(
                chunks[-1], part * late_up, late_rows
            )


def rotate(values, cosine_table, sine_table):
    halfway = values.shape[-1] // 2
    first_half = values[..., :halfway]
    second_half = values[..., halfway:]
    return jnp.concatenate(
        [
            first_half * cosine_table - second_half * sine_table,
            second_half * cosine_table + first_half * sine_table,
        ],
        axis=-1,
    )


def inverse_size(values):
    return lax.rsqrt(jnp.mean(values * values, axis=-1, keepdims=True) + EPS)


def norm_back(values, gain_row, grad):
    inverse = inverse_size(values)
    weighted = grad * gain_row
    inner = jnp.mean(weighted * values, axis=-1, keepdims=True)
    gain_grad = jnp.sum(grad * values * inverse, axis=0, keepdims=True)
    return inverse * weighted - values * (inverse * inverse * inverse) * inner, gain_grad


def shape(rows, cols, kind=BF):
    return jax.ShapeDtypeStruct((rows, cols), kind)


def pack_body(
    sizes, wq_ref, qd_ref, ql_ref, gain_ref, wo_ref, od_ref, ol_ref, first_ref, second_ref
):
    qkv_up, ql_up, out_up, ol_up = sizes
    for ref in (first_ref, second_ref):
        ref[...] = jnp.zeros_like(ref)
    rows, cols = wq_ref.shape
    lift_rows = ql_ref.shape[1]
    rank = qd_ref.shape[2]
    first_ref[:rows, :cols] = wq_ref[...]
    first_ref[qkv_up : qkv_up + lift_rows, :cols] = ql_ref[0]
    for loop in range(2):
        at = cols + loop * rank
        first_ref[:rows, at : at + rank] = qd_ref[loop]
    first_ref[qkv_up : qkv_up + 2, cols : cols + gain_ref.shape[1]] = gain_ref[...]
    rows, width = wo_ref.shape
    last_rows = ol_ref.shape[1]
    second_ref[:rows, :width] = wo_ref[...]
    for loop in range(2):
        at = out_up + loop * ol_up
        second_ref[at : at + last_rows, :width] = ol_ref[loop]
        at = width + loop * rank
        second_ref[:rows, at : at + rank] = od_ref[loop]
    for part in range(cols // rank):
        second_ref[part * ql_up : part * ql_up + lift_rows, width + 2 * rank :] = ql_ref[
            1, :, part * rank : (part + 1) * rank
        ]


def halves_body(w_ref, left_ref, right_ref):
    rows = w_ref.shape[0]
    left = left_ref.shape[1]
    for ref in (left_ref, right_ref):
        ref[...] = jnp.zeros_like(ref)
    left_ref[:rows] = w_ref[:, :left]
    right_ref[:rows] = w_ref[:, left:]


def project_kv_body(first_loop, addends, *refs):
    add_refs = refs[:addends]
    gain_ref, qd_ref, w_ref, ql_ref, cos_ref, sin_ref = refs[addends : addends + 6]
    kv_ref, normed_ref, low_ref, residual_ref = refs[addends + 6 :]
    rank = low_ref.shape[1]
    width_q = w_ref.shape[1] - 2 * HD
    values = add_refs[0][...].astype(F32)
    for ref in add_refs[1:]:
        values = values + ref[...].astype(F32)
    residual_ref[...] = values
    normed = rounded(values * inverse_size(values) * gain_ref[0:1])
    normed_ref[...] = normed
    down = qd_ref[:, :rank] if first_loop else qd_ref[:, rank:]
    low = rounded(matmul(normed, down))
    low_ref[...] = low
    kv = matmul(normed, w_ref[:, width_q:]) + matmul(low, ql_ref[:, width_q:])
    kv_ref[:, :HD] = rounded(rotate(kv[:, :HD], cos_ref[...], sin_ref[...]))
    kv_ref[:, HD:] = rounded(kv[:, HD:])


def project_q_body(normed_ref, low_ref, w_ref, ql_ref, cos_ref, sin_ref, q_ref):
    for head in range(H):
        at = slice(head * HD, (head + 1) * HD)
        part = matmul(normed_ref[...], w_ref[:, at]) + matmul(low_ref[...], ql_ref[:, at])
        q_ref[:, at] = rounded(rotate(part, cos_ref[...], sin_ref[...]) * HD ** (-0.5))


def mask_of(segs_ref, places_ref, row_ref):
    seq_len = row_ref.shape[1]
    key_places = lax.broadcasted_iota(jnp.int32, (segs_ref.shape[0], seq_len), 1)
    allowed = (segs_ref[...] == row_ref[...]) & (key_places <= places_ref[...])
    return jnp.where(allowed, 0.0, NEG)


def attend_body(q_ref, kv_ref, segs_ref, places_ref, row_ref, mixed_ref, log_ref):
    mask = mask_of(segs_ref, places_ref, row_ref)
    for head in range(H):
        at = slice(head * HD, (head + 1) * HD)
        scores = matmul_nt(q_ref[:, at], kv_ref[:, :HD]) + mask
        top = jnp.max(scores, axis=1, keepdims=True)
        probabilities = jnp.exp(scores - top)
        total = jnp.sum(probabilities, axis=1, keepdims=True)
        mixed_ref[:, at] = rounded(matmul(rounded(probabilities), kv_ref[:, HD:]) / total)
        log_ref[head] = top + jnp.log(total)


def attend_back_body(
    q_ref, kv_ref, segs_ref, places_ref, row_ref, log_ref, grad_ref, cos_ref, sin_ref,
    coords_ref, own_ref, sent_ref, gq_ref, keys_ref, values_ref,
):
    mask = mask_of(segs_ref, places_ref, row_ref)
    size = own_ref.shape[1]
    for head in range(H):
        at = slice(head * HD, (head + 1) * HD)
        queries = q_ref[:, at]
        grad = grad_ref[:, at]
        probabilities = jnp.exp(matmul_nt(queries, kv_ref[:, :HD]) + mask - log_ref[head])
        grad_probs = matmul_nt(grad, kv_ref[:, HD:])
        weighted = probabilities * grad_probs
        delta = jnp.sum(weighted, axis=1, keepdims=True)
        grad_scores = rounded(weighted - probabilities * delta)
        grad_q = matmul(grad_scores, kv_ref[:, :HD])
        gq_ref[:, at] = rounded(rotate(grad_q, cos_ref[...], -sin_ref[...]) * HD ** (-0.5))
        key_term = matmul_tn(grad_scores, queries)
        value_term = matmul_tn(rounded(probabilities), grad)
        if head == 0:
            keys_ref[...] = key_term
            values_ref[...] = value_term
        else:
            keys_ref[...] += key_term
            values_ref[...] += value_term
    core = coords_ref[4]
    for number in range(own_ref.shape[0]):
        for out_ref, which in ((own_ref, core), (sent_ref, 1 - core)):
            place = pl.ds(pl.multiple_of((2 * number + which) * size, size), size)
            out_ref[number, :, :HD] = rounded(keys_ref[place, :])
            out_ref[number, :, HD:] = rounded(values_ref[place, :])


def leave_body(
    first_loop, mixed_ref, od_ref, w_ref, ol_ref, residual_ref, gain_ref,
    side_ref, middle_ref, normed_ref,
):
    rank = side_ref.shape[1]
    down = od_ref[:, :rank] if first_loop else od_ref[:, rank:]
    side = rounded(matmul(mixed_ref[...], down))
    side_ref[...] = side
    middle = residual_ref[...] + (matmul(mixed_ref[...], w_ref[...]) + matmul(side, ol_ref[...]))
    middle_ref[...] = middle
    normed_ref[...] = rounded(middle * inverse_size(middle) * gain_ref[1:2])


def enter_back_body(
    first_loop, own_ref, other_ref, result_ref, middle_ref, gain_ref, w_ref, ol_ref, od_ref,
    grad_ref, branch_ref, side_ref, mixed_ref, gain_grad_ref,
):
    rank = side_ref.shape[1]
    grad_normed = own_ref[...] + other_ref[...].astype(F32)
    back, gain_grad = norm_back(middle_ref[...], gain_ref[1:2], grad_normed)
    gain_grad_ref[...] = jnp.broadcast_to(gain_grad, gain_grad_ref.shape)
    grad = result_ref[...].astype(F32) + back
    grad_ref[...] = grad
    branch = rounded(grad)
    branch_ref[...] = branch
    side = rounded(matmul_nt(branch, ol_ref[...]))
    side_ref[...] = side
    down = od_ref[:, :rank] if first_loop else od_ref[:, rank:]
    mixed_ref[...] = rounded(matmul_nt(branch, w_ref[...]) + matmul_nt(side, down))


def rope_back_body(count, *refs):
    gq_ref, ql_ref, cos_ref, sin_ref, out_ref, low_ref = refs[count:]
    width_q = gq_ref.shape[1]
    kv = refs[0][...].astype(F32)
    for ref in refs[1:count]:
        kv = kv + ref[...].astype(F32)
    keys = rounded(rotate(kv[:, :HD], cos_ref[...], -sin_ref[...]))
    values = rounded(kv[:, HD:])
    out_ref[:, :HD] = keys
    out_ref[:, HD:] = values
    low_ref[...] = rounded(
        matmul_nt(gq_ref[...], ql_ref[:, :width_q])
        + matmul_nt(keys, ql_ref[:, width_q : width_q + HD])
        + matmul_nt(values, ql_ref[:, width_q + HD :])
    )


def leave_back_body(
    first_loop, kv_ref, gq_ref, low_ref, w_ref, qd_ref, residual_ref, gain_ref, grad_ref,
    other_gain_ref, *refs,
):
    out_ref, out_b_ref, gain_grad_ref = refs[-3:]
    rank = low_ref.shape[1]
    width_q = gq_ref.shape[1]
    down = qd_ref[:, :rank] if first_loop else qd_ref[:, rank:]
    grad_normed = (
        matmul_nt(gq_ref[...], w_ref[:, :width_q])
        + matmul_nt(kv_ref[...], w_ref[:, width_q:])
        + matmul_nt(low_ref[...], down)
    )
    back, gain_grad = norm_back(residual_ref[...], gain_ref[0:1], grad_normed)
    gain_grad_ref[0:1] = gain_grad
    gain_grad_ref[1:2] = other_gain_ref[1:2]
    if len(refs) > 3:
        gain_grad_ref[0:2] += refs[0][0:2]
    grad = grad_ref[...] + back
    out_ref[...] = grad
    out_b_ref[...] = rounded(grad)


def late_body(sizes, coords_ref, kv_ref, qd_ref, *refs):
    count, rows, gain_cols = sizes
    gain_refs, out_ref = refs[:-1], refs[-1]
    kv_cols = kv_ref.shape[2]
    out_ref[:, :, :kv_cols] = kv_ref[...]
    out_ref[:, :, kv_cols:] = qd_ref[...]
    for row in range(2):
        gains = rounded(gain_refs[0][row : row + 1] + gain_refs[1][row : row + 1])
        for number in range(count):
            at = 2 * number * gain_cols
            value = jnp.where(
                coords_ref[4] == 0,
                gains[:, at : at + gain_cols],
                gains[:, at + gain_cols : at + 2 * gain_cols],
            )
            out_ref[number, rows + row : rows + row + 1, kv_cols : kv_cols + gain_cols] = value


def down_body(count, *refs):
    out_ref = refs[-1]
    at = 0
    for group in range(2):
        value = refs[group * count][...].astype(F32)
        for ref in refs[group * count + 1 : (group + 1) * count]:
            value = value + ref[...].astype(F32)
        out_ref[:, at : at + value.shape[1]] = value[: out_ref.shape[0]]
        at += value.shape[1]


def result_body(middle_ref, own_ref, other_ref, out_ref):
    out_ref[...] = rounded(middle_ref[...] + (own_ref[...] + other_ref[...].astype(F32)))


def finish_body(count, sizes, *refs):
    rows, rows_up, lift_rows, lift_up, out_rows, out_up, last_rows, last_up, gain_cols = sizes
    totals = []
    for group in range(3):
        value = refs[group * count][...].astype(F32)
        for ref in refs[group * count + 1 : (group + 1) * count]:
            value = value + ref[...].astype(F32)
        totals.append(value)
    outs, queries, late = totals
    gains_ref, qkv_ref, out_ref, qd_ref, ql_ref, od_ref, ol_ref = refs[3 * count :]
    width = out_ref.shape[1]
    rank = qd_ref.shape[2]
    half = queries.shape[1] - rank
    rest = qkv_ref.shape[1] - half
    gains_ref[...] = late[rows : rows + 2, rest : rest + gain_cols]
    qkv_ref[:, :half] = queries[:rows, :half]
    qkv_ref[:, half:] = late[:rows, :rest]
    out_ref[...] = outs[:out_rows, :width]
    qd_ref[0] = late[:rows, rest:]
    qd_ref[1] = queries[:rows, half:]
    for loop in range(2):
        at = rows_up + loop * lift_up
        ql_ref[loop, :, :half] = queries[at : at + lift_rows, :half]
        ql_ref[loop, :, half:] = late[at : at + lift_rows, :rest]
        at = width + loop * rank
        od_ref[loop] = outs[:out_rows, at : at + rank]
        at = out_up + loop * last_up
        ol_ref[loop] = outs[at : at + last_rows, :width]


def outer_body(columns, rights, olds, own_ref, came_ref, *refs):
    out_refs = refs[2 * rights + olds :]
    own, came = own_ref[:, columns], came_ref[:, columns]
    for number in range(rights):
        right_ref, right_came_ref = refs[2 * number], refs[2 * number + 1]
        out_ref = out_refs[number]
        cols = out_ref.shape[1]
        step = 512 if cols % 512 == 0 else 384 if cols % 384 == 0 else cols
        for start in range(0, cols, step):
            part = slice(start, start + step)
            total = matmul_tn(own, right_ref[:, part]) + matmul_tn(came, right_came_ref[:, part])
            if number < olds:
                total = total + refs[2 * rights + number][:, part].astype(F32)
            out_ref[:, part] = rounded(total)


def outer(left, columns, rights, olds=(), ties=()):
    rows = columns.stop - columns.start
    return whole_call(
        functools.partial(outer_body, columns, len(rights), len(olds)),
        [shape(rows, right[0].shape[1]) for right in rights],
        None,
        [*left, *[value for right in rights for value in right], *olds],
        ties,
    )


def per_device(
    grid,
    inputs,
    segments,
    cotangent,
    norm_gain_rows,
    query_key_value_weight,
    output_weight,
    gate_up_weight,
    down_weight,
    adapter_query_down,
    adapter_query_lift,
    adapter_output_down,
    adapter_output_lift,
):
    tokens = inputs.shape[0]
    width = inputs.shape[1]
    groups = grid.groups
    gain_cols = norm_gain_rows.shape[1]
    qkv_rows = query_key_value_weight.shape[0]
    out_rows = output_weight.shape[0]
    ql_rows = adapter_query_lift.shape[1]
    ol_rows = adapter_output_lift.shape[1]
    rank = adapter_query_down.shape[2]
    hidden_block = down_weight.shape[0]
    width_q = H * HD

    qkv_up, ql_up = up8(qkv_rows), up8(ql_rows)
    out_up, ol_up = up8(out_rows), up8(ol_rows)
    wide = -(-groups * hidden_block // TILE) * TILE
    block_up = wide // groups
    qkv_cols = query_key_value_weight.shape[1]
    left_cols = left_columns(width)
    coordinates = grid.coordinates()
    straight = ("p", "h", "x", "y", "c")
    turned = ("p", "h", "y", "x", "c")

    def flat(parts):
        return [part.reshape((-1,) + part.shape[-2:]) for part in parts]

    def parts(values, name):
        return grid.parts(values, name)

    segrow = segments[0]
    seq_len = segrow.shape[0]
    position = lax.axis_index("blk")
    places = position * tokens + jnp.arange(tokens, dtype=jnp.int32)
    own_segs = lax.dynamic_slice_in_dim(segrow, position * tokens, tokens, 0)
    below_one = jnp.sum((segrow < 1).astype(jnp.int32))
    below_two = jnp.sum((segrow < 2).astype(jnp.int32))
    starts = jnp.where(own_segs == 0, 0, jnp.where(own_segs == 1, below_one, below_two))
    offsets = (places - starts).astype(F32)
    frequency = jnp.exp(jnp.arange(HD // 2, dtype=F32) * (-2.0 * math.log(ROPE_BASE) / HD))
    angles = offsets[:, None] * frequency[None, :]
    tables = [jnp.cos(angles), jnp.sin(angles)]
    masks = [own_segs[:, None], places[:, None], segments]

    second_rows = max(out_up + 2 * ol_up, qkv_cols // rank * ql_up)
    first, second = whole_call(
        functools.partial(pack_body, (qkv_up, ql_up, out_up, ol_up)),
        [shape(qkv_up + ql_up, qkv_cols + 2 * rank), shape(second_rows, width + 3 * rank)],
        None,
        [
            query_key_value_weight, adapter_query_down, adapter_query_lift, norm_gain_rows,
            output_weight, adapter_output_down, adapter_output_lift,
        ],
    )
    first, second = stack([(parts(first, "p"), None, None), (parts(second, "p"), None, None)])
    cut = whole_call(
        functools.partial(cut_body, groups, hidden_block, block_up),
        [jax.ShapeDtypeStruct((2, qkv_rows, wide), BF)] * 4,
        coordinates,
        [gate_up_weight],
        [first],
        [pltpu.VMEM((4, 2, qkv_rows, wide), BF)],
    )
    down_left, down_right = whole_call(
        halves_body,
        [shape(block_up, left_cols), shape(block_up, width - left_cols)],
        None,
        [down_weight],
        [cut[0]],
    )
    first, second = stack(
        [(parts(first, "h"), None, None), (parts(second, "h"), None, None)], [down_left]
    )
    gate_up = whole_call(
        pieces_body,
        jax.ShapeDtypeStruct((2, 4 * qkv_rows, wide), BF),
        coordinates,
        [
            cut[0],
            grid.permute(cut[1], {"c": 1}),
            grid.permute(cut[2], {"h": 1}),
            grid.permute(cut[3], {"h": 1, "c": 1}),
        ],
        [first],
    )
    first, second = stack(
        [(parts(first, "x"), None, None), (parts(second, "y"), None, None)], [gate_up]
    )
    gate_up = parts(gate_up, "p")
    first_chunks = [qkv_cols // 3] * 3 + [2 * rank]
    second_chunks = [width - left_cols, left_cols, 2 * rank, rank]
    chunks = stack(
        [
            (parts(first, "y"), None, first_chunks),
            (parts(second, "x"), None, second_chunks),
        ]
    )
    chunks = [flat(parts(chunk, "c")) for chunk in chunks]
    first = [part for chunk in chunks[:4] for part in chunk]
    second = [part for chunk in chunks[4:] for part in chunk]
    gate, up, down_left, down_right = stack(
        [
            (gate_up, 0, None),
            (gate_up, 1, None),
            ([down_left], None, None),
            ([down_right], None, None),
        ],
        [chunks[0][0]],
    )
    gate, up = parts(gate, "x"), parts(up, "y")
    down_left, down_right = parts(down_left, "p"), parts(down_right, "p")
    w_qkv, ql_0, qd, gains = whole_call(
        functools.partial(
            unpack_first_body,
            grid.blocks_of(straight),
            grid.order(straight),
            (qkv_rows, qkv_up, ql_rows, gain_cols),
            2,
        ),
        [shape(width, qkv_cols), shape(rank, qkv_cols), shape(width, 2 * rank), shape(8, width, F32)],
        coordinates,
        first,
        [gate[0]],
    )
    lifts_in = [ql_0, None]

    def project_kv(addends, loop):
        own_kv, normed_b, low_rank_b, residual = whole_call(
            functools.partial(project_kv_body, loop == 0, len(addends)),
            [
                shape(tokens, 2 * HD), shape(tokens, width), shape(tokens, rank),
                shape(tokens, width, F32),
            ],
            None,
            [*addends, gains, qd, w_qkv, lifts_in[loop], *tables],
        )
        both = lax.all_gather(own_kv, "blk", axis=0, tiled=True)
        return own_kv, normed_b, low_rank_b, residual, both

    def project_q(projected, loop, ties=()):
        return whole_call(
            project_q_body,
            shape(tokens, width_q),
            None,
            [projected[1], projected[2], w_qkv, lifts_in[loop], *tables],
            ties,
        )

    def attend(queries, both, ties=()):
        return whole_call(
            attend_body,
            [shape(tokens, width_q), jax.ShapeDtypeStruct((H, tokens, 1), F32)],
            None,
            [queries, both, *masks],
            ties,
        )

    projected_one = project_kv([inputs], 0)
    queries_one = project_q(projected_one, 0)
    gate, up = stack([(gate, None, None), (up, None, None)], [queries_one])
    gate, up = parts(gate, "y"), parts(up, "x")
    w_out, ol_0, ol_1, od, ql_1 = whole_call(
        functools.partial(
            unpack_second_body,
            grid.blocks_of(straight),
            grid.order(turned),
            (out_rows, out_up, ol_rows, ol_up, ql_rows, ql_up),
            2,
        ),
        [
            shape(width_q, width), shape(rank, width), shape(rank, width),
            shape(width_q, 2 * rank), shape(rank, qkv_cols),
        ],
        coordinates,
        second,
        [gate[0]],
    )
    attended_one = attend(queries_one, projected_one[4], [w_out])
    down_left, down_right = stack(
        [(down_left, None, None), (down_right, None, None)], [attended_one[0]]
    )
    down_left, down_right = parts(down_left, "x"), parts(down_right, "y")
    lifts_in[1] = ql_1
    lifts_out = (ol_0, ol_1)

    def leave(loop, mixed_b, residual):
        return whole_call(
            functools.partial(leave_body, loop == 0),
            [shape(tokens, rank), shape(tokens, width, F32), shape(tokens, width)],
            None,
            [mixed_b, od, w_out, lifts_out[loop], residual, gains],
        )

    left_one = leave(0, attended_one[0], projected_one[3])
    ff_in_one = grid.tokens_in(left_one[2])
    down_left, down_right = stack(
        [(down_left, None, None), (down_right, None, None)], [left_one[2]]
    )
    down_left, down_right = parts(down_left, "y"), parts(down_right, "x")
    w_gate = in_order(grid, coordinates, (gate, ("p", "x", "y")))
    w_up = in_order(grid, coordinates, (up, ("p", "y", "x")))
    w_down = in_order(
        grid, coordinates, (down_left, ("p", "x", "y")), (down_right, ("p", "y", "x"))
    )

    qkv_block = qkv_up + 2 * ql_up
    out_block = out_up + 2 * ol_up

    cotangent_in = grid.tokens_in(cotangent)

    def feed_forward(loop, projected, queries, attended, left, ff_in, ties=()):
        own_kv, normed_b, low_rank_b, residual, both = projected
        mixed_b, log_total = attended
        side_b, middle, unused = left
        ff_own, gate_b, up_b, *ff_sent = ff_forward(ff_in, w_gate, w_up, w_down)
        own, other = tokens_out(grid, ff_own, ff_sent, ties)
        spread_own, spread_sent = whole_call(
            functools.partial(
                spread_body,
                (
                    grid.devices, qkv_rows, qkv_block, ql_rows, qkv_up + loop * ql_up,
                    out_rows, out_block, ol_rows, out_up + loop * ol_up,
                ),
            ),
            [shape(tokens, grid.devices // 2 * (qkv_block + out_block))] * 2,
            coordinates,
            [normed_b, low_rank_b, mixed_b, side_b],
            [gate_b],
            [pltpu.VMEM((2, tokens, grid.devices // 2 * (qkv_block + out_block)), BF)],
        )
        cache = (
            residual, (spread_own, grid.permute(spread_sent, {"c": 1})), queries, both, log_total,
            middle, ff_in, gate_b, up_b,
        )
        return [middle, own, other], cache

    addends, cache_one = feed_forward(
        0, projected_one, queries_one, attended_one, left_one, ff_in_one, [cotangent_in[1]]
    )
    projected_two = project_kv(addends, 1)
    queries_two = project_q(projected_two, 1)
    attended_two = attend(queries_two, projected_two[4])
    left_two = leave(1, attended_two[0], projected_two[3])
    addends, cache_two = feed_forward(
        1, projected_two, queries_two, attended_two, left_two, grid.tokens_in(left_two[2])
    )
    result = whole_call(result_body, shape(tokens, width), None, addends)

    group_names = ("y", "x", "p")
    names = ("y", "x", "p", "h")
    half = grid.devices // 2
    joined_columns = slice(0, half * qkv_block)
    mixed_columns = slice(half * qkv_block, half * (qkv_block + out_block))

    def step(stages, ties=()):
        return fold(
            grid, coordinates, [(item[0], stage, [item[1]]) for item, stage in stages], ties
        )

    def with_core(values):
        return values, grid.permute(values, {"c": 1})

    def backward_loop(cache, grad_result, blocks_in, loop, old):
        (
            residual, spreads, queries, both, log_total, middle, ff_in, gate_b, up_b,
        ) = cache
        last = old is not None
        ql, ol = lifts_in[loop], lifts_out[loop]

        def before(name):
            return old[name] if last else None

        def grouped(values):
            return values.reshape(groups, values.shape[0] // groups, values.shape[1])

        own, grad_gate_b, grad_up_b, *down = ff_backward(
            blocks_in, gate_b, up_b, w_gate, w_up, w_down, before("down")
        )
        down, sent = down[:2], down[2:]
        ties = [] if last else [result]
        if last:
            down = fold(
                grid,
                coordinates,
                [
                    (group_names, "x", [[grouped(down[0])]]),
                    (group_names, "y", [[grouped(down[1])]]),
                ],
            )
            ties = [down[0][1][0]]
        own, other = tokens_out(grid, own, sent, ties)
        d_gate, d_up = ff_weights(
            ff_in,
            grad_gate_b,
            grad_up_b,
            (old["gate"], old["up"]) if last else None,
            [own],
        )
        ties = [d_gate]
        if last:
            d_gate, d_up = fold(
                grid,
                coordinates,
                [
                    (group_names, "x", [[grouped(d_gate)]]),
                    (group_names, "y", [[grouped(d_up)]]),
                ],
            )
        grad_middle, grad_branch_b, grad_side_b, grad_mixed_b, gain_grad_ff = whole_call(
            functools.partial(enter_back_body, loop == 0),
            [
                shape(tokens, width, F32), shape(tokens, width), shape(tokens, rank),
                shape(tokens, width_q), shape(8, width, F32),
            ],
            None,
            [own, other, grad_result, middle, gains, w_out, ol, od],
            ties,
        )
        ties = []
        if last:
            down = fold(
                grid,
                coordinates,
                [(down[0][0], "y", [down[0][1]]), (down[1][0], "x", [down[1][1]])],
                [grad_mixed_b, d_gate[1][0]],
            )
            ties = [down[0][1][0]]
        kv_own, kv_sent, grad_queries_b = pl.pallas_call(
            tied(attend_back_body, 10, ties),
            out_shape=[jax.ShapeDtypeStruct((grid.blk // 2, tokens, 2 * HD), BF)] * 2
            + [shape(tokens, width_q)],
            in_specs=[pl.BlockSpec(memory_space=pltpu.VMEM)] * 9
            + [pl.BlockSpec(memory_space=pltpu.SMEM)]
            + [ANY] * len(ties),
            scratch_shapes=[pltpu.VMEM((seq_len, HD), F32)] * 2,
            cost_estimate=LIGHT,
            compiler_params=pltpu.CompilerParams(vmem_limit_bytes=48 * 1024 * 1024),
        )(queries, both, *masks, log_total, grad_mixed_b, *tables, coordinates, *ties)
        grad_kv = (("p", "h"), [kv_own, grid.permute(kv_sent, {"c": 1})])
        (grad_kv,) = step([(grad_kv, "h")])
        (grad_kv,) = step([(grad_kv, "p")])
        branch, side = with_core(grad_branch_b), with_core(grad_side_b)
        d_out, d_od = outer(
            spreads, mixed_columns, [branch, side], [old["out"]] if last else [], [grad_kv[1][0]]
        )
        (d_queries,) = outer(
            spreads,
            joined_columns,
            [with_core(grad_queries_b)],
            [old["queries"]] if last else [],
            [d_out],
        )
        sums = {"out": d_out, "od": d_od, "queries": d_queries}
        ties = [] if last else [d_queries, cache_one[1][1]]
        if last:
            sums["out"], sums["queries"] = fold(
                grid,
                coordinates,
                [
                    (names, "x", [[blocks(value)] for value in (d_out, d_od, old["od"])]),
                    (names, "y", [[blocks(value)] for value in (d_queries, old["qd"])]),
                ],
            )
            sums["gate"], sums["up"], down[0], down[1] = fold(
                grid,
                coordinates,
                [
                    (d_gate[0], "y", [d_gate[1]]),
                    (d_up[0], "x", [d_up[1]]),
                    (down[0][0], "p", [down[0][1]]),
                    (down[1][0], "p", [down[1][1]]),
                ],
                [sums["out"][1][0]],
            )
            ties = [sums["gate"][1][0]]
        else:
            sums["gate"], sums["up"] = d_gate, d_up
        sums["down"] = down
        grad_kv_b, grad_low_rank_b = whole_call(
            functools.partial(rope_back_body, len(grad_kv[1])),
            [shape(tokens, 2 * HD), shape(tokens, rank)],
            None,
            [*grad_kv[1], grad_queries_b, ql, *tables],
            ties,
        )
        sums["kv"], sums["qd"] = outer(
            spreads,
            joined_columns,
            [with_core(grad_kv_b), with_core(grad_low_rank_b)],
            [old["kv"]] if last else [],
        )
        following, following_b, gain_grads = whole_call(
            functools.partial(leave_back_body, loop == 0),
            [shape(tokens, width, F32), shape(tokens, width), shape(8, width, F32)],
            None,
            [
                grad_kv_b, grad_queries_b, grad_low_rank_b, w_qkv, qd, residual, gains,
                grad_middle, gain_grad_ff,
            ]
            + ([old["gains"]] if last else []),
        )
        sums["gains"] = gain_grads
        return following, following_b, sums

    def blocks(values):
        return values.reshape(half, values.shape[0] // half, values.shape[1])

    grad_one, grad_one_b, sums_two = backward_loop(cache_two, cotangent, cotangent_in, 1, None)
    grad_inputs, unused, sums = backward_loop(
        cache_one, grad_one, grid.tokens_in(grad_one_b), 0, sums_two
    )

    late = whole_call(
        functools.partial(late_body, (half, qkv_rows, gain_cols)),
        jax.ShapeDtypeStruct((half, qkv_block, 2 * HD + rank), BF),
        coordinates,
        [blocks(sums["kv"]), blocks(sums["qd"]), *with_core(sums["gains"])],
    )
    (late,) = step([((names, [late]), "x")])
    d_down = whole_call(
        functools.partial(down_body, len(sums["down"][0][1])),
        shape(hidden_block, width, F32),
        None,
        sums["down"][0][1] + sums["down"][1][1],
        [late[1][0]],
    )
    gate, up = step([(sums["gate"], "p"), (sums["up"], "p")], [d_down])
    outs, queries = step([(sums["out"], "y"), (sums["queries"], "x")], [gate[1][0]])
    (late,) = step([(late, "y")], [outs[1][0]])
    split = whole_call(
        functools.partial(split_body, len(gate[1])),
        [jax.ShapeDtypeStruct((2, qkv_rows, wide), BF)] * 4,
        coordinates,
        gate[1] + up[1],
        [late[1][0]],
    )
    back = [
        split[0],
        grid.permute(split[1], {"c": 1}),
        grid.permute(split[2], {"h": 1}),
        grid.permute(split[3], {"h": 1, "c": 1}),
    ]
    outs, queries, late = step([(outs, "h"), (queries, "h"), (late, "h")], [split[0]])
    outs, queries, late = step([(outs, "p"), (queries, "p"), (late, "p")])
    d_gate_up = whole_call(
        functools.partial(join_body, groups, hidden_block, block_up),
        shape(qkv_rows, 8 * groups * hidden_block, F32),
        coordinates,
        back,
        [late[1][0]],
    )
    last = [outs[1], queries[1], late[1]]
    d_gains, d_qkv, d_out, d_qd, d_ql, d_od, d_ol = whole_call(
        functools.partial(
            finish_body,
            len(outs[1]),
            (
                qkv_rows, qkv_up, ql_rows, ql_up, out_rows, out_up, ol_rows, ol_up, gain_cols,
            ),
        ),
        [
            shape(2, gain_cols, F32),
            shape(qkv_rows, qkv_cols, F32),
            shape(out_rows, width, F32),
            jax.ShapeDtypeStruct(adapter_query_down.shape, F32),
            jax.ShapeDtypeStruct(adapter_query_lift.shape, F32),
            jax.ShapeDtypeStruct(adapter_output_down.shape, F32),
            jax.ShapeDtypeStruct(adapter_output_lift.shape, F32),
        ],
        None,
        [value for values in last for value in values],
    )
    return (
        result, grad_inputs, d_gains, d_qkv, d_out, d_gate_up, d_down, d_qd, d_ql, d_od, d_ol,
    )


def solution(mesh):
    grid = Grid(mesh)
    rows = P(AXES, None)
    deep = P(None, AXES, None)
    in_specs = (
        rows, P("fsdp", None), rows, P(None, AXES), rows, rows, rows, rows, deep, deep, deep, deep,
    )
    out_specs = (
        rows, rows, P(None, AXES), rows, rows, rows, rows, deep, deep, deep, deep,
    )

    def run(*arguments):
        return per_device(grid, *arguments)

    return jax.shard_map(
        run, mesh=mesh, in_specs=in_specs, out_specs=out_specs, check_vma=False
    )
```

time: 1060 us -> 831 us (0.78)
  Pallas kernels: 0 us -> 295 us
  matrix products: 252 us -> 0 us
  other arithmetic: 128 us -> 2.52 us
  local copies, waits for them, and re-layouts: 158 us -> 68.4 us
  waiting for transfers between devices: 419 us -> 362 us
    pallas_call x0 -> x72, Pallas kernels: none -> 295 us  [the longest x64 140 us: whole_call(): pl.pallas_call(tied(body, len(specs), ties), out_shape=out_shape, in_spec...]
    dot_general x66 -> x0, matrix products: 252 us -> none  [the longest x22 101 us: matmul_nt(): lax.dot_general(left_side, right_side, (((1,), (1,)), ((), ())), preferre...]
    another operation x65 -> x0, other arithmetic: 52.4 us -> none  [the longest x53 41.1 us: gather(): jnp.stack([jnp.where(first, values, other), jnp.where(first, other, value...]
    unnamed x484 -> x308, local copies, waits for them, and re-layouts: 34.1 us -> 68.2 us
    convert_element_type x32 -> x0, local copies, waits for them, and re-layouts: 32.1 us -> none  [the longest x27 17.9 us: scatter(): total = total + self.permute(sent.astype(BF), {name: shift}).astype(F32)]
    reduce_scatter x2 -> x0, waiting for transfers between devices: 30.7 us -> none  [backward_loop(): lax.psum_scatter(jnp.concatenate([rounded(grad_k_all), rounded(grad_v_all...]
    reshape x13 -> x0, local copies, waits for them, and re-layouts: 27.6 us -> none  [the longest x3 11.7 us: blocks(): values.reshape(grid.devices, values.shape[0] // grid.devices, values.shap...]
    add x32 -> x1, other arithmetic: 27 us -> 0.01 us  [per_device(): places = position * tokens + jnp.arange(tokens, dtype=jnp.int32)]
  transfers between devices with their start and end apart: 80 -> 110, of which waited for: 39 -> 52; matrix products, arithmetic and copies ran while one was open for 31% -> 0% of each run, Pallas kernels for 0% -> 24%
where the time goes in v2:
time: 831 us; the launch traced here: 824 us
  waiting for transfers between devices  362 us (44%)
  Pallas kernels  295 us (35%)
  starting transfers between devices  80.3 us (10%)
  local copies, waits for them, and re-layouts  68.4 us (8%)
  between operations  15.6 us (2%)
    ppermute x108, waiting for transfers between devices, permute(): return lax.ppermute(values, AXES, pairs)  337 us
    pallas_call x64, Pallas kernels, whole_call(): pl.pallas_call(tied(body, len(specs), ties), out_shape=out_shape, in_spec...  140 us
    ppermute x108, starting transfers between devices, permute(): return lax.ppermute(values, AXES, pairs)  79.8 us
    unnamed x308, local copies, waits for them, and re-layouts  68.2 us
    pallas_call x2, Pallas kernels, ff_backward(): kernel_call(functools.partial(ff_backward_body, old is not None), (wide /...  61.3 us
    pallas_call x2, Pallas kernels, ff_forward(): kernel_call(ff_forward_body, (wide // TILE,), [full((size, width))] * 4 +...  45.1 us
    pallas_call x2, Pallas kernels, ff_weights(): kernel_call(functools.partial(ff_weights_body, old is not None), (wide //...  29.5 us
    all_gather x2, waiting for transfers between devices, project_kv(): both = lax.all_gather(own_kv, 'blk', axis=0, tiled=True)  24.7 us
  transfers between devices with their start and end apart: 110, of which 52 were waited for; matrix products, arithmetic and copies ran while one was open for 0% of the time, Pallas kernels for 24%

profile of v2, /device:TPU:0, one launch (start us, length us, event | category | flops | bytes accessed | tf_op | source)
XLA Modules:
  0.0 823.5 jit_solution(12894151692735299600)
XLA Ops:
  12.9 4.1 collective-permute-start
  17.1 16.9 %collective-permute-done.1.refs_3_ = bf16[48,1920]{1,0:T(8,128)(2,1)S(1)} collective-permute-done((bf16[48,1920]{1,0:T(8,128)(2,1)S(1)}, bf16[48,1920]{1,0:T(8,128)(2,1)S(1)}, u32[]{:S(2)}, u32[]{:S(2)}) %collective-permute-start.1) | collective-permute-done | bytes 184352 | tf_op jit(solution)/shard_map/ppermute | solution.py:75
  37.6 14.8 %collective-permute-done.3.refs_3_ = bf16[2,48,1920]{2,1,0:T(8,128)(2,1)S(1)} collective-permute-done((bf16[2,48,1920]{2,1,0:T(8,128)(2,1)S(1)}, bf16[2,48,1920]{2,1,0:T(8,128)(2,1)S(1)}, u32[]{:S(2)}, u32[]{:S(2)}) %collective-permute-start.3) | collective-permute-done | bytes 368672 | tf_op jit(solution)/shard_map/ppermute | solution.py:75
  57.2 7.8 collective-permute-done.7.refs_3_
  65.0 5.4 collective-permute-done.8.refs_4_
  74.5 4.4 collective-permute-start.15
  79.0 28.6 %collective-permute-done.10.refs_3_ = bf16[2,2,2,48,1920]{4,3,2,1,0:T(8,128)(2,1)} collective-permute-done((bf16[2,2,2,48,1920]{4,3,2,1,0:T(8,128)(2,1)S(1)}, bf16[2,2,2,48,1920]{4,3,2,1,0:T(8,128)(2,1)}, u32[]{:S(2)}, u32[]{:S(2)}) %collective-permute-start.10) | collective-permute-done | bytes 1474592 | tf_op jit(solution)/shard_map/ppermute | solution.py:75
  117.8 4.3 collective-permute-done.15.refs_1_.refs_3_
  125.2 4.4 shard_map.212
  141.6 20.4 %collective-permute-done.21.refs_3_ = bf16[2,144,1792]{2,1,0:T(8,128)(2,1)S(1)} collective-permute-done((bf16[2,144,1792]{2,1,0:T(8,128)(2,1)}, bf16[2,144,1792]{2,1,0:T(8,128)(2,1)S(1)}, u32[]{:S(2)}, u32[]{:S(2)}) %collective-permute-start.21) | collective-permute-done | bytes 1032224 | tf_op jit(solution)/shard_map/ppermute | solution.py:75
  186.2 3.9 shard_map.216
  193.7 4.1 shard_map.217
  207.5 22.6 %collective-permute-done.30.refs_3_ = bf16[2,224,512]{2,1,0:T(8,128)(2,1)S(1)} collective-permute-done((bf16[2,224,512]{2,1,0:T(8,128)(2,1)S(1)}, bf16[2,224,512]{2,1,0:T(8,128)(2,1)S(1)}, u32[]{:S(2)}, u32[]{:S(2)}) %collective-permute-start.30) | collective-permute-done | bytes 458784 | tf_op jit(solution)/shard_map/ppermute | solution.py:75
  240.1 4.0 shard_map.219.wg_ref.refs_6_
  244.1 11.1 %collective-permute-done.32 = bf16[2,2,224,512]{3,2,1,0:T(8,128)(2,1)} collective-permute-done((bf16[2,2,224,512]{3,2,1,0:T(8,128)(2,1)}, bf16[2,2,224,512]{3,2,1,0:T(8,128)(2,1)}, u32[]{:S(2)}, u32[]{:S(2)}) %collective-permute-start.32) | collective-permute-done | bytes 917536 | tf_op jit(solution)/shard_map/ppermute | solution.py:75
  258.6 3.9 shard_map.223.wd_ref.refs_8_
  262.5 22.8 %shard_map.224 = (f32[512,1152]{1,0:T(8,128)S(1)}, bf16[1024,1792]{1,0:T(8,128)(2,1)}, bf16[1024,1792]{1,0:T(8,128)(2,1)}, bf16[128,1152]{1,0:T(8,128)(2,1)S(1)}...) custom-call(bf16[256,1152]{1,0:T(8,128)(2,1)S(1)} %get-tuple-element.256.refs_4_.x0_ref, ...), custom_call_target="tpu_custom_call" | custom-call | tf_op jit(solution)/shard_map/pallas_call | solution.py:232
  290.3 13.6 %collective-permute-done.38.refs_2_ = bf16[256,1152]{1,0:T(8,128)(2,1)S(1)} collective-permute-done((bf16[256,1152]{1,0:T(8,128)(2,1)S(1)}, bf16[256,1152]{1,0:T(8,128)(2,1)S(1)}, u32[]{:S(2)}, u32[]{:S(2)}) %collective-permute-start.38) | collective-permute-done | bytes 589856 | tf_op jit(solution)/shard_map/ppermute | solution.py:75
  317.4 24.7 %all-gather.5.cloned.1.call-done.kv_ref = bf16[2048,512]{1,0:T(8,128)(2,1)} async-done(((bf16[256,512]{1,0:T(8,128)(2,1)}), bf16[2048,512]{1,0:T(8,128)(2,1)}) %all-gather.5.cloned.1.call-update) | async-done | bytes 2097168 | tf_op jit(solution)/shard_map/all_gather | solution.py:1164
  346.6 4.1 shard_map.228
  355.3 14.0 %collective-permute-done.39.x1_ref.refs_1_ = bf16[256,1152]{1,0:T(8,128)(2,1)S(1)} collective-permute-done((bf16[256,1152]{1,0:T(8,128)(2,1)S(1)}, bf16[256,1152]{1,0:T(8,128)(2,1)S(1)}, u32[]{:S(2)}, u32[]{:S(2)}) %collective-permute-start.39) | collective-permute-done | bytes 589856 | tf_op jit(solution)/shard_map/ppermute | solution.py:75
  371.3 22.3 %shard_map.230 = (f32[512,1152]{1,0:T(8,128)S(1)}, bf16[1024,1792]{1,0:T(8,128)(2,1)}, bf16[1024,1792]{1,0:T(8,128)(2,1)}, bf16[128,1152]{1,0:T(8,128)(2,1)S(1)}...) custom-call(bf16[256,1152]{1,0:T(8,128)(2,1)S(1)} %get-tuple-element.279.x0_ref.refs_0_, ...), custom_call_target="tpu_custom_call" | custom-call | tf_op jit(solution)/shard_map/pallas_call | solution.py:232
  401.6 30.7 %shard_map.233 = (f32[512,1152]{1,0:T(8,128)}, bf16[1024,1792]{1,0:T(8,128)(2,1)}, bf16[1024,1792]{1,0:T(8,128)(2,1)}, bf16[1792,640]{1,0:T(8,128)(2,1)}, bf16[1...) custom-call(bf16[256,1152]{1,0:T(8,128)(2,1)S(1)} %copy-done.74, ...), custom_call_target="tpu_custom_call" | custom-call | tf_op jit(solution)/shard_map/pallas_call | solution.py:319
  438.4 14.0 %shard_map.235 = (bf16[1152,1792]{1,0:T(8,128)(2,1)}, bf16[1152,1792]{1,0:T(8,128)(2,1)}) custom-call(bf16[256,1152]{1,0:T(8,128)(2,1)S(1)} %get-tuple-element.279.x0_ref.refs_0_, bf16[256,1152]{1,0:T(8,128)(2,1)S(1)} %collective-permute-done.39.x1_ref.refs_1_, bf16[256,1152]{1,0:T(8,128)(2,1)S(1)} %collective-permute-done.40.x2_ref.refs_2_, ...), custom_call_target="tpu_custom_call" | custom-call | tf_op jit(solution)/shard_map/pallas_call | solution.py:370
  453.2 4.2 shard_map.236
  458.5 9.8 %shard_map.237 = (bf16[4,256,512]{2,1,0:T(8,128)(2,1)S(1)}, bf16[4,256,512]{2,1,0:T(8,128)(2,1)S(1)}, bf16[256,1024]{1,0:T(8,128)(2,1)S(1)}) custom-call(bf16[256,1024]{1,0:T(8,128)(2,1)S(1)} %copy-done.40, bf16[2048,512]{1,0:T(8,128)(2,1)} %all-gather.5.cloned.1.call-done.kv_ref, s32[256,1]{1,0:T(8,128)S(1)} %copy-done.54, s32[256,1]{1,0:T(8,128)S(1)} %copy-done.57, ...), custom_call_target="tpu_custom_call" | custom-call | tf_op jit(solution)/shard_map/pallas_call | solution.py:1355
  468.4 5.8 shard_map.240
  474.7 4.7 shard_map.243
  481.6 13.1 %collective-permute-done.55.refs_1_ = bf16[2,256,512]{2,1,0:T(8,128)(2,1)S(1)} collective-permute-done((bf16[2,256,512]{2,1,0:T(8,128)(2,1)S(1)}, bf16[2,256,512]{2,1,0:T(8,128)(2,1)S(1)}, u32[]{:S(2)}, u32[]{:S(2)}) %collective-permute-start.55) | collective-permute-done | bytes 524320 | tf_op jit(solution)/shard_map/ppermute | solution.py:75
  502.7 7.2 collective-permute-done.56.refs_1_
  511.8 4.1 shard_map.245
  516.9 15.1 %collective-permute-done.62.refs_1_ = bf16[256,1152]{1,0:T(8,128)(2,1)S(1)} collective-permute-done((bf16[256,1152]{1,0:T(8,128)(2,1)S(1)}, bf16[256,1152]{1,0:T(8,128)(2,1)S(1)}, u32[]{:S(2)}, u32[]{:S(2)}) %collective-permute-start.62) | collective-permute-done | bytes 589856 | tf_op jit(solution)/shard_map/ppermute | solution.py:75
  534.0 30.6 %shard_map.246 = (f32[512,1152]{1,0:T(8,128)}, bf16[1024,1792]{1,0:T(8,128)(2,1)}, bf16[1024,1792]{1,0:T(8,128)(2,1)}, bf16[1792,640]{1,0:T(8,128)(2,1)}, bf16[1...) custom-call(bf16[256,1152]{1,0:T(8,128)(2,1)S(1)} %get-tuple-element, ...), custom_call_target="tpu_custom_call" | custom-call | tf_op jit(solution)/shard_map/pallas_call | solution.py:319
  577.5 15.5 %shard_map.249 = (bf16[1152,1792]{1,0:T(8,128)(2,1)}, bf16[1152,1792]{1,0:T(8,128)(2,1)}) custom-call(bf16[256,1152]{1,0:T(8,128)(2,1)S(1)} %copy-done.34, bf16[256,1152]{1,0:T(8,128)(2,1)S(1)} %copy-done.64, bf16[256,1152]{1,0:T(8,128)(2,1)S(1)} %copy-done.66, bf16[256,1152]{1,0:T(8,128)(2,1)S(1)} %copy-done.68, ...), custom_call_target="tpu_custom_call" | custom-call | tf_op jit(solution)/shard_map/pallas_call | solution.py:370
  593.0 6.0 shard_map.251
  602.9 4.3 shard_map.250
  611.9 9.8 %shard_map.253 = (bf16[4,256,512]{2,1,0:T(8,128)(2,1)S(1)}, bf16[4,256,512]{2,1,0:T(8,128)(2,1)S(1)}, bf16[256,1024]{1,0:T(8,128)(2,1)S(1)}) custom-call(bf16[256,1024]{1,0:T(8,128)(2,1)S(1)} %copy-done.20, bf16[2048,512]{1,0:T(8,128)(2,1)} %all-gather.3.cloned.1.call-done.refs_1_, s32[256,1]{1,0:T(8,128)S(1)} %copy-done.54, s32[256,1]{1,0:T(8,128)S(1)} %copy-done.57, ...), custom_call_target="tpu_custom_call" | custom-call | tf_op jit(solution)/shard_map/pallas_call | solution.py:1355
  631.7 7.6 collective-permute-done.73.refs_1_
  648.6 4.5 shard_map.257
  662.2 5.5 shard_map.260
  672.0 5.1 shard_map.262
  686.9 12.9 %collective-permute-done.88.refs_1_ = bf16[224,640]{1,0:T(8,128)(2,1)S(1)} collective-permute-done((bf16[224,640]{1,0:T(8,128)(2,1)S(1)}, bf16[224,640]{1,0:T(8,128)(2,1)S(1)}, u32[]{:S(2)}, u32[]{:S(2)}) %collective-permute-start.88) | collective-permute-done | bytes 286752 | tf_op jit(solution)/shard_map/ppermute | solution.py:75
  701.3 17.5 %collective-permute-done.86.refs_2_ = bf16[2,144,1792]{2,1,0:T(8,128)(2,1)S(1)} collective-permute-done((bf16[2,144,1792]{2,1,0:T(8,128)(2,1)}, bf16[2,144,1792]{2,1,0:T(8,128)(2,1)S(1)}, u32[]{:S(2)}, u32[]{:S(2)}) %collective-permute-start.86) | collective-permute-done | bytes 1032224 | tf_op jit(solution)/shard_map/ppermute | solution.py:75
  732.2 28.3 %collective-permute-done.97.refs_2_ = bf16[144,1792]{1,0:T(8,128)(2,1)S(1)} collective-permute-done((bf16[144,1792]{1,0:T(8,128)(2,1)S(1)}, bf16[144,1792]{1,0:T(8,128)(2,1)S(1)}, u32[]{:S(2)}, u32[]{:S(2)}) %collective-permute-start.97) | collective-permute-done | bytes 516128 | tf_op jit(solution)/shard_map/ppermute | solution.py:75
  760.5 11.0 %collective-permute-done.98.refs_4_ = bf16[144,1792]{1,0:T(8,128)(2,1)S(1)} collective-permute-done((bf16[144,1792]{1,0:T(8,128)(2,1)S(1)}, bf16[144,1792]{1,0:T(8,128)(2,1)S(1)}, u32[]{:S(2)}, u32[]{:S(2)}) %collective-permute-start.98) | collective-permute-done | bytes 516128 | tf_op jit(solution)/shard_map/ppermute | solution.py:75
  777.7 16.2 %collective-permute-done.101.refs_5_ = bf16[2,56,768]{2,1,0:T(8,128)(2,1)S(1)} collective-permute-done((bf16[2,56,768]{2,1,0:T(8,128)(2,1)S(1)}, bf16[2,56,768]{2,1,0:T(8,128)(2,1)S(1)}, u32[]{:S(2)}, u32[]{:S(2)}) %collective-permute-start.101) | collective-permute-done | bytes 172064 | tf_op jit(solution)/shard_map/ppermute | solution.py:75
  798.0 9.2 %collective-permute-done.106.refs_3_ = bf16[2,36,1792]{2,1,0:T(8,128)(2,1)S(1)} collective-permute-done((bf16[2,36,1792]{2,1,0:T(8,128)(2,1)S(1)}, bf16[2,36,1792]{2,1,0:T(8,128)(2,1)S(1)}, u32[]{:S(2)}, u32[]{:S(2)}) %collective-permute-start.106) | collective-permute-done | bytes 258080 | tf_op jit(solution)/shard_map/ppermute | solution.py:75
  807.2 4.3 collective-permute-done.107.refs_4_
  (562 shorter events, 249.0 us)
Async XLA Ops:
  7.2 184.7 %all-gather.3.cloned.1.call-start = ((), (), s32[]{:S(2)}) async-start(), calls=%async_computation | async-start | bytes 2359296 | tf_op jit(solution)/shard_map/all_gather | solution.py:1164
  12.9 21.1 %collective-permute-start = (bf16[48,2048]{1,0:T(8,128)(2,1)S(1)}, bf16[48,2048]{1,0:T(8,128)(2,1)S(1)}, u32[]{:S(2)}, u32[]{:S(2)}) collective-permute-start(bf16[48,2048]{1,0:T(8,128)(2,1)S(1)} %get-tuple-element.218.refs_0_), channel_id=1, source_target_pairs={{0,4},{1,5},{2,6},{3,7},{4,0},{5,1},{6,2},{7,3},{8,12},{9,13},{10,... | collective-permute-start | bytes 589832 | tf_op jit(solution)/shard_map/ppermute | solution.py:75
  72.5 36.8 %collective-permute-start.9 = (bf16[2,2,2,48,2048]{4,3,2,1,0:T(8,128)(2,1)}, bf16[2,2,2,48,2048]{4,3,2,1,0:T(8,128)(2,1)}, u32[]{:S(2)}, u32[]{:S(2)}) collective-permute-start(bf16[2,2,2,48,2048]{4,3,2,1,0:T(8,128)(2,1)} %get-tuple-element.229.refs_0_), channel_id=1, source_target_pairs={{0,16},{1,17},{2,18},{3,19},{4,20},{5,21},{6,22},{7,23},{8,24},{9,... | collective-permute-start | bytes 4718600 | tf_op jit(solution)/shard_map/ppermute | solution.py:75
  73.2 34.4 %collective-permute-start.10 = (bf16[2,2,2,48,1920]{4,3,2,1,0:T(8,128)(2,1)S(1)}, bf16[2,2,2,48,1920]{4,3,2,1,0:T(8,128)(2,1)}, u32[]{:S(2)}, u32[]{:S(2)}) collective-permute-start(bf16[2,2,2,48,1920]{4,3,2,1,0:T(8,128)(2,1)S(1)} %get-tuple-element.230.refs_2_), channel_id=1, source_target_pairs={{0,8},{1,9},{2,10},{3,11},{4,12},{5,13},{6,14},{7,15},{8,0},{9,1},... | collective-permute-start | bytes 4423688 | tf_op jit(solution)/shard_map/ppermute | solution.py:75
  74.5 47.5 %collective-permute-start.15 = (bf16[2,144,1792]{2,1,0:T(8,128)(2,1)S(1)}, bf16[2,144,1792]{2,1,0:T(8,128)(2,1)S(1)}, u32[]{:S(2)}, u32[]{:S(2)}) collective-permute-start(bf16[2,144,1792]{2,1,0:T(8,128)(2,1)S(1)} %shard_map.208.refs_4_.refs_0_.refs_2_), channel_id=1, source_target_pairs={{0,4},{1,5},{2,6},{3,7},{4,0},{5,1},{6,2},{7,3},{8,12},{9,13},{10,... | collective-permute-start | bytes 3096584 | tf_op jit(solution)/shard_map/ppermute | solution.py:75
  137.6 204.5 %all-gather.5.cloned.1.call-start = ((), (), s32[]{:S(2)}) async-start(), calls=%async_computation.1 | async-start | bytes 2359296 | tf_op jit(solution)/shard_map/all_gather | solution.py:1164
  138.1 23.9 %collective-permute-start.21 = (bf16[2,144,1792]{2,1,0:T(8,128)(2,1)}, bf16[2,144,1792]{2,1,0:T(8,128)(2,1)S(1)}, u32[]{:S(2)}, u32[]{:S(2)}) collective-permute-start(bf16[2,144,1792]{2,1,0:T(8,128)(2,1)} %copy-done.94), channel_id=1, source_target_pairs={{0,16},{1,17},{2,18},{3,19},{4,20},{5,21},{6,22},{7,23},{8,24},{9,... | collective-permute-start | bytes 3096584 | tf_op jit(solution)/shard_map/ppermute | solution.py:75
  139.6 28.3 %collective-permute-start.20 = (bf16[2,144,1792]{2,1,0:T(8,128)(2,1)}, bf16[2,144,1792]{2,1,0:T(8,128)(2,1)S(1)}, u32[]{:S(2)}, u32[]{:S(2)}) collective-permute-start(bf16[2,144,1792]{2,1,0:T(8,128)(2,1)} %copy-done.49), channel_id=1, source_target_pairs={{0,8},{1,9},{2,10},{3,11},{4,12},{5,13},{6,14},{7,15},{8,0},{9,1},... | collective-permute-start | bytes 3096584 | tf_op jit(solution)/shard_map/ppermute | solution.py:75
  141.1 33.6 %collective-permute-start.16 = (bf16[2,2,2,2,48,512]{5,4,3,2,1,0:T(8,128)(2,1)}, bf16[2,2,2,2,48,512]{5,4,3,2,1,0:T(8,128)(2,1)S(1)}, u32[]{:S(2)}, u32[]{:S(2)}) collective-permute-start(bf16[2,2,2,2,48,512]{5,4,3,2,1,0:T(8,128)(2,1)} %copy-done.102), channel_id=1, source_target_pairs={{0,1},{1,0},{2,3},{3,2},{4,5},{5,4},{6,7},{7,6},{8,9},{9,8},{10,11... | collective-permute-start | bytes 2359304 | tf_op jit(solution)/shard_map/ppermute | solution.py:75
  141.1 31.1 %collective-permute-start.19 = (bf16[2,2,2,2,48,256]{5,4,3,2,1,0:T(8,128)(2,1)}, bf16[2,2,2,2,48,256]{5,4,3,2,1,0:T(8,128)(2,1)S(1)}, u32[]{:S(2)}, u32[]{:S(2)}) collective-permute-start(bf16[2,2,2,2,48,256]{5,4,3,2,1,0:T(8,128)(2,1)} %copy-done.126), channel_id=1, source_target_pairs={{0,1},{1,0},{2,3},{3,2},{4,5},{5,4},{6,7},{7,6},{8,9},{9,8},{10,11... | collective-permute-start | bytes 1179656 | tf_op jit(solution)/shard_map/ppermute | solution.py:75
  141.6 34.0 %collective-permute-start.18 = (bf16[2,2,2,2,48,512]{5,4,3,2,1,0:T(8,128)(2,1)}, bf16[2,2,2,2,48,512]{5,4,3,2,1,0:T(8,128)(2,1)S(1)}, u32[]{:S(2)}, u32[]{:S(2)}) collective-permute-start(bf16[2,2,2,2,48,512]{5,4,3,2,1,0:T(8,128)(2,1)} %copy-done.104), channel_id=1, source_target_pairs={{0,1},{1,0},{2,3},{3,2},{4,5},{5,4},{6,7},{7,6},{8,9},{9,8},{10,11... | collective-permute-start | bytes 2359304 | tf_op jit(solution)/shard_map/ppermute | solution.py:75
  170.7 64.1 %collective-permute-start.26 = (bf16[2,2,144,1792]{3,2,1,0:T(8,128)(2,1)}, bf16[2,2,144,1792]{3,2,1,0:T(8,128)(2,1)S(1)}, u32[]{:S(2)}, u32[]{:S(2)}) collective-permute-start(bf16[2,2,144,1792]{3,2,1,0:T(8,128)(2,1)} %get-tuple-element.257), channel_id=1, source_target_pairs={{0,8},{1,9},{2,10},{3,11},{4,12},{5,13},{6,14},{7,15},{8,0},{9,1},... | collective-permute-start | bytes 6193160 | tf_op jit(solution)/shard_map/ppermute | solution.py:75
  172.9 62.4 %collective-permute-start.25 = (bf16[2,2,144,1792]{3,2,1,0:T(8,128)(2,1)}, bf16[2,2,144,1792]{3,2,1,0:T(8,128)(2,1)}, u32[]{:S(2)}, u32[]{:S(2)}) collective-permute-start(bf16[2,2,144,1792]{3,2,1,0:T(8,128)(2,1)} %get-tuple-element.249.refs_9_), channel_id=1, source_target_pairs={{0,16},{1,17},{2,18},{3,19},{4,20},{5,21},{6,22},{7,23},{8,24},{9,... | collective-permute-start | bytes 6193160 | tf_op jit(solution)/shard_map/ppermute | solution.py:75
  175.6 25.9 %collective-permute-start.27 = (bf16[224,640]{1,0:T(8,128)(2,1)}, bf16[224,640]{1,0:T(8,128)(2,1)}, u32[]{:S(2)}, u32[]{:S(2)}) collective-permute-start(bf16[224,640]{1,0:T(8,128)(2,1)} %get-tuple-element.258.refs_0_), channel_id=1, source_target_pairs={{0,4},{1,5},{2,6},{3,7},{4,0},{5,1},{6,2},{7,3},{8,12},{9,13},{10,... | collective-permute-start | bytes 860168 | tf_op jit(solution)/shard_map/ppermute | solution.py:75
  176.5 24.9 %collective-permute-start.28 = (bf16[224,512]{1,0:T(8,128)(2,1)}, bf16[224,512]{1,0:T(8,128)(2,1)}, u32[]{:S(2)}, u32[]{:S(2)}) collective-permute-start(bf16[224,512]{1,0:T(8,128)(2,1)} %get-tuple-element.259.refs_2_), channel_id=1, source_target_pairs={{0,4},{1,5},{2,6},{3,7},{4,0},{5,1},{6,2},{7,3},{8,12},{9,13},{10,... | collective-permute-start | bytes 688136 | tf_op jit(solution)/shard_map/ppermute | solution.py:75
  202.7 27.9 %collective-permute-start.29 = (bf16[2,224,640]{2,1,0:T(8,128)(2,1)S(1)}, bf16[2,224,640]{2,1,0:T(8,128)(2,1)S(1)}, u32[]{:S(2)}, u32[]{:S(2)}) collective-permute-start(bf16[2,224,640]{2,1,0:T(8,128)(2,1)S(1)} %get-tuple-element.260.refs_0_), channel_id=1, source_target_pairs={{0,8},{1,9},{2,10},{3,11},{4,12},{5,13},{6,14},{7,15},{8,0},{9,1},... | collective-permute-start | bytes 1720328 | tf_op jit(solution)/shard_map/ppermute | solution.py:75
  203.1 27.0 %collective-permute-start.30 = (bf16[2,224,512]{2,1,0:T(8,128)(2,1)S(1)}, bf16[2,224,512]{2,1,0:T(8,128)(2,1)S(1)}, u32[]{:S(2)}, u32[]{:S(2)}) collective-permute-start(bf16[2,224,512]{2,1,0:T(8,128)(2,1)S(1)} %get-tuple-element.261.refs_2_), channel_id=1, source_target_pairs={{0,16},{1,17},{2,18},{3,19},{4,20},{5,21},{6,22},{7,23},{8,24},{9,... | collective-permute-start | bytes 1376264 | tf_op jit(solution)/shard_map/ppermute | solution.py:75
  207.4 27.4 %collective-permute-start.22 = (bf16[256,1152]{1,0:T(8,128)(2,1)S(1)}, bf16[256,1152]{1,0:T(8,128)(2,1)S(1)}, u32[]{:S(2)}, u32[]{:S(2)}) collective-permute-start(bf16[256,1152]{1,0:T(8,128)(2,1)S(1)} %get-tuple-element.256.refs_4_.x0_ref.refs_0_), channel_id=1, source_target_pairs={{0,2},{1,3},{2,0},{3,1},{4,6},{5,7},{6,4},{7,5},{8,10},{9,11},{10,... | collective-permute-start | bytes 1769480 | tf_op jit(solution)/shard_map/ppermute | solution.py:75
  231.7 26.9 %collective-permute-start.31 = (bf16[2,2,224,640]{3,2,1,0:T(8,128)(2,1)S(1)}, bf16[2,2,224,640]{3,2,1,0:T(8,128)(2,1)S(1)}, u32[]{:S(2)}, u32[]{:S(2)}) collective-permute-start(bf16[2,2,224,640]{3,2,1,0:T(8,128)(2,1)S(1)} %get-tuple-element.262), channel_id=1, source_target_pairs={{0,16},{1,17},{2,18},{3,19},{4,20},{5,21},{6,22},{7,23},{8,24},{9,... | collective-permute-start | bytes 3440648 | tf_op jit(solution)/shard_map/ppermute | solution.py:75
  233.1 22.1 %collective-permute-start.32 = (bf16[2,2,224,512]{3,2,1,0:T(8,128)(2,1)}, bf16[2,2,224,512]{3,2,1,0:T(8,128)(2,1)}, u32[]{:S(2)}, u32[]{:S(2)}) collective-permute-start(bf16[2,2,224,512]{3,2,1,0:T(8,128)(2,1)} %get-tuple-element.263), channel_id=1, source_target_pairs={{0,8},{1,9},{2,10},{3,11},{4,12},{5,13},{6,14},{7,15},{8,0},{9,1},... | collective-permute-start | bytes 2752520 | tf_op jit(solution)/shard_map/ppermute | solution.py:75
  234.8 27.6 %collective-permute-start.23 = (bf16[256,1152]{1,0:T(8,128)(2,1)S(1)}, bf16[256,1152]{1,0:T(8,128)(2,1)S(1)}, u32[]{:S(2)}, u32[]{:S(2)}) collective-permute-start(bf16[256,1152]{1,0:T(8,128)(2,1)S(1)} %get-tuple-element.256.refs_4_.x0_ref.refs_0_), channel_id=1, source_target_pairs={{0,1},{1,0},{2,3},{3,2},{4,5},{5,4},{6,7},{7,6},{8,9},{9,8},{10,11... | collective-permute-start | bytes 1769480 | tf_op jit(solution)/shard_map/ppermute | solution.py:75
  234.9 27.6 %collective-permute-start.24 = (bf16[256,1152]{1,0:T(8,128)(2,1)S(1)}, bf16[256,1152]{1,0:T(8,128)(2,1)S(1)}, u32[]{:S(2)}, u32[]{:S(2)}) collective-permute-start(bf16[256,1152]{1,0:T(8,128)(2,1)S(1)} %collective-permute-done.22.x1_ref.refs_1_), channel_id=1, source_target_pairs={{0,1},{1,0},{2,3},{3,2},{4,5},{5,4},{6,7},{7,6},{8,9},{9,8},{10,11... | collective-permute-start | bytes 1769480 | tf_op jit(solution)/shard_map/ppermute | solution.py:75
  235.4 51.0 %collective-permute-start.37 = (bf16[256,1152]{1,0:T(8,128)(2,1)S(1)}, bf16[256,1152]{1,0:T(8,128)(2,1)S(1)}, u32[]{:S(2)}, u32[]{:S(2)}) collective-permute-start(bf16[256,1152]{1,0:T(8,128)(2,1)S(1)} %copy-done.73), channel_id=1, source_target_pairs={{0,2},{1,3},{2,0},{3,1},{4,6},{5,7},{6,4},{7,5},{8,10},{9,11},{10,... | collective-permute-start | bytes 1769480 | tf_op jit(solution)/shard_map/ppermute | solution.py:75
  400.1 34.5 %collective-permute-start.46 = (bf16[256,1152]{1,0:T(8,128)(2,1)}, bf16[256,1152]{1,0:T(8,128)(2,1)S(1)}, u32[]{:S(2)}, u32[]{:S(2)}) collective-permute-start(bf16[256,1152]{1,0:T(8,128)(2,1)} %get-tuple-element.286), channel_id=1, source_target_pairs={{0,2},{1,3},{2,0},{3,1},{4,6},{5,7},{6,4},{7,5},{8,10},{9,11},{10,... | collective-permute-start | bytes 1769480 | tf_op jit(solution)/shard_map/ppermute | solution.py:75
  474.2 22.3 %collective-permute-start.57 = (bf16[256,1664]{1,0:T(8,128)(2,1)}, bf16[256,1664]{1,0:T(8,128)(2,1)S(1)}, u32[]{:S(2)}, u32[]{:S(2)}) collective-permute-start(bf16[256,1664]{1,0:T(8,128)(2,1)} %get-tuple-element.311), channel_id=1, source_target_pairs={{0,1},{1,0},{2,3},{3,2},{4,5},{5,4},{6,7},{7,6},{8,9},{9,8},{10,11... | collective-permute-start | bytes 2555912 | tf_op jit(solution)/shard_map/ppermute | solution.py:75
  479.4 23.3 %collective-permute-start.61 = (bf16[256,1664]{1,0:T(8,128)(2,1)S(1)}, bf16[256,1664]{1,0:T(8,128)(2,1)S(1)}, u32[]{:S(2)}, u32[]{:S(2)}) collective-permute-start(bf16[256,1664]{1,0:T(8,128)(2,1)S(1)} %get-tuple-element.317), channel_id=1, source_target_pairs={{0,1},{1,0},{2,3},{3,2},{4,5},{5,4},{6,7},{7,6},{8,9},{9,8},{10,11... | collective-permute-start | bytes 2555912 | tf_op jit(solution)/shard_map/ppermute | solution.py:75
  569.0 39.0 %collective-permute-start.70 = (bf16[2,2,224,640]{3,2,1,0:T(8,128)(2,1)}, bf16[2,2,224,640]{3,2,1,0:T(8,128)(2,1)}, u32[]{:S(2)}, u32[]{:S(2)}) collective-permute-start(bf16[2,2,224,640]{3,2,1,0:T(8,128)(2,1)} %get-tuple-element.342), channel_id=1, source_target_pairs={{0,8},{1,9},{2,10},{3,11},{4,12},{5,13},{6,14},{7,15},{8,0},{9,1},... | collective-permute-start | bytes 3440648 | tf_op jit(solution)/shard_map/ppermute | solution.py:75
  570.5 37.6 %collective-permute-start.71 = (bf16[2,2,224,512]{3,2,1,0:T(8,128)(2,1)}, bf16[2,2,224,512]{3,2,1,0:T(8,128)(2,1)}, u32[]{:S(2)}, u32[]{:S(2)}) collective-permute-start(bf16[2,2,224,512]{3,2,1,0:T(8,128)(2,1)} %get-tuple-element.344), channel_id=1, source_target_pairs={{0,16},{1,17},{2,18},{3,19},{4,20},{5,21},{6,22},{7,23},{8,24},{9,... | collective-permute-start | bytes 2752520 | tf_op jit(solution)/shard_map/ppermute | solution.py:75
  577.2 25.7 %collective-permute-start.69 = (bf16[256,1152]{1,0:T(8,128)(2,1)}, bf16[256,1152]{1,0:T(8,128)(2,1)}, u32[]{:S(2)}, u32[]{:S(2)}) collective-permute-start(bf16[256,1152]{1,0:T(8,128)(2,1)} %get-tuple-element.335), channel_id=1, source_target_pairs={{0,2},{1,3},{2,0},{3,1},{4,6},{5,7},{6,4},{7,5},{8,10},{9,11},{10,... | collective-permute-start | bytes 1769480 | tf_op jit(solution)/shard_map/ppermute | solution.py:75
  601.7 59.5 %collective-permute-start.75 = (bf16[2,2,144,1792]{3,2,1,0:T(8,128)(2,1)}, bf16[2,2,144,1792]{3,2,1,0:T(8,128)(2,1)}, u32[]{:S(2)}, u32[]{:S(2)}) collective-permute-start(bf16[2,2,144,1792]{3,2,1,0:T(8,128)(2,1)} %get-tuple-element.355), channel_id=1, source_target_pairs={{0,8},{1,9},{2,10},{3,11},{4,12},{5,13},{6,14},{7,15},{8,0},{9,1},... | collective-permute-start | bytes 6193160 | tf_op jit(solution)/shard_map/ppermute | solution.py:75
  602.3 58.9 %collective-permute-start.76 = (bf16[2,2,144,1792]{3,2,1,0:T(8,128)(2,1)}, bf16[2,2,144,1792]{3,2,1,0:T(8,128)(2,1)}, u32[]{:S(2)}, u32[]{:S(2)}) collective-permute-start(bf16[2,2,144,1792]{3,2,1,0:T(8,128)(2,1)} %get-tuple-element.357), channel_id=1, source_target_pairs={{0,16},{1,17},{2,18},{3,19},{4,20},{5,21},{6,22},{7,23},{8,24},{9,... | collective-permute-start | bytes 6193160 | tf_op jit(solution)/shard_map/ppermute | solution.py:75
  630.1 31.1 %collective-permute-start.77 = (bf16[2,224,640]{2,1,0:T(8,128)(2,1)}, bf16[2,224,640]{2,1,0:T(8,128)(2,1)S(1)}, u32[]{:S(2)}, u32[]{:S(2)}) collective-permute-start(bf16[2,224,640]{2,1,0:T(8,128)(2,1)} %get-tuple-element.358), channel_id=1, source_target_pairs={{0,16},{1,17},{2,18},{3,19},{4,20},{5,21},{6,22},{7,23},{8,24},{9,... | collective-permute-start | bytes 1720328 | tf_op jit(solution)/shard_map/ppermute | solution.py:75
  641.4 30.1 %collective-permute-start.74 = (bf16[256,512]{1,0:T(8,128)(2,1)S(1)}, bf16[256,512]{1,0:T(8,128)(2,1)S(1)}, u32[]{:S(2)}, u32[]{:S(2)}) collective-permute-start(bf16[256,512]{1,0:T(8,128)(2,1)S(1)} %get-tuple-element.353), channel_id=1, source_target_pairs={{0,4},{1,5},{2,6},{3,7},{4,0},{5,1},{6,2},{7,3},{8,12},{9,13},{10,... | collective-permute-start | bytes 786440 | tf_op jit(solution)/shard_map/ppermute | solution.py:75
  659.6 63.1 %collective-permute-start.84 = (bf16[2,2,2,48,1664]{4,3,2,1,0:T(8,128)(2,1)}, bf16[2,2,2,48,1664]{4,3,2,1,0:T(8,128)(2,1)}, u32[]{:S(2)}, u32[]{:S(2)}) collective-permute-start(bf16[2,2,2,48,1664]{4,3,2,1,0:T(8,128)(2,1)} %get-tuple-element.376), channel_id=1, source_target_pairs={{0,8},{1,9},{2,10},{3,11},{4,12},{5,13},{6,14},{7,15},{8,0},{9,1},... | collective-permute-start | bytes 3833864 | tf_op jit(solution)/shard_map/ppermute | solution.py:75
  670.9 51.8 %collective-permute-start.85 = (bf16[2,2,2,56,1280]{4,3,2,1,0:T(8,128)(2,1)}, bf16[2,2,2,56,1280]{4,3,2,1,0:T(8,128)(2,1)S(1)}, u32[]{:S(2)}, u32[]{:S(2)}) collective-permute-start(bf16[2,2,2,56,1280]{4,3,2,1,0:T(8,128)(2,1)} %copy-done.149), channel_id=1, source_target_pairs={{0,16},{1,17},{2,18},{3,19},{4,20},{5,21},{6,22},{7,23},{8,24},{9,... | collective-permute-start | bytes 3440648 | tf_op jit(solution)/shard_map/ppermute | solution.py:75
  681.0 37.8 %collective-permute-start.86 = (bf16[2,144,1792]{2,1,0:T(8,128)(2,1)}, bf16[2,144,1792]{2,1,0:T(8,128)(2,1)S(1)}, u32[]{:S(2)}, u32[]{:S(2)}) collective-permute-start(bf16[2,144,1792]{2,1,0:T(8,128)(2,1)} %copy-done.150), channel_id=1, source_target_pairs={{0,16},{1,17},{2,18},{3,19},{4,20},{5,21},{6,22},{7,23},{8,24},{9,... | collective-permute-start | bytes 3096584 | tf_op jit(solution)/shard_map/ppermute | solution.py:75
  681.6 37.3 %collective-permute-start.87 = (bf16[2,144,1792]{2,1,0:T(8,128)(2,1)}, bf16[2,144,1792]{2,1,0:T(8,128)(2,1)S(1)}, u32[]{:S(2)}, u32[]{:S(2)}) collective-permute-start(bf16[2,144,1792]{2,1,0:T(8,128)(2,1)} %get-tuple-element.381), channel_id=1, source_target_pairs={{0,8},{1,9},{2,10},{3,11},{4,12},{5,13},{6,14},{7,15},{8,0},{9,1},... | collective-permute-start | bytes 3096584 | tf_op jit(solution)/shard_map/ppermute | solution.py:75
  699.7 30.3 %collective-permute-start.95 = (bf16[2,2,2,56,768]{4,3,2,1,0:T(8,128)(2,1)S(1)}, bf16[2,2,2,56,768]{4,3,2,1,0:T(8,128)(2,1)S(1)}, u32[]{:S(2)}, u32[]{:S(2)}) collective-permute-start(bf16[2,2,2,56,768]{4,3,2,1,0:T(8,128)(2,1)S(1)} %get-tuple-element.396), channel_id=1, source_target_pairs={{0,8},{1,9},{2,10},{3,11},{4,12},{5,13},{6,14},{7,15},{8,0},{9,1},... | collective-permute-start | bytes 2064392 | tf_op jit(solution)/shard_map/ppermute | solution.py:75
  725.0 47.7 %collective-permute-start.93 = (bf16[2,2,48,1664]{3,2,1,0:T(8,128)(2,1)S(1)}, bf16[2,2,48,1664]{3,2,1,0:T(8,128)(2,1)S(1)}, u32[]{:S(2)}, u32[]{:S(2)}) collective-permute-start(bf16[2,2,48,1664]{3,2,1,0:T(8,128)(2,1)S(1)} %get-tuple-element.393), channel_id=1, source_target_pairs={{0,16},{1,17},{2,18},{3,19},{4,20},{5,21},{6,22},{7,23},{8,24},{9,... | collective-permute-start | bytes 1916936 | tf_op jit(solution)/shard_map/ppermute | solution.py:75
  725.6 47.1 %collective-permute-start.94 = (bf16[2,2,56,1280]{3,2,1,0:T(8,128)(2,1)S(1)}, bf16[2,2,56,1280]{3,2,1,0:T(8,128)(2,1)S(1)}, u32[]{:S(2)}, u32[]{:S(2)}) collective-permute-start(bf16[2,2,56,1280]{3,2,1,0:T(8,128)(2,1)S(1)} %get-tuple-element.395), channel_id=1, source_target_pairs={{0,8},{1,9},{2,10},{3,11},{4,12},{5,13},{6,14},{7,15},{8,0},{9,1},... | collective-permute-start | bytes 1720328 | tf_op jit(solution)/shard_map/ppermute | solution.py:75
  727.1 33.4 %collective-permute-start.97 = (bf16[144,1792]{1,0:T(8,128)(2,1)S(1)}, bf16[144,1792]{1,0:T(8,128)(2,1)S(1)}, u32[]{:S(2)}, u32[]{:S(2)}) collective-permute-start(bf16[144,1792]{1,0:T(8,128)(2,1)S(1)} %get-tuple-element.399), channel_id=1, source_target_pairs={{0,4},{1,5},{2,6},{3,7},{4,0},{5,1},{6,2},{7,3},{8,12},{9,13},{10,... | collective-permute-start | bytes 1548296 | tf_op jit(solution)/shard_map/ppermute | solution.py:75
  727.8 43.6 %collective-permute-start.98 = (bf16[144,1792]{1,0:T(8,128)(2,1)S(1)}, bf16[144,1792]{1,0:T(8,128)(2,1)S(1)}, u32[]{:S(2)}, u32[]{:S(2)}) collective-permute-start(bf16[144,1792]{1,0:T(8,128)(2,1)S(1)} %get-tuple-element.401), channel_id=1, source_target_pairs={{0,4},{1,5},{2,6},{3,7},{4,0},{5,1},{6,2},{7,3},{8,12},{9,13},{10,... | collective-permute-start | bytes 1548296 | tf_op jit(solution)/shard_map/ppermute | solution.py:75
  730.7 41.9 %collective-permute-start.96 = (bf16[2,2,56,768]{3,2,1,0:T(8,128)(2,1)S(1)}, bf16[2,2,56,768]{3,2,1,0:T(8,128)(2,1)S(1)}, u32[]{:S(2)}, u32[]{:S(2)}) collective-permute-start(bf16[2,2,56,768]{3,2,1,0:T(8,128)(2,1)S(1)} %get-tuple-element.398), channel_id=1, source_target_pairs={{0,16},{1,17},{2,18},{3,19},{4,20},{5,21},{6,22},{7,23},{8,24},{9,... | collective-permute-start | bytes 1032200 | tf_op jit(solution)/shard_map/ppermute | solution.py:75
  773.6 20.3 %collective-permute-start.99 = (bf16[2,48,1664]{2,1,0:T(8,128)(2,1)S(1)}, bf16[2,48,1664]{2,1,0:T(8,128)(2,1)S(1)}, u32[]{:S(2)}, u32[]{:S(2)}) collective-permute-start(bf16[2,48,1664]{2,1,0:T(8,128)(2,1)S(1)} %get-tuple-element.404), channel_id=1, source_target_pairs={{0,2},{1,3},{2,0},{3,1},{4,6},{5,7},{6,4},{7,5},{8,10},{9,11},{10,... | collective-permute-start | bytes 958472 | tf_op jit(solution)/shard_map/ppermute | solution.py:75
  773.6 20.2 %collective-permute-start.100 = (bf16[2,56,1280]{2,1,0:T(8,128)(2,1)S(1)}, bf16[2,56,1280]{2,1,0:T(8,128)(2,1)S(1)}, u32[]{:S(2)}, u32[]{:S(2)}) collective-permute-start(bf16[2,56,1280]{2,1,0:T(8,128)(2,1)S(1)} %get-tuple-element.406), channel_id=1, source_target_pairs={{0,2},{1,3},{2,0},{3,1},{4,6},{5,7},{6,4},{7,5},{8,10},{9,11},{10,... | collective-permute-start | bytes 860168 | tf_op jit(solution)/shard_map/ppermute | solution.py:75
  775.7 21.9 %collective-permute-start.105 = (bf16[2,36,1792]{2,1,0:T(8,128)(2,1)S(1)}, bf16[2,36,1792]{2,1,0:T(8,128)(2,1)S(1)}, u32[]{:S(2)}, u32[]{:S(2)}) collective-permute-start(bf16[2,36,1792]{2,1,0:T(8,128)(2,1)S(1)} %get-tuple-element.418), channel_id=1, source_target_pairs={{0,1},{1,0},{2,3},{3,2},{4,5},{5,4},{6,7},{7,6},{8,9},{9,8},{10,11... | collective-permute-start | bytes 774152 | tf_op jit(solution)/shard_map/ppermute | solution.py:75
  775.7 31.5 %collective-permute-start.106 = (bf16[2,36,1792]{2,1,0:T(8,128)(2,1)S(1)}, bf16[2,36,1792]{2,1,0:T(8,128)(2,1)S(1)}, u32[]{:S(2)}, u32[]{:S(2)}) collective-permute-start(bf16[2,36,1792]{2,1,0:T(8,128)(2,1)S(1)} %get-tuple-element.419), channel_id=1, source_target_pairs={{0,2},{1,3},{2,0},{3,1},{4,6},{5,7},{6,4},{7,5},{8,10},{9,11},{10,... | collective-permute-start | bytes 774152 | tf_op jit(solution)/shard_map/ppermute | solution.py:75
  794.6 20.4 %collective-permute-start.102 = (bf16[48,1664]{1,0:T(8,128)(2,1)S(1)}, bf16[48,1664]{1,0:T(8,128)(2,1)S(1)}, u32[]{:S(2)}, u32[]{:S(2)}) collective-permute-start(bf16[48,1664]{1,0:T(8,128)(2,1)S(1)} %get-tuple-element.410), channel_id=1, source_target_pairs={{0,4},{1,5},{2,6},{3,7},{4,0},{5,1},{6,2},{7,3},{8,12},{9,13},{10,... | collective-permute-start | bytes 479240 | tf_op jit(solution)/shard_map/ppermute | solution.py:75
  (215 other events, 1942.5 us)
Sparse Core Ops, SparseCore 0:
  137.7 30.1 all-gather.2
  310.8 31.2 all-gather.4

commit v3 on v2

--- a/solution.py
+++ b/solution.py
@@ -338,11 +338,14 @@
     )(*operands, *ties)
 
 
-def ff_weights_body(with_old, *refs):
+def ff_weights_body(split, with_old, *refs):
+    if split:
+        (extent, stages), coords_ref, refs = split, refs[0], refs[1:]
     x_refs = refs[:4]
     dg_ref, du_ref = refs[4:6]
     old_refs = refs[6:8] if with_old else (None, None)
-    wg_ref, wu_ref, turned_ref = refs[8 if with_old else 6 :]
+    refs = refs[8 if with_old else 6 :]
+    outs, turned_ref = refs[: 4 if split else 2], refs[4 if split else 2]
     size = x_refs[0].shape[0]
 
     @pl.when(pl.program_id(0) == 0)
@@ -350,32 +353,66 @@
         for number, x_ref in enumerate(x_refs):
             turned_ref[:, number * size : (number + 1) * size] = x_ref[...].T
 
-    for grad_ref, old_ref, out_ref in (
-        (dg_ref, old_refs[0], wg_ref),
-        (du_ref, old_refs[1], wu_ref),
-    ):
+    for kind, grad_ref in enumerate((dg_ref, du_ref)):
         total = matmul(turned_ref[...], grad_ref[...])
-        if old_ref is not None:
-            total = total + old_ref[...].astype(F32)
-        out_ref[...] = rounded(total)
-
-
-def ff_weights(blocks, grad_gate, grad_up, old, ties=()):
+        if with_old:
+            total = total + old_refs[kind][...].astype(F32)
+        total = rounded(total)
+        if not split:
+            outs[kind][...] = total
+            continue
+        held_ref = refs[5]
+        rows = held_ref.shape[-2]
+        for number, index in enumerate(itertools.product(*[range(count) for count in extent])):
+            held_ref[index] = total[number * rows : (number + 1) * rows]
+        name, position = stages[kind]
+        rest = [range(count) for number, count in enumerate(extent) if number != position]
+        for side in range(2):
+            for index in itertools.product(*rest):
+                source = index[:position] + (coords_ref[name] ^ side,) + index[position:]
+                outs[2 * kind + side][index] = held_ref[source]
+
+
+def ff_weights(grid, coordinates, blocks, grad_gate, grad_up, old, stages=None, ties=()):
     size, width = blocks[0].shape
     rows = 4 * size
     wide = grad_gate.shape[1]
     column = pl.BlockSpec((rows, TILE), lambda j: (0, j))
     block = pl.BlockSpec((width, TILE), lambda j: (0, j))
-    operands = [*blocks, grad_gate, grad_up] + (list(old) if old is not None else [])
+    in_specs = [full((size, width))] * 4 + [column, column]
+    operands = [*blocks, grad_gate, grad_up]
+    scratch = [pltpu.VMEM((width, rows), BF)]
+    if old is not None:
+        in_specs += [block, block]
+        operands += list(old)
+    if stages is None:
+        split = None
+        outs = [jax.ShapeDtypeStruct((width, wide), BF)] * 2
+        out_specs = [block, block]
+    else:
+        names = ("y", "x", "p")
+        extent = grid.extent(names)
+        split = (extent, [(NAMES.index(stage), names.index(stage)) for stage in stages])
+        piece = width // grid.groups
+        in_specs = [pl.BlockSpec(memory_space=pltpu.SMEM)] + in_specs
+        operands = [coordinates] + operands
+        scratch.append(pltpu.VMEM(extent + (piece, TILE), BF))
+        outs = []
+        out_specs = []
+        for stage in stages:
+            left = grid.extent([name for name in names if name != stage])
+            for side in range(2):
+                outs.append(jax.ShapeDtypeStruct(left + (piece, wide), BF))
+                out_specs.append(
+                    pl.BlockSpec(left + (piece, TILE), lambda j: (0,) * (len(left) + 1) + (j,))
+                )
     return kernel_call(
-        functools.partial(ff_weights_body, old is not None),
+        functools.partial(ff_weights_body, split, old is not None),
         (wide // TILE,),
-        [full((size, width))] * 4
-        + [column, column]
-        + ([block, block] if old is not None else []),
-        [block, block],
-        [jax.ShapeDtypeStruct((width, wide), BF)] * 2,
-        [pltpu.VMEM((width, rows), BF)],
+        in_specs,
+        out_specs,
+        outs,
+        scratch,
         ties,
     )(*operands, *ties)
 
@@ -1239,8 +1276,6 @@
         own_kv, normed_b, low_rank_b, residual, both = projected
         mixed_b, log_total = attended
         side_b, middle, unused = left
-        ff_own, gate_b, up_b, *ff_sent = ff_forward(ff_in, w_gate, w_up, w_down)
-        own, other = tokens_out(grid, ff_own, ff_sent, ties)
         spread_own, spread_sent = whole_call(
             functools.partial(
                 spread_body,
@@ -1252,9 +1287,13 @@
             [shape(tokens, grid.devices // 2 * (qkv_block + out_block))] * 2,
             coordinates,
             [normed_b, low_rank_b, mixed_b, side_b],
-            [gate_b],
+            (),
             [pltpu.VMEM((2, tokens, grid.devices // 2 * (qkv_block + out_block)), BF)],
         )
+        ff_own, gate_b, up_b, *ff_sent = ff_forward(
+            ff_in, w_gate, w_up, w_down, [spread_sent]
+        )
+        own, other = tokens_out(grid, ff_own, ff_sent, ties)
         cache = (
             residual, (spread_own, grid.permute(spread_sent, {"c": 1})), queries, both, log_total,
             middle, ff_in, gate_b, up_b,
@@ -1283,6 +1322,8 @@
         return fold(
             grid, coordinates, [(item[0], stage, [item[1]]) for item, stage in stages], ties
         )
+
+    y_size = grid.sizes["y"]
 
     def with_core(values):
         return values, grid.permute(values, {"c": 1})
@@ -1316,23 +1357,25 @@
             )
             ties = [down[0][1][0]]
         own, other = tokens_out(grid, own, sent, ties)
-        d_gate, d_up = ff_weights(
+        pair = ff_weights(
+            grid,
+            coordinates,
             ff_in,
             grad_gate_b,
             grad_up_b,
             (old["gate"], old["up"]) if last else None,
+            ("x", "y" if y_size == 2 else "x") if last else None,
             [own],
         )
-        ties = [d_gate]
+        ties = [pair[0]]
         if last:
-            d_gate, d_up = fold(
-                grid,
-                coordinates,
-                [
-                    (group_names, "x", [[grouped(d_gate)]]),
-                    (group_names, "y", [[grouped(d_up)]]),
-                ],
-            )
+            d_gate = (("y", "p"), [pair[0], grid.permute(pair[1], {"x": 1})])
+            if y_size == 2:
+                d_up = (("x", "p"), [pair[2], grid.permute(pair[3], {"y": 1})])
+            else:
+                d_up = (("y", "p"), [pair[2], grid.permute(pair[3], {"x": 1})])
+        else:
+            d_gate, d_up = pair
         grad_middle, grad_branch_b, grad_side_b, grad_mixed_b, gain_grad_ff = whole_call(
             functools.partial(enter_back_body, loop == 0),
             [
@@ -1349,7 +1392,7 @@
                 grid,
                 coordinates,
                 [(down[0][0], "y", [down[0][1]]), (down[1][0], "x", [down[1][1]])],
-                [grad_mixed_b, d_gate[1][0]],
+                [grad_mixed_b],
             )
             ties = [down[0][1][0]]
         kv_own, kv_sent, grad_queries_b = pl.pallas_call(
@@ -1393,7 +1436,7 @@
                 coordinates,
                 [
                     (d_gate[0], "y", [d_gate[1]]),
-                    (d_up[0], "x", [d_up[1]]),
+                    (d_up[0], d_up[0][0], [d_up[1]]),
                     (down[0][0], "p", [down[0][1]]),
                     (down[1][0], "p", [down[1][1]]),
                 ],

time: 831 us -> 823 us (level)
  waiting for transfers between devices: 362 us -> 350 us
    ppermute x108, waiting for transfers between devices: 337 us -> 325 us  [permute(): return lax.ppermute(values, AXES, pairs)]
    unnamed x308 -> x310, local copies, waits for them, and re-layouts: 68.2 us -> 73.8 us
    pallas_call x64 -> x63, Pallas kernels: 140 us -> 134 us  [whole_call(): pl.pallas_call(tied(body, len(specs), ties), out_shape=out_shape, in_spec...]
  transfers between devices with their start and end apart: 110 -> 110, of which waited for: 52 -> 51; matrix products, arithmetic and copies ran while one was open for 0% -> 0% of each run, Pallas kernels for 24% -> 24%
where the time goes in v3:
time: 823 us; the launch traced here: 816 us
  waiting for transfers between devices  350 us (43%)
  Pallas kernels  291 us (35%)
  starting transfers between devices  81.9 us (10%)
  local copies, waits for them, and re-layouts  74.1 us (9%)
  between operations  15.6 us (2%)
    ppermute x108, waiting for transfers between devices, permute(): return lax.ppermute(values, AXES, pairs)  325 us
    pallas_call x63, Pallas kernels, whole_call(): pl.pallas_call(tied(body, len(specs), ties), out_shape=out_shape, in_spec...  134 us
    ppermute x108, starting transfers between devices, permute(): return lax.ppermute(values, AXES, pairs)  81.7 us
    unnamed x310, local copies, waits for them, and re-layouts  73.8 us
    pallas_call x2, Pallas kernels, ff_backward(): kernel_call(functools.partial(ff_backward_body, old is not None), (wide /...  61.7 us
    pallas_call x2, Pallas kernels, ff_forward(): kernel_call(ff_forward_body, (wide // TILE,), [full((size, width))] * 4 +...  46.8 us
    pallas_call x2, Pallas kernels, ff_weights(): kernel_call(functools.partial(ff_weights_body, split, old is not None), (...  29.3 us
    all_gather x2, waiting for transfers between devices, project_kv(): both = lax.all_gather(own_kv, 'blk', axis=0, tiled=True)  24.7 us
  transfers between devices with their start and end apart: 110, of which 51 were waited for; matrix products, arithmetic and copies ran while one was open for 0% of the time, Pallas kernels for 24%

profile of v3, /device:TPU:0, one launch (start us, length us, event | category | flops | bytes accessed | tf_op | source)
XLA Modules:
  0.0 815.6 jit_solution(2290624138927154988)
XLA Ops:
  12.9 4.1 collective-permute-start
  17.1 16.9 %collective-permute-done.1.refs_3_ = bf16[48,1920]{1,0:T(8,128)(2,1)S(1)} collective-permute-done((bf16[48,1920]{1,0:T(8,128)(2,1)S(1)}, bf16[48,1920]{1,0:T(8,128)(2,1)S(1)}, u32[]{:S(2)}, u32[]{:S(2)}) %collective-permute-start.1) | collective-permute-done | bytes 184352 | tf_op jit(solution)/shard_map/ppermute | solution.py:75
  37.5 14.8 %collective-permute-done.3.refs_3_ = bf16[2,48,1920]{2,1,0:T(8,128)(2,1)S(1)} collective-permute-done((bf16[2,48,1920]{2,1,0:T(8,128)(2,1)S(1)}, bf16[2,48,1920]{2,1,0:T(8,128)(2,1)S(1)}, u32[]{:S(2)}, u32[]{:S(2)}) %collective-permute-start.3) | collective-permute-done | bytes 368672 | tf_op jit(solution)/shard_map/ppermute | solution.py:75
  57.2 7.8 collective-permute-done.7.refs_3_
  65.0 5.4 collective-permute-done.8.refs_4_
  74.5 4.4 collective-permute-start.15
  79.0 28.6 %collective-permute-done.10.refs_3_ = bf16[2,2,2,48,1920]{4,3,2,1,0:T(8,128)(2,1)} collective-permute-done((bf16[2,2,2,48,1920]{4,3,2,1,0:T(8,128)(2,1)S(1)}, bf16[2,2,2,48,1920]{4,3,2,1,0:T(8,128)(2,1)}, u32[]{:S(2)}, u32[]{:S(2)}) %collective-permute-start.10) | collective-permute-done | bytes 1474592 | tf_op jit(solution)/shard_map/ppermute | solution.py:75
  125.8 4.3 shard_map.212
  141.8 20.4 %collective-permute-done.21.refs_3_ = bf16[2,144,1792]{2,1,0:T(8,128)(2,1)S(1)} collective-permute-done((bf16[2,144,1792]{2,1,0:T(8,128)(2,1)}, bf16[2,144,1792]{2,1,0:T(8,128)(2,1)S(1)}, u32[]{:S(2)}, u32[]{:S(2)}) %collective-permute-start.21) | collective-permute-done | bytes 1032224 | tf_op jit(solution)/shard_map/ppermute | solution.py:75
  186.3 3.9 shard_map.216
  193.8 4.6 shard_map.217
  207.5 22.7 %collective-permute-done.30.refs_3_ = bf16[2,224,512]{2,1,0:T(8,128)(2,1)S(1)} collective-permute-done((bf16[2,224,512]{2,1,0:T(8,128)(2,1)S(1)}, bf16[2,224,512]{2,1,0:T(8,128)(2,1)S(1)}, u32[]{:S(2)}, u32[]{:S(2)}) %collective-permute-start.30) | collective-permute-done | bytes 458784 | tf_op jit(solution)/shard_map/ppermute | solution.py:75
  239.4 4.2 shard_map.219.refs_4_.refs_6_
  243.6 5.1 shard_map.224
  249.6 4.7 collective-permute-done.32
  254.3 3.6 collective-permute-done.31
  257.9 4.0 shard_map.223.refs_6_.refs_8_
  262.0 23.6 %shard_map.225 = (f32[512,1152]{1,0:T(8,128)}, bf16[1024,1792]{1,0:T(8,128)(2,1)}, bf16[1024,1792]{1,0:T(8,128)(2,1)}, bf16[128,1152]{1,0:T(8,128)(2,1)S(1)}, bf...) custom-call(bf16[256,1152]{1,0:T(8,128)(2,1)S(1)} %get-tuple-element.254.refs_4_.refs_0_.re, ...), custom_call_target="tpu_custom_call" | custom-call | tf_op jit(solution)/shard_map/pallas_call | solution.py:232
  292.3 13.6 %collective-permute-done.38.refs_2_ = bf16[256,1152]{1,0:T(8,128)(2,1)S(1)} collective-permute-done((bf16[256,1152]{1,0:T(8,128)(2,1)S(1)}, bf16[256,1152]{1,0:T(8,128)(2,1)S(1)}, u32[]{:S(2)}, u32[]{:S(2)}) %collective-permute-start.38) | collective-permute-done | bytes 589856 | tf_op jit(solution)/shard_map/ppermute | solution.py:75
  306.0 3.6 shard_map.227
  319.5 24.7 %all-gather.5.cloned.1.call-done.kv_ref = bf16[2048,512]{1,0:T(8,128)(2,1)} async-done(((bf16[256,512]{1,0:T(8,128)(2,1)}), bf16[2048,512]{1,0:T(8,128)(2,1)}) %all-gather.5.cloned.1.call-update) | async-done | bytes 2097168 | tf_op jit(solution)/shard_map/all_gather | solution.py:1201
  348.7 4.6 shard_map.229
  358.2 14.0 %collective-permute-done.39.refs_1_ = bf16[256,1152]{1,0:T(8,128)(2,1)S(1)} collective-permute-done((bf16[256,1152]{1,0:T(8,128)(2,1)S(1)}, bf16[256,1152]{1,0:T(8,128)(2,1)S(1)}, u32[]{:S(2)}, u32[]{:S(2)}) %collective-permute-start.39) | collective-permute-done | bytes 589856 | tf_op jit(solution)/shard_map/ppermute | solution.py:75
  372.2 4.9 shard_map.231
  377.1 23.2 %shard_map.232 = (f32[512,1152]{1,0:T(8,128)}, bf16[1024,1792]{1,0:T(8,128)(2,1)}, bf16[1024,1792]{1,0:T(8,128)(2,1)}, bf16[128,1152]{1,0:T(8,128)(2,1)S(1)}, bf...) custom-call(bf16[256,1152]{1,0:T(8,128)(2,1)S(1)} %get-tuple-element.279.refs_0_, ...), custom_call_target="tpu_custom_call" | custom-call | tf_op jit(solution)/shard_map/pallas_call | solution.py:232
  409.3 30.9 %shard_map.235 = (f32[512,1152]{1,0:T(8,128)}, bf16[1024,1792]{1,0:T(8,128)(2,1)}, bf16[1024,1792]{1,0:T(8,128)(2,1)}, bf16[1792,640]{1,0:T(8,128)(2,1)}, bf16[1...) custom-call(bf16[256,1152]{1,0:T(8,128)(2,1)S(1)} %copy-done.76, ...), custom_call_target="tpu_custom_call" | custom-call | tf_op jit(solution)/shard_map/pallas_call | solution.py:319
  446.5 13.8 %shard_map.237 = (bf16[1152,1792]{1,0:T(8,128)(2,1)}, bf16[1152,1792]{1,0:T(8,128)(2,1)}) custom-call(bf16[256,1152]{1,0:T(8,128)(2,1)S(1)} %get-tuple-element.279.refs_0_, bf16[256,1152]{1,0:T(8,128)(2,1)S(1)} %collective-permute-done.39.refs_1_, bf16[256,1152]{1,0:T(8,128)(2,1)S(1)} %collective-permute-done.40.refs_2_, ...), custom_call_target="tpu_custom_call" | custom-call | tf_op jit(solution)/shard_map/pallas_call | solution.py:409
  461.3 4.2 shard_map.238
  466.7 9.9 %shard_map.239 = (bf16[4,256,512]{2,1,0:T(8,128)(2,1)S(1)}, bf16[4,256,512]{2,1,0:T(8,128)(2,1)S(1)}, bf16[256,1024]{1,0:T(8,128)(2,1)S(1)}) custom-call(bf16[256,1024]{1,0:T(8,128)(2,1)S(1)} %copy-done.43, bf16[2048,512]{1,0:T(8,128)(2,1)} %all-gather.5.cloned.1.call-done.kv_ref, s32[256,1]{1,0:T(8,128)S(1)} %copy-done.54, s32[256,1]{1,0:T(8,128)S(1)} %copy-done.57, ...), custom_call_target="tpu_custom_call" | custom-call | tf_op jit(solution)/shard_map/pallas_call | solution.py:1398
  481.2 12.9 %collective-permute-done.55.refs_1_ = bf16[2,256,512]{2,1,0:T(8,128)(2,1)S(1)} collective-permute-done((bf16[2,256,512]{2,1,0:T(8,128)(2,1)S(1)}, bf16[2,256,512]{2,1,0:T(8,128)(2,1)S(1)}, u32[]{:S(2)}, u32[]{:S(2)}) %collective-permute-start.55) | collective-permute-done | bytes 524320 | tf_op jit(solution)/shard_map/ppermute | solution.py:75
  502.4 6.4 collective-permute-done.56.refs_1_
  510.7 4.2 shard_map.245
  516.0 15.2 %collective-permute-done.62.refs_1_ = bf16[256,1152]{1,0:T(8,128)(2,1)S(1)} collective-permute-done((bf16[256,1152]{1,0:T(8,128)(2,1)S(1)}, bf16[256,1152]{1,0:T(8,128)(2,1)S(1)}, u32[]{:S(2)}, u32[]{:S(2)}) %collective-permute-start.62) | collective-permute-done | bytes 589856 | tf_op jit(solution)/shard_map/ppermute | solution.py:75
  533.3 30.8 %shard_map.246 = (f32[512,1152]{1,0:T(8,128)}, bf16[1024,1792]{1,0:T(8,128)(2,1)}, bf16[1024,1792]{1,0:T(8,128)(2,1)}, bf16[1792,640]{1,0:T(8,128)(2,1)}, bf16[1...) custom-call(bf16[256,1152]{1,0:T(8,128)(2,1)S(1)} %get-tuple-element, ...), custom_call_target="tpu_custom_call" | custom-call | tf_op jit(solution)/shard_map/pallas_call | solution.py:319
  576.0 15.5 %shard_map.249 = (bf16[2,2,144,1792]{3,2,1,0:T(8,128)(2,1)S(1)}, bf16[2,2,144,1792]{3,2,1,0:T(8,128)(2,1)}, bf16[2,2,144,1792]{3,2,1,0:T(8,128)(2,1)}, bf16[2,2,144,1792]{3,2,1,0:T(8,128)(2,1)}) custom-call(s32[5]{0:T(128)S(1)} %stack.23.refs_0_.coords_ref.refs_9_, bf16[256,1152]{1,0:T(8,128)(2,1)S(1)} %copy-done.36, bf16[256,1152]{1,0:T(8,128)(2,1)S(1)} %copy-done.80, ...), custom_call_target="tpu_custom_call" | custom-call | tf_op jit(solution)/shard_map/pallas_call | solution.py:409
  595.9 4.1 shard_map.250
  604.0 9.8 %shard_map.252 = (bf16[4,256,512]{2,1,0:T(8,128)(2,1)S(1)}, bf16[4,256,512]{2,1,0:T(8,128)(2,1)S(1)}, bf16[256,1024]{1,0:T(8,128)(2,1)S(1)}) custom-call(bf16[256,1024]{1,0:T(8,128)(2,1)S(1)} %copy-done.20, bf16[2048,512]{1,0:T(8,128)(2,1)} %all-gather.3.cloned.1.call-done.refs_1_, s32[256,1]{1,0:T(8,128)S(1)} %copy-done.54, s32[256,1]{1,0:T(8,128)S(1)} %copy-done.57, ...), custom_call_target="tpu_custom_call" | custom-call | tf_op jit(solution)/shard_map/pallas_call | solution.py:1398
  623.6 7.7 collective-permute-done.73.refs_1_
  640.0 4.5 shard_map.256
  653.4 5.5 shard_map.259
  663.8 5.2 shard_map.261
  679.6 12.0 %collective-permute-done.88.refs_1_ = bf16[224,640]{1,0:T(8,128)(2,1)S(1)} collective-permute-done((bf16[224,640]{1,0:T(8,128)(2,1)S(1)}, bf16[224,640]{1,0:T(8,128)(2,1)S(1)}, u32[]{:S(2)}, u32[]{:S(2)}) %collective-permute-start.88) | collective-permute-done | bytes 286752 | tf_op jit(solution)/shard_map/ppermute | solution.py:75
  693.9 16.7 %collective-permute-done.86.refs_2_ = bf16[2,144,1792]{2,1,0:T(8,128)(2,1)S(1)} collective-permute-done((bf16[2,144,1792]{2,1,0:T(8,128)(2,1)S(1)}, bf16[2,144,1792]{2,1,0:T(8,128)(2,1)S(1)}, u32[]{:S(2)}, u32[]{:S(2)}) %collective-permute-start.86) | collective-permute-done | bytes 1032224 | tf_op jit(solution)/shard_map/ppermute | solution.py:75
  724.1 28.4 %collective-permute-done.97.refs_2_ = bf16[144,1792]{1,0:T(8,128)(2,1)S(1)} collective-permute-done((bf16[144,1792]{1,0:T(8,128)(2,1)S(1)}, bf16[144,1792]{1,0:T(8,128)(2,1)S(1)}, u32[]{:S(2)}, u32[]{:S(2)}) %collective-permute-start.97) | collective-permute-done | bytes 516128 | tf_op jit(solution)/shard_map/ppermute | solution.py:75
  752.5 11.0 %collective-permute-done.98.refs_4_ = bf16[144,1792]{1,0:T(8,128)(2,1)S(1)} collective-permute-done((bf16[144,1792]{1,0:T(8,128)(2,1)S(1)}, bf16[144,1792]{1,0:T(8,128)(2,1)S(1)}, u32[]{:S(2)}, u32[]{:S(2)}) %collective-permute-start.98) | collective-permute-done | bytes 516128 | tf_op jit(solution)/shard_map/ppermute | solution.py:75
  769.7 16.2 %collective-permute-done.101.refs_5_ = bf16[2,56,768]{2,1,0:T(8,128)(2,1)S(1)} collective-permute-done((bf16[2,56,768]{2,1,0:T(8,128)(2,1)S(1)}, bf16[2,56,768]{2,1,0:T(8,128)(2,1)S(1)}, u32[]{:S(2)}, u32[]{:S(2)}) %collective-permute-start.101) | collective-permute-done | bytes 172064 | tf_op jit(solution)/shard_map/ppermute | solution.py:75
  790.0 9.2 %collective-permute-done.106.refs_3_ = bf16[2,36,1792]{2,1,0:T(8,128)(2,1)S(1)} collective-permute-done((bf16[2,36,1792]{2,1,0:T(8,128)(2,1)S(1)}, bf16[2,36,1792]{2,1,0:T(8,128)(2,1)S(1)}, u32[]{:S(2)}, u32[]{:S(2)}) %collective-permute-start.106) | collective-permute-done | bytes 258080 | tf_op jit(solution)/shard_map/ppermute | solution.py:75
  799.2 4.3 collective-permute-done.107.refs_4_
  (563 shorter events, 249.9 us)
Async XLA Ops:
  7.2 184.8 %all-gather.3.cloned.1.call-start = ((), (), s32[]{:S(2)}) async-start(), calls=%async_computation | async-start | bytes 2359296 | tf_op jit(solution)/shard_map/all_gather | solution.py:1201
  12.9 21.1 %collective-permute-start = (bf16[48,2048]{1,0:T(8,128)(2,1)S(1)}, bf16[48,2048]{1,0:T(8,128)(2,1)S(1)}, u32[]{:S(2)}, u32[]{:S(2)}) collective-permute-start(bf16[48,2048]{1,0:T(8,128)(2,1)S(1)} %get-tuple-element.216.refs_0_), channel_id=1, source_target_pairs={{0,4},{1,5},{2,6},{3,7},{4,0},{5,1},{6,2},{7,3},{8,12},{9,13},{10,... | collective-permute-start | bytes 589832 | tf_op jit(solution)/shard_map/ppermute | solution.py:75
  72.5 36.8 %collective-permute-start.9 = (bf16[2,2,2,48,2048]{4,3,2,1,0:T(8,128)(2,1)}, bf16[2,2,2,48,2048]{4,3,2,1,0:T(8,128)(2,1)}, u32[]{:S(2)}, u32[]{:S(2)}) collective-permute-start(bf16[2,2,2,48,2048]{4,3,2,1,0:T(8,128)(2,1)} %get-tuple-element.227.refs_0_), channel_id=1, source_target_pairs={{0,16},{1,17},{2,18},{3,19},{4,20},{5,21},{6,22},{7,23},{8,24},{9,... | collective-permute-start | bytes 4718600 | tf_op jit(solution)/shard_map/ppermute | solution.py:75
  73.2 34.4 %collective-permute-start.10 = (bf16[2,2,2,48,1920]{4,3,2,1,0:T(8,128)(2,1)S(1)}, bf16[2,2,2,48,1920]{4,3,2,1,0:T(8,128)(2,1)}, u32[]{:S(2)}, u32[]{:S(2)}) collective-permute-start(bf16[2,2,2,48,1920]{4,3,2,1,0:T(8,128)(2,1)S(1)} %get-tuple-element.228.refs_2_), channel_id=1, source_target_pairs={{0,8},{1,9},{2,10},{3,11},{4,12},{5,13},{6,14},{7,15},{8,0},{9,1},... | collective-permute-start | bytes 4423688 | tf_op jit(solution)/shard_map/ppermute | solution.py:75
  74.5 47.5 %collective-permute-start.15 = (bf16[2,144,1792]{2,1,0:T(8,128)(2,1)S(1)}, bf16[2,144,1792]{2,1,0:T(8,128)(2,1)S(1)}, u32[]{:S(2)}, u32[]{:S(2)}) collective-permute-start(bf16[2,144,1792]{2,1,0:T(8,128)(2,1)S(1)} %shard_map.208.refs_4_.refs_0_.refs_2_), channel_id=1, source_target_pairs={{0,4},{1,5},{2,6},{3,7},{4,0},{5,1},{6,2},{7,3},{8,12},{9,13},{10,... | collective-permute-start | bytes 3096584 | tf_op jit(solution)/shard_map/ppermute | solution.py:75
  138.1 206.2 %all-gather.5.cloned.1.call-start = ((), (), s32[]{:S(2)}) async-start(), calls=%async_computation.1 | async-start | bytes 2359296 | tf_op jit(solution)/shard_map/all_gather | solution.py:1201
  138.3 23.9 %collective-permute-start.21 = (bf16[2,144,1792]{2,1,0:T(8,128)(2,1)}, bf16[2,144,1792]{2,1,0:T(8,128)(2,1)S(1)}, u32[]{:S(2)}, u32[]{:S(2)}) collective-permute-start(bf16[2,144,1792]{2,1,0:T(8,128)(2,1)} %copy-done.93), channel_id=1, source_target_pairs={{0,16},{1,17},{2,18},{3,19},{4,20},{5,21},{6,22},{7,23},{8,24},{9,... | collective-permute-start | bytes 3096584 | tf_op jit(solution)/shard_map/ppermute | solution.py:75
  139.8 28.3 %collective-permute-start.20 = (bf16[2,144,1792]{2,1,0:T(8,128)(2,1)}, bf16[2,144,1792]{2,1,0:T(8,128)(2,1)S(1)}, u32[]{:S(2)}, u32[]{:S(2)}) collective-permute-start(bf16[2,144,1792]{2,1,0:T(8,128)(2,1)} %copy-done.49), channel_id=1, source_target_pairs={{0,8},{1,9},{2,10},{3,11},{4,12},{5,13},{6,14},{7,15},{8,0},{9,1},... | collective-permute-start | bytes 3096584 | tf_op jit(solution)/shard_map/ppermute | solution.py:75
  141.3 33.6 %collective-permute-start.16 = (bf16[2,2,2,2,48,512]{5,4,3,2,1,0:T(8,128)(2,1)}, bf16[2,2,2,2,48,512]{5,4,3,2,1,0:T(8,128)(2,1)S(1)}, u32[]{:S(2)}, u32[]{:S(2)}) collective-permute-start(bf16[2,2,2,2,48,512]{5,4,3,2,1,0:T(8,128)(2,1)} %copy-done.99), channel_id=1, source_target_pairs={{0,1},{1,0},{2,3},{3,2},{4,5},{5,4},{6,7},{7,6},{8,9},{9,8},{10,11... | collective-permute-start | bytes 2359304 | tf_op jit(solution)/shard_map/ppermute | solution.py:75
  141.3 31.1 %collective-permute-start.19 = (bf16[2,2,2,2,48,256]{5,4,3,2,1,0:T(8,128)(2,1)}, bf16[2,2,2,2,48,256]{5,4,3,2,1,0:T(8,128)(2,1)S(1)}, u32[]{:S(2)}, u32[]{:S(2)}) collective-permute-start(bf16[2,2,2,2,48,256]{5,4,3,2,1,0:T(8,128)(2,1)} %copy-done.125), channel_id=1, source_target_pairs={{0,1},{1,0},{2,3},{3,2},{4,5},{5,4},{6,7},{7,6},{8,9},{9,8},{10,11... | collective-permute-start | bytes 1179656 | tf_op jit(solution)/shard_map/ppermute | solution.py:75
  141.8 34.3 %collective-permute-start.18 = (bf16[2,2,2,2,48,512]{5,4,3,2,1,0:T(8,128)(2,1)}, bf16[2,2,2,2,48,512]{5,4,3,2,1,0:T(8,128)(2,1)S(1)}, u32[]{:S(2)}, u32[]{:S(2)}) collective-permute-start(bf16[2,2,2,2,48,512]{5,4,3,2,1,0:T(8,128)(2,1)} %copy-done.101), channel_id=1, source_target_pairs={{0,1},{1,0},{2,3},{3,2},{4,5},{5,4},{6,7},{7,6},{8,9},{9,8},{10,11... | collective-permute-start | bytes 2359304 | tf_op jit(solution)/shard_map/ppermute | solution.py:75
  170.9 63.2 %collective-permute-start.26 = (bf16[2,2,144,1792]{3,2,1,0:T(8,128)(2,1)}, bf16[2,2,144,1792]{3,2,1,0:T(8,128)(2,1)S(1)}, u32[]{:S(2)}, u32[]{:S(2)}) collective-permute-start(bf16[2,2,144,1792]{3,2,1,0:T(8,128)(2,1)} %get-tuple-element.255), channel_id=1, source_target_pairs={{0,8},{1,9},{2,10},{3,11},{4,12},{5,13},{6,14},{7,15},{8,0},{9,1},... | collective-permute-start | bytes 6193160 | tf_op jit(solution)/shard_map/ppermute | solution.py:75
  173.1 61.5 %collective-permute-start.25 = (bf16[2,2,144,1792]{3,2,1,0:T(8,128)(2,1)}, bf16[2,2,144,1792]{3,2,1,0:T(8,128)(2,1)}, u32[]{:S(2)}, u32[]{:S(2)}) collective-permute-start(bf16[2,2,144,1792]{3,2,1,0:T(8,128)(2,1)} %get-tuple-element.247.refs_9_), channel_id=1, source_target_pairs={{0,16},{1,17},{2,18},{3,19},{4,20},{5,21},{6,22},{7,23},{8,24},{9,... | collective-permute-start | bytes 6193160 | tf_op jit(solution)/shard_map/ppermute | solution.py:75
  175.7 25.9 %collective-permute-start.27 = (bf16[224,640]{1,0:T(8,128)(2,1)}, bf16[224,640]{1,0:T(8,128)(2,1)}, u32[]{:S(2)}, u32[]{:S(2)}) collective-permute-start(bf16[224,640]{1,0:T(8,128)(2,1)} %get-tuple-element.256.refs_0_), channel_id=1, source_target_pairs={{0,4},{1,5},{2,6},{3,7},{4,0},{5,1},{6,2},{7,3},{8,12},{9,13},{10,... | collective-permute-start | bytes 860168 | tf_op jit(solution)/shard_map/ppermute | solution.py:75
  177.0 24.5 %collective-permute-start.28 = (bf16[224,512]{1,0:T(8,128)(2,1)}, bf16[224,512]{1,0:T(8,128)(2,1)}, u32[]{:S(2)}, u32[]{:S(2)}) collective-permute-start(bf16[224,512]{1,0:T(8,128)(2,1)} %get-tuple-element.257.refs_2_), channel_id=1, source_target_pairs={{0,4},{1,5},{2,6},{3,7},{4,0},{5,1},{6,2},{7,3},{8,12},{9,13},{10,... | collective-permute-start | bytes 688136 | tf_op jit(solution)/shard_map/ppermute | solution.py:75
  202.8 27.9 %collective-permute-start.29 = (bf16[2,224,640]{2,1,0:T(8,128)(2,1)S(1)}, bf16[2,224,640]{2,1,0:T(8,128)(2,1)S(1)}, u32[]{:S(2)}, u32[]{:S(2)}) collective-permute-start(bf16[2,224,640]{2,1,0:T(8,128)(2,1)S(1)} %get-tuple-element.258.refs_0_), channel_id=1, source_target_pairs={{0,8},{1,9},{2,10},{3,11},{4,12},{5,13},{6,14},{7,15},{8,0},{9,1},... | collective-permute-start | bytes 1720328 | tf_op jit(solution)/shard_map/ppermute | solution.py:75
  203.2 27.0 %collective-permute-start.30 = (bf16[2,224,512]{2,1,0:T(8,128)(2,1)S(1)}, bf16[2,224,512]{2,1,0:T(8,128)(2,1)S(1)}, u32[]{:S(2)}, u32[]{:S(2)}) collective-permute-start(bf16[2,224,512]{2,1,0:T(8,128)(2,1)S(1)} %get-tuple-element.259.refs_2_), channel_id=1, source_target_pairs={{0,16},{1,17},{2,18},{3,19},{4,20},{5,21},{6,22},{7,23},{8,24},{9,... | collective-permute-start | bytes 1376264 | tf_op jit(solution)/shard_map/ppermute | solution.py:75
  206.9 27.2 %collective-permute-start.22 = (bf16[256,1152]{1,0:T(8,128)(2,1)S(1)}, bf16[256,1152]{1,0:T(8,128)(2,1)S(1)}, u32[]{:S(2)}, u32[]{:S(2)}) collective-permute-start(bf16[256,1152]{1,0:T(8,128)(2,1)S(1)} %get-tuple-element.254.refs_4_.refs_0_.refs_1_), channel_id=1, source_target_pairs={{0,2},{1,3},{2,0},{3,1},{4,6},{5,7},{6,4},{7,5},{8,10},{9,11},{10,... | collective-permute-start | bytes 1769480 | tf_op jit(solution)/shard_map/ppermute | solution.py:75
  230.9 27.0 %collective-permute-start.31 = (bf16[2,2,224,640]{3,2,1,0:T(8,128)(2,1)S(1)}, bf16[2,2,224,640]{3,2,1,0:T(8,128)(2,1)}, u32[]{:S(2)}, u32[]{:S(2)}) collective-permute-start(bf16[2,2,224,640]{3,2,1,0:T(8,128)(2,1)S(1)} %get-tuple-element.260), channel_id=1, source_target_pairs={{0,16},{1,17},{2,18},{3,19},{4,20},{5,21},{6,22},{7,23},{8,24},{9,... | collective-permute-start | bytes 3440648 | tf_op jit(solution)/shard_map/ppermute | solution.py:75
  232.4 21.9 %collective-permute-start.32 = (bf16[2,2,224,512]{3,2,1,0:T(8,128)(2,1)S(1)}, bf16[2,2,224,512]{3,2,1,0:T(8,128)(2,1)}, u32[]{:S(2)}, u32[]{:S(2)}) collective-permute-start(bf16[2,2,224,512]{3,2,1,0:T(8,128)(2,1)S(1)} %get-tuple-element.261), channel_id=1, source_target_pairs={{0,8},{1,9},{2,10},{3,11},{4,12},{5,13},{6,14},{7,15},{8,0},{9,1},... | collective-permute-start | bytes 2752520 | tf_op jit(solution)/shard_map/ppermute | solution.py:75
  234.1 27.9 %collective-permute-start.23 = (bf16[256,1152]{1,0:T(8,128)(2,1)S(1)}, bf16[256,1152]{1,0:T(8,128)(2,1)S(1)}, u32[]{:S(2)}, u32[]{:S(2)}) collective-permute-start(bf16[256,1152]{1,0:T(8,128)(2,1)S(1)} %get-tuple-element.254.refs_4_.refs_0_.refs_1_), channel_id=1, source_target_pairs={{0,1},{1,0},{2,3},{3,2},{4,5},{5,4},{6,7},{7,6},{8,9},{9,8},{10,11... | collective-permute-start | bytes 1769480 | tf_op jit(solution)/shard_map/ppermute | solution.py:75
  234.1 27.8 %collective-permute-start.24 = (bf16[256,1152]{1,0:T(8,128)(2,1)S(1)}, bf16[256,1152]{1,0:T(8,128)(2,1)S(1)}, u32[]{:S(2)}, u32[]{:S(2)}) collective-permute-start(bf16[256,1152]{1,0:T(8,128)(2,1)S(1)} %collective-permute-done.22.refs_1_.refs_2_), channel_id=1, source_target_pairs={{0,1},{1,0},{2,3},{3,2},{4,5},{5,4},{6,7},{7,6},{8,9},{9,8},{10,11... | collective-permute-start | bytes 1769480 | tf_op jit(solution)/shard_map/ppermute | solution.py:75
  234.6 52.1 %collective-permute-start.37 = (bf16[256,1152]{1,0:T(8,128)(2,1)S(1)}, bf16[256,1152]{1,0:T(8,128)(2,1)S(1)}, u32[]{:S(2)}, u32[]{:S(2)}) collective-permute-start(bf16[256,1152]{1,0:T(8,128)(2,1)S(1)} %copy-done.75), channel_id=1, source_target_pairs={{0,2},{1,3},{2,0},{3,1},{4,6},{5,7},{6,4},{7,5},{8,10},{9,11},{10,... | collective-permute-start | bytes 1769480 | tf_op jit(solution)/shard_map/ppermute | solution.py:75
  407.8 34.7 %collective-permute-start.46 = (bf16[256,1152]{1,0:T(8,128)(2,1)}, bf16[256,1152]{1,0:T(8,128)(2,1)S(1)}, u32[]{:S(2)}, u32[]{:S(2)}) collective-permute-start(bf16[256,1152]{1,0:T(8,128)(2,1)} %copy-done.149), channel_id=1, source_target_pairs={{0,2},{1,3},{2,0},{3,1},{4,6},{5,7},{6,4},{7,5},{8,10},{9,11},{10,... | collective-permute-start | bytes 1769480 | tf_op jit(solution)/shard_map/ppermute | solution.py:75
  477.1 25.3 %collective-permute-start.61 = (bf16[256,1664]{1,0:T(8,128)(2,1)S(1)}, bf16[256,1664]{1,0:T(8,128)(2,1)S(1)}, u32[]{:S(2)}, u32[]{:S(2)}) collective-permute-start(bf16[256,1664]{1,0:T(8,128)(2,1)S(1)} %copy-done.97), channel_id=1, source_target_pairs={{0,1},{1,0},{2,3},{3,2},{4,5},{5,4},{6,7},{7,6},{8,9},{9,8},{10,11... | collective-permute-start | bytes 2555912 | tf_op jit(solution)/shard_map/ppermute | solution.py:75
  480.6 19.3 %collective-permute-start.58 = (bf16[256,1024]{1,0:T(8,128)(2,1)S(1)}, bf16[256,1024]{1,0:T(8,128)(2,1)S(1)}, u32[]{:S(2)}, u32[]{:S(2)}) collective-permute-start(bf16[256,1024]{1,0:T(8,128)(2,1)S(1)} %get-tuple-element.310.refs_2_.gq_ref), channel_id=1, source_target_pairs={{0,1},{1,0},{2,3},{3,2},{4,5},{5,4},{6,7},{7,6},{8,9},{9,8},{10,11... | collective-permute-start | bytes 1572872 | tf_op jit(solution)/shard_map/ppermute | solution.py:75
  567.5 33.1 %collective-permute-start.70 = (bf16[2,2,224,640]{3,2,1,0:T(8,128)(2,1)}, bf16[2,2,224,640]{3,2,1,0:T(8,128)(2,1)}, u32[]{:S(2)}, u32[]{:S(2)}) collective-permute-start(bf16[2,2,224,640]{3,2,1,0:T(8,128)(2,1)} %get-tuple-element.340), channel_id=1, source_target_pairs={{0,8},{1,9},{2,10},{3,11},{4,12},{5,13},{6,14},{7,15},{8,0},{9,1},... | collective-permute-start | bytes 3440648 | tf_op jit(solution)/shard_map/ppermute | solution.py:75
  569.0 31.6 %collective-permute-start.71 = (bf16[2,2,224,512]{3,2,1,0:T(8,128)(2,1)}, bf16[2,2,224,512]{3,2,1,0:T(8,128)(2,1)S(1)}, u32[]{:S(2)}, u32[]{:S(2)}) collective-permute-start(bf16[2,2,224,512]{3,2,1,0:T(8,128)(2,1)} %get-tuple-element.342), channel_id=1, source_target_pairs={{0,16},{1,17},{2,18},{3,19},{4,20},{5,21},{6,22},{7,23},{8,24},{9,... | collective-permute-start | bytes 2752520 | tf_op jit(solution)/shard_map/ppermute | solution.py:75
  592.8 59.5 %collective-permute-start.75 = (bf16[2,2,144,1792]{3,2,1,0:T(8,128)(2,1)}, bf16[2,2,144,1792]{3,2,1,0:T(8,128)(2,1)}, u32[]{:S(2)}, u32[]{:S(2)}) collective-permute-start(bf16[2,2,144,1792]{3,2,1,0:T(8,128)(2,1)} %get-tuple-element.351), channel_id=1, source_target_pairs={{0,8},{1,9},{2,10},{3,11},{4,12},{5,13},{6,14},{7,15},{8,0},{9,1},... | collective-permute-start | bytes 6193160 | tf_op jit(solution)/shard_map/ppermute | solution.py:75
  593.4 58.9 %collective-permute-start.76 = (bf16[2,2,144,1792]{3,2,1,0:T(8,128)(2,1)}, bf16[2,2,144,1792]{3,2,1,0:T(8,128)(2,1)}, u32[]{:S(2)}, u32[]{:S(2)}) collective-permute-start(bf16[2,2,144,1792]{3,2,1,0:T(8,128)(2,1)} %get-tuple-element.353), channel_id=1, source_target_pairs={{0,16},{1,17},{2,18},{3,19},{4,20},{5,21},{6,22},{7,23},{8,24},{9,... | collective-permute-start | bytes 6193160 | tf_op jit(solution)/shard_map/ppermute | solution.py:75
  622.1 30.2 %collective-permute-start.77 = (bf16[2,224,640]{2,1,0:T(8,128)(2,1)}, bf16[2,224,640]{2,1,0:T(8,128)(2,1)S(1)}, u32[]{:S(2)}, u32[]{:S(2)}) collective-permute-start(bf16[2,224,640]{2,1,0:T(8,128)(2,1)} %get-tuple-element.354), channel_id=1, source_target_pairs={{0,16},{1,17},{2,18},{3,19},{4,20},{5,21},{6,22},{7,23},{8,24},{9,... | collective-permute-start | bytes 1720328 | tf_op jit(solution)/shard_map/ppermute | solution.py:75
  633.5 29.8 %collective-permute-start.74 = (bf16[256,512]{1,0:T(8,128)(2,1)S(1)}, bf16[256,512]{1,0:T(8,128)(2,1)S(1)}, u32[]{:S(2)}, u32[]{:S(2)}) collective-permute-start(bf16[256,512]{1,0:T(8,128)(2,1)S(1)} %get-tuple-element.349), channel_id=1, source_target_pairs={{0,4},{1,5},{2,6},{3,7},{4,0},{5,1},{6,2},{7,3},{8,12},{9,13},{10,... | collective-permute-start | bytes 786440 | tf_op jit(solution)/shard_map/ppermute | solution.py:75
  650.8 63.7 %collective-permute-start.84 = (bf16[2,2,2,48,1664]{4,3,2,1,0:T(8,128)(2,1)}, bf16[2,2,2,48,1664]{4,3,2,1,0:T(8,128)(2,1)}, u32[]{:S(2)}, u32[]{:S(2)}) collective-permute-start(bf16[2,2,2,48,1664]{4,3,2,1,0:T(8,128)(2,1)} %get-tuple-element.372), channel_id=1, source_target_pairs={{0,8},{1,9},{2,10},{3,11},{4,12},{5,13},{6,14},{7,15},{8,0},{9,1},... | collective-permute-start | bytes 3833864 | tf_op jit(solution)/shard_map/ppermute | solution.py:75
  662.8 51.8 %collective-permute-start.85 = (bf16[2,2,2,56,1280]{4,3,2,1,0:T(8,128)(2,1)}, bf16[2,2,2,56,1280]{4,3,2,1,0:T(8,128)(2,1)S(1)}, u32[]{:S(2)}, u32[]{:S(2)}) collective-permute-start(bf16[2,2,2,56,1280]{4,3,2,1,0:T(8,128)(2,1)} %copy-done.146), channel_id=1, source_target_pairs={{0,16},{1,17},{2,18},{3,19},{4,20},{5,21},{6,22},{7,23},{8,24},{9,... | collective-permute-start | bytes 3440648 | tf_op jit(solution)/shard_map/ppermute | solution.py:75
  672.8 37.8 %collective-permute-start.86 = (bf16[2,144,1792]{2,1,0:T(8,128)(2,1)S(1)}, bf16[2,144,1792]{2,1,0:T(8,128)(2,1)S(1)}, u32[]{:S(2)}, u32[]{:S(2)}) collective-permute-start(bf16[2,144,1792]{2,1,0:T(8,128)(2,1)S(1)} %copy-done.148), channel_id=1, source_target_pairs={{0,16},{1,17},{2,18},{3,19},{4,20},{5,21},{6,22},{7,23},{8,24},{9,... | collective-permute-start | bytes 3096584 | tf_op jit(solution)/shard_map/ppermute | solution.py:75
  674.1 36.5 %collective-permute-start.87 = (bf16[2,144,1792]{2,1,0:T(8,128)(2,1)}, bf16[2,144,1792]{2,1,0:T(8,128)(2,1)S(1)}, u32[]{:S(2)}, u32[]{:S(2)}) collective-permute-start(bf16[2,144,1792]{2,1,0:T(8,128)(2,1)} %get-tuple-element.377), channel_id=1, source_target_pairs={{0,8},{1,9},{2,10},{3,11},{4,12},{5,13},{6,14},{7,15},{8,0},{9,1},... | collective-permute-start | bytes 3096584 | tf_op jit(solution)/shard_map/ppermute | solution.py:75
  691.5 30.3 %collective-permute-start.95 = (bf16[2,2,2,56,768]{4,3,2,1,0:T(8,128)(2,1)}, bf16[2,2,2,56,768]{4,3,2,1,0:T(8,128)(2,1)S(1)}, u32[]{:S(2)}, u32[]{:S(2)}) collective-permute-start(bf16[2,2,2,56,768]{4,3,2,1,0:T(8,128)(2,1)} %get-tuple-element.392), channel_id=1, source_target_pairs={{0,8},{1,9},{2,10},{3,11},{4,12},{5,13},{6,14},{7,15},{8,0},{9,1},... | collective-permute-start | bytes 2064392 | tf_op jit(solution)/shard_map/ppermute | solution.py:75
  716.8 47.9 %collective-permute-start.93 = (bf16[2,2,48,1664]{3,2,1,0:T(8,128)(2,1)S(1)}, bf16[2,2,48,1664]{3,2,1,0:T(8,128)(2,1)S(1)}, u32[]{:S(2)}, u32[]{:S(2)}) collective-permute-start(bf16[2,2,48,1664]{3,2,1,0:T(8,128)(2,1)S(1)} %get-tuple-element.389), channel_id=1, source_target_pairs={{0,16},{1,17},{2,18},{3,19},{4,20},{5,21},{6,22},{7,23},{8,24},{9,... | collective-permute-start | bytes 1916936 | tf_op jit(solution)/shard_map/ppermute | solution.py:75
  717.4 47.3 %collective-permute-start.94 = (bf16[2,2,56,1280]{3,2,1,0:T(8,128)(2,1)S(1)}, bf16[2,2,56,1280]{3,2,1,0:T(8,128)(2,1)S(1)}, u32[]{:S(2)}, u32[]{:S(2)}) collective-permute-start(bf16[2,2,56,1280]{3,2,1,0:T(8,128)(2,1)S(1)} %get-tuple-element.391), channel_id=1, source_target_pairs={{0,8},{1,9},{2,10},{3,11},{4,12},{5,13},{6,14},{7,15},{8,0},{9,1},... | collective-permute-start | bytes 1720328 | tf_op jit(solution)/shard_map/ppermute | solution.py:75
  718.9 33.6 %collective-permute-start.97 = (bf16[144,1792]{1,0:T(8,128)(2,1)S(1)}, bf16[144,1792]{1,0:T(8,128)(2,1)S(1)}, u32[]{:S(2)}, u32[]{:S(2)}) collective-permute-start(bf16[144,1792]{1,0:T(8,128)(2,1)S(1)} %get-tuple-element.395), channel_id=1, source_target_pairs={{0,4},{1,5},{2,6},{3,7},{4,0},{5,1},{6,2},{7,3},{8,12},{9,13},{10,... | collective-permute-start | bytes 1548296 | tf_op jit(solution)/shard_map/ppermute | solution.py:75
  719.7 43.8 %collective-permute-start.98 = (bf16[144,1792]{1,0:T(8,128)(2,1)S(1)}, bf16[144,1792]{1,0:T(8,128)(2,1)S(1)}, u32[]{:S(2)}, u32[]{:S(2)}) collective-permute-start(bf16[144,1792]{1,0:T(8,128)(2,1)S(1)} %get-tuple-element.397), channel_id=1, source_target_pairs={{0,4},{1,5},{2,6},{3,7},{4,0},{5,1},{6,2},{7,3},{8,12},{9,13},{10,... | collective-permute-start | bytes 1548296 | tf_op jit(solution)/shard_map/ppermute | solution.py:75
  722.5 42.1 %collective-permute-start.96 = (bf16[2,2,56,768]{3,2,1,0:T(8,128)(2,1)S(1)}, bf16[2,2,56,768]{3,2,1,0:T(8,128)(2,1)S(1)}, u32[]{:S(2)}, u32[]{:S(2)}) collective-permute-start(bf16[2,2,56,768]{3,2,1,0:T(8,128)(2,1)S(1)} %get-tuple-element.394), channel_id=1, source_target_pairs={{0,16},{1,17},{2,18},{3,19},{4,20},{5,21},{6,22},{7,23},{8,24},{9,... | collective-permute-start | bytes 1032200 | tf_op jit(solution)/shard_map/ppermute | solution.py:75
  765.6 20.3 %collective-permute-start.99 = (bf16[2,48,1664]{2,1,0:T(8,128)(2,1)S(1)}, bf16[2,48,1664]{2,1,0:T(8,128)(2,1)S(1)}, u32[]{:S(2)}, u32[]{:S(2)}) collective-permute-start(bf16[2,48,1664]{2,1,0:T(8,128)(2,1)S(1)} %get-tuple-element.400), channel_id=1, source_target_pairs={{0,2},{1,3},{2,0},{3,1},{4,6},{5,7},{6,4},{7,5},{8,10},{9,11},{10,... | collective-permute-start | bytes 958472 | tf_op jit(solution)/shard_map/ppermute | solution.py:75
  765.7 20.2 %collective-permute-start.100 = (bf16[2,56,1280]{2,1,0:T(8,128)(2,1)S(1)}, bf16[2,56,1280]{2,1,0:T(8,128)(2,1)S(1)}, u32[]{:S(2)}, u32[]{:S(2)}) collective-permute-start(bf16[2,56,1280]{2,1,0:T(8,128)(2,1)S(1)} %get-tuple-element.402), channel_id=1, source_target_pairs={{0,2},{1,3},{2,0},{3,1},{4,6},{5,7},{6,4},{7,5},{8,10},{9,11},{10,... | collective-permute-start | bytes 860168 | tf_op jit(solution)/shard_map/ppermute | solution.py:75
  767.8 21.9 %collective-permute-start.105 = (bf16[2,36,1792]{2,1,0:T(8,128)(2,1)S(1)}, bf16[2,36,1792]{2,1,0:T(8,128)(2,1)S(1)}, u32[]{:S(2)}, u32[]{:S(2)}) collective-permute-start(bf16[2,36,1792]{2,1,0:T(8,128)(2,1)S(1)} %get-tuple-element.414), channel_id=1, source_target_pairs={{0,1},{1,0},{2,3},{3,2},{4,5},{5,4},{6,7},{7,6},{8,9},{9,8},{10,11... | collective-permute-start | bytes 774152 | tf_op jit(solution)/shard_map/ppermute | solution.py:75
  767.8 31.4 %collective-permute-start.106 = (bf16[2,36,1792]{2,1,0:T(8,128)(2,1)S(1)}, bf16[2,36,1792]{2,1,0:T(8,128)(2,1)S(1)}, u32[]{:S(2)}, u32[]{:S(2)}) collective-permute-start(bf16[2,36,1792]{2,1,0:T(8,128)(2,1)S(1)} %get-tuple-element.415), channel_id=1, source_target_pairs={{0,2},{1,3},{2,0},{3,1},{4,6},{5,7},{6,4},{7,5},{8,10},{9,11},{10,... | collective-permute-start | bytes 774152 | tf_op jit(solution)/shard_map/ppermute | solution.py:75
  786.6 20.4 %collective-permute-start.102 = (bf16[48,1664]{1,0:T(8,128)(2,1)S(1)}, bf16[48,1664]{1,0:T(8,128)(2,1)S(1)}, u32[]{:S(2)}, u32[]{:S(2)}) collective-permute-start(bf16[48,1664]{1,0:T(8,128)(2,1)S(1)} %get-tuple-element.406), channel_id=1, source_target_pairs={{0,4},{1,5},{2,6},{3,7},{4,0},{5,1},{6,2},{7,3},{8,12},{9,13},{10,... | collective-permute-start | bytes 479240 | tf_op jit(solution)/shard_map/ppermute | solution.py:75
  787.1 19.9 %collective-permute-start.103 = (bf16[56,1280]{1,0:T(8,128)(2,1)S(1)}, bf16[56,1280]{1,0:T(8,128)(2,1)S(1)}, u32[]{:S(2)}, u32[]{:S(2)}) collective-permute-start(bf16[56,1280]{1,0:T(8,128)(2,1)S(1)} %get-tuple-element.408), channel_id=1, source_target_pairs={{0,4},{1,5},{2,6},{3,7},{4,0},{5,1},{6,2},{7,3},{8,12},{9,13},{10,... | collective-permute-start | bytes 430088 | tf_op jit(solution)/shard_map/ppermute | solution.py:75
  (216 other events, 1909.5 us)
Sparse Core Ops, SparseCore 0:
  138.2 30.1 all-gather.2
  312.9 31.2 all-gather.4

commit v4 on v3

--- a/solution.py
+++ b/solution.py
@@ -97,8 +97,10 @@
                             out.append((y, x, p, h, c))
         return tuple(out)
 
-    def tokens_in(self, rows):
+    def tokens_in(self, rows, ties=()):
         other = self.permute(rows, {"h": 1})
+        if ties:
+            (other,) = stack([([other], None, None)], ties)
         return [rows, other, self.permute(rows, {"c": 1}), self.permute(other, {"c": 1})]
 
     def extent(self, names):
@@ -118,6 +120,14 @@
     return min(rows, 256)
 
 
+COST_FORWARD = 6
+COST_BACKWARD = 0
+COST_WEIGHTS = 4
+COST_ATTEND = 4
+COST_ATTEND_BACK = 10
+COST_OUTER = 0
+COST_LEAVE = 2
+COST_ENTER = 2
 LIGHT = pl.CostEstimate(flops=0, bytes_accessed=0, transcendentals=0)
 
 
@@ -138,7 +148,7 @@
     return run
 
 
-def kernel_call(body, grid, in_specs, out_specs, out_shape, scratch, ties=()):
+def kernel_call(body, grid, in_specs, out_specs, out_shape, scratch, ties=(), flops=0):
     return pl.pallas_call(
         tied(body, len(in_specs), ties),
         grid=grid,
@@ -146,14 +156,14 @@
         out_specs=out_specs,
         out_shape=out_shape,
         scratch_shapes=scratch,
-        cost_estimate=LIGHT,
+        cost_estimate=pl.CostEstimate(flops=flops, bytes_accessed=0, transcendentals=0),
         compiler_params=pltpu.CompilerParams(
             dimension_semantics=("arbitrary",), vmem_limit_bytes=48 * 1024 * 1024
         ),
     )
 
 
-def whole_call(body, out_shape, coordinates, operands, ties=(), scratch=()):
+def whole_call(body, out_shape, coordinates, operands, ties=(), scratch=(), flops=0):
     count = len(operands)
     specs = [pl.BlockSpec(memory_space=pltpu.VMEM)] * count
     if coordinates is not None:
@@ -164,7 +174,7 @@
         out_shape=out_shape,
         in_specs=specs + [ANY] * len(ties),
         scratch_shapes=list(scratch),
-        cost_estimate=LIGHT,
+        cost_estimate=pl.CostEstimate(flops=flops, bytes_accessed=0, transcendentals=0),
         compiler_params=pltpu.CompilerParams(vmem_limit_bytes=48 * 1024 * 1024),
     )(*operands, *ties)
 
@@ -247,6 +257,7 @@
         + sent_chunks(rows, width)[1],
         [pltpu.VMEM((rows // 2, width), F32)],
         ties,
+        int(COST_FORWARD * rows * width * wide),
     )(*blocks, w_gate, w_up, w_down, *ties)
 
 
@@ -335,6 +346,7 @@
             pltpu.VMEM((rows, width), BF),
         ],
         ties,
+        int(COST_BACKWARD * rows * width * wide),
     )(*operands, *ties)
 
 
@@ -414,6 +426,7 @@
         outs,
         scratch,
         ties,
+        int(COST_WEIGHTS * rows * width * wide),
     )(*operands, *ties)
 
 
@@ -800,13 +813,9 @@
         ]
 
 
-def halves_body(w_ref, left_ref, right_ref):
-    rows = w_ref.shape[0]
-    left = left_ref.shape[1]
-    for ref in (left_ref, right_ref):
-        ref[...] = jnp.zeros_like(ref)
-    left_ref[:rows] = w_ref[:, :left]
-    right_ref[:rows] = w_ref[:, left:]
+def rows_body(w_ref, out_ref):
+    out_ref[...] = jnp.zeros_like(out_ref)
+    out_ref[: w_ref.shape[0]] = w_ref[...]
 
 
 def project_kv_body(first_loop, addends, *refs):
@@ -843,7 +852,14 @@
     return jnp.where(allowed, 0.0, NEG)
 
 
-def attend_body(q_ref, kv_ref, segs_ref, places_ref, row_ref, mixed_ref, log_ref):
+def attend_body(entries, coords_ref, q_ref, segs_ref, places_ref, row_ref, *refs):
+    mixed_ref, log_ref, kv_ref = refs[-3:]
+    for (p_mask, h_mask, c_mask), number, index in entries:
+        value = refs[number][...] if index is None else refs[number][index]
+        size = value.shape[0]
+        block = (coords_ref[2] ^ p_mask) * 4 + (coords_ref[3] ^ h_mask) * 2
+        block = block + (coords_ref[4] ^ c_mask)
+        kv_ref[pl.ds(pl.multiple_of(block * size, size), size), :] = value
     mask = mask_of(segs_ref, places_ref, row_ref)
     for head in range(H):
         at = slice(head * HD, (head + 1) * HD)
@@ -1046,6 +1062,7 @@
         None,
         [*left, *[value for right in rights for value in right], *olds],
         ties,
+        flops=int(COST_OUTER * rows * columns.stop * sum(value[0].shape[1] for value in rights)),
     )
 
 
@@ -1125,15 +1142,11 @@
         [first],
         [pltpu.VMEM((4, 2, qkv_rows, wide), BF)],
     )
-    down_left, down_right = whole_call(
-        halves_body,
-        [shape(block_up, left_cols), shape(block_up, width - left_cols)],
-        None,
-        [down_weight],
-        [cut[0]],
+    down = whole_call(
+        rows_body, shape(block_up, width), None, [down_weight], [cut[0]]
     )
     first, second = stack(
-        [(parts(first, "h"), None, None), (parts(second, "h"), None, None)], [down_left]
+        [(parts(first, "h"), None, None), (parts(second, "h"), None, None)], [down]
     )
     gate_up = whole_call(
         pieces_body,
@@ -1162,17 +1175,16 @@
     chunks = [flat(parts(chunk, "c")) for chunk in chunks]
     first = [part for chunk in chunks[:4] for part in chunk]
     second = [part for chunk in chunks[4:] for part in chunk]
-    gate, up, down_left, down_right = stack(
+    gate, up, down = stack(
         [
             (gate_up, 0, None),
             (gate_up, 1, None),
-            ([down_left], None, None),
-            ([down_right], None, None),
+            ([down], None, None),
         ],
         [chunks[0][0]],
     )
     gate, up = parts(gate, "x"), parts(up, "y")
-    down_left, down_right = parts(down_left, "p"), parts(down_right, "p")
+    down = parts(down, "p")
     w_qkv, ql_0, qd, gains = whole_call(
         functools.partial(
             unpack_first_body,
@@ -1198,8 +1210,30 @@
             None,
             [*addends, gains, qd, w_qkv, lifts_in[loop], *tables],
         )
-        both = lax.all_gather(own_kv, "blk", axis=0, tiled=True)
-        return own_kv, normed_b, low_rank_b, residual, both
+        return own_kv, normed_b, low_rank_b, residual
+
+    def gather_kv(own_kv):
+        chips = {(0, 0): own_kv}
+        for p_mask in range(grid.sizes["p"]):
+            for h_mask in range(2):
+                if p_mask or h_mask:
+                    chips[p_mask, h_mask] = grid.permute(own_kv, {"p": p_mask, "h": h_mask})
+        kv_parts = {(*mask, 0): value for mask, value in chips.items()}
+        for mask, value in chips.items():
+            kv_parts[(*mask, 1)] = grid.permute(value, {"c": 1})
+        entries = [(mask, number, None) for number, mask in enumerate(kv_parts)]
+        return entries, list(kv_parts.values())
+
+    def gather_kv_staged(own_kv, ties):
+        (near,) = stack([(parts(own_kv, "p"), None, None)], ties)
+        far = grid.permute(near, {"h": 1})
+        entries = [
+            ((p_mask, h_mask, c_mask), 2 * c_mask + h_mask, p_mask)
+            for c_mask in range(2)
+            for h_mask in range(2)
+            for p_mask in range(grid.sizes["p"])
+        ]
+        return entries, [near, far, grid.permute(near, {"c": 1}), grid.permute(far, {"c": 1})]
 
     def project_q(projected, loop, ties=()):
         return whole_call(
@@ -1210,18 +1244,25 @@
             ties,
         )
 
-    def attend(queries, both, ties=()):
+    def attend(queries, gathered, ties=()):
+        entries, operands = gathered
         return whole_call(
-            attend_body,
-            [shape(tokens, width_q), jax.ShapeDtypeStruct((H, tokens, 1), F32)],
-            None,
-            [queries, both, *masks],
+            functools.partial(attend_body, entries),
+            [
+                shape(tokens, width_q),
+                jax.ShapeDtypeStruct((H, tokens, 1), F32),
+                shape(seq_len, 2 * HD),
+            ],
+            coordinates,
+            [queries, *masks, *operands],
             ties,
+            flops=int(COST_ATTEND * tokens * width_q * seq_len),
         )
 
     projected_one = project_kv([inputs], 0)
-    queries_one = project_q(projected_one, 0)
-    gate, up = stack([(gate, None, None), (up, None, None)], [queries_one])
+    gate, up, own_kv = stack(
+        [(gate, None, None), (up, None, None), ([projected_one[0]], None, None)]
+    )
     gate, up = parts(gate, "y"), parts(up, "x")
     w_out, ol_0, ol_1, od, ql_1 = whole_call(
         functools.partial(
@@ -1239,11 +1280,14 @@
         second,
         [gate[0]],
     )
-    attended_one = attend(queries_one, projected_one[4], [w_out])
+    queries_one = project_q(projected_one, 0, [gate[0]])
+    down_left, down_right = stack([(down, None, [left_cols, width - left_cols])], [queries_one])
+    down_left, down_right = parts(down_left, "x"), parts(down_right, "y")
+    attended_one = attend(queries_one, gather_kv_staged(own_kv, [down_left[0]]))
     down_left, down_right = stack(
         [(down_left, None, None), (down_right, None, None)], [attended_one[0]]
     )
-    down_left, down_right = parts(down_left, "x"), parts(down_right, "y")
+    down_left, down_right = parts(down_left, "y"), parts(down_right, "x")
     lifts_in[1] = ql_1
     lifts_out = (ol_0, ol_1)
 
@@ -1253,14 +1297,10 @@
             [shape(tokens, rank), shape(tokens, width, F32), shape(tokens, width)],
             None,
             [mixed_b, od, w_out, lifts_out[loop], residual, gains],
+            flops=int(COST_LEAVE * tokens * width_q * width),
         )
 
     left_one = leave(0, attended_one[0], projected_one[3])
-    ff_in_one = grid.tokens_in(left_one[2])
-    down_left, down_right = stack(
-        [(down_left, None, None), (down_right, None, None)], [left_one[2]]
-    )
-    down_left, down_right = parts(down_left, "y"), parts(down_right, "x")
     w_gate = in_order(grid, coordinates, (gate, ("p", "x", "y")))
     w_up = in_order(grid, coordinates, (up, ("p", "y", "x")))
     w_down = in_order(
@@ -1272,10 +1312,10 @@
 
     cotangent_in = grid.tokens_in(cotangent)
 
-    def feed_forward(loop, projected, queries, attended, left, ff_in, ties=()):
-        own_kv, normed_b, low_rank_b, residual, both = projected
-        mixed_b, log_total = attended
-        side_b, middle, unused = left
+    def feed_forward(loop, projected, queries, attended, left, ties=()):
+        own_kv, normed_b, low_rank_b, residual = projected
+        mixed_b, log_total, both = attended
+        side_b, middle, normed_ff_b = left
         spread_own, spread_sent = whole_call(
             functools.partial(
                 spread_body,
@@ -1290,9 +1330,8 @@
             (),
             [pltpu.VMEM((2, tokens, grid.devices // 2 * (qkv_block + out_block)), BF)],
         )
-        ff_own, gate_b, up_b, *ff_sent = ff_forward(
-            ff_in, w_gate, w_up, w_down, [spread_sent]
-        )
+        ff_in = grid.tokens_in(normed_ff_b, [spread_sent])
+        ff_own, gate_b, up_b, *ff_sent = ff_forward(ff_in, w_gate, w_up, w_down)
         own, other = tokens_out(grid, ff_own, ff_sent, ties)
         cache = (
             residual, (spread_own, grid.permute(spread_sent, {"c": 1})), queries, both, log_total,
@@ -1301,14 +1340,14 @@
         return [middle, own, other], cache
 
     addends, cache_one = feed_forward(
-        0, projected_one, queries_one, attended_one, left_one, ff_in_one, [cotangent_in[1]]
+        0, projected_one, queries_one, attended_one, left_one, [cotangent_in[1]]
     )
     projected_two = project_kv(addends, 1)
     queries_two = project_q(projected_two, 1)
-    attended_two = attend(queries_two, projected_two[4])
+    attended_two = attend(queries_two, gather_kv(projected_two[0]))
     left_two = leave(1, attended_two[0], projected_two[3])
     addends, cache_two = feed_forward(
-        1, projected_two, queries_two, attended_two, left_two, grid.tokens_in(left_two[2])
+        1, projected_two, queries_two, attended_two, left_two
     )
     result = whole_call(result_body, shape(tokens, width), None, addends)
 
@@ -1385,6 +1424,7 @@
             None,
             [own, other, grad_result, middle, gains, w_out, ol, od],
             ties,
+            flops=int(COST_ENTER * tokens * width_q * width),
         )
         ties = []
         if last:
@@ -1403,7 +1443,11 @@
             + [pl.BlockSpec(memory_space=pltpu.SMEM)]
             + [ANY] * len(ties),
             scratch_shapes=[pltpu.VMEM((seq_len, HD), F32)] * 2,
-            cost_estimate=LIGHT,
+            cost_estimate=pl.CostEstimate(
+                flops=int(COST_ATTEND_BACK * tokens * width_q * seq_len),
+                bytes_accessed=0,
+                transcendentals=0,
+            ),
             compiler_params=pltpu.CompilerParams(vmem_limit_bytes=48 * 1024 * 1024),
         )(queries, both, *masks, log_total, grad_mixed_b, *tables, coordinates, *ties)
         grad_kv = (("p", "h"), [kv_own, grid.permute(kv_sent, {"c": 1})])
@@ -1421,6 +1465,20 @@
             [d_out],
         )
         sums = {"out": d_out, "od": d_od, "queries": d_queries}
+
+        def second_sums(ties):
+            sums["gate"], sums["up"], down[0], down[1] = fold(
+                grid,
+                coordinates,
+                [
+                    (d_gate[0], "y", [d_gate[1]]),
+                    (d_up[0], d_up[0][0], [d_up[1]]),
+                    (down[0][0], "p", [down[0][1]]),
+                    (down[1][0], "p", [down[1][1]]),
+                ],
+                ties,
+            )
+
         ties = [] if last else [d_queries, cache_one[1][1]]
         if last:
             sums["out"], sums["queries"] = fold(
@@ -1431,17 +1489,7 @@
                     (names, "y", [[blocks(value)] for value in (d_queries, old["qd"])]),
                 ],
             )
-            sums["gate"], sums["up"], down[0], down[1] = fold(
-                grid,
-                coordinates,
-                [
-                    (d_gate[0], "y", [d_gate[1]]),
-                    (d_up[0], d_up[0][0], [d_up[1]]),
-                    (down[0][0], "p", [down[0][1]]),
-                    (down[1][0], "p", [down[1][1]]),
-                ],
-                [sums["out"][1][0]],
-            )
+            second_sums([sums["out"][1][0]])
             ties = [sums["gate"][1][0]]
         else:
             sums["gate"], sums["up"] = d_gate, d_up
@@ -1517,7 +1565,6 @@
         shape(qkv_rows, 8 * groups * hidden_block, F32),
         coordinates,
         back,
-        [late[1][0]],
     )
     last = [outs[1], queries[1], late[1]]
     d_gains, d_qkv, d_out, d_qd, d_ql, d_od, d_ol = whole_call(

time: 823 us -> 800 us (0.972)
  local copies, waits for them, and re-layouts: 74.1 us -> 49.7 us
  between operations: 15.6 us -> 2.36 us
  Pallas kernels: 291 us -> 301 us
    ppermute x108 -> x118, waiting for transfers between devices: 325 us -> 354 us  [permute(): return lax.ppermute(values, AXES, pairs)]
    unnamed x310 -> x242, local copies, waits for them, and re-layouts: 73.8 us -> 48.8 us
    all_gather x2 -> x0, waiting for transfers between devices: 24.7 us -> none  [project_kv(): both = lax.all_gather(own_kv, 'blk', axis=0, tiled=True)]
    pallas_call x63 -> x66, Pallas kernels: 134 us -> 143 us  [whole_call(): pl.pallas_call(tied(body, len(specs), ties), out_shape=out_shape, in_spec...]
    ppermute x108 -> x118, starting transfers between devices: 81.7 us -> 79.9 us  [permute(): return lax.ppermute(values, AXES, pairs)]
  transfers between devices with their start and end apart: 110 -> 118, of which waited for: 51 -> 57; matrix products, arithmetic and copies ran while one was open for 0% -> 0% of each run, Pallas kernels for 24% -> 27%
where the time goes in v4:
time: 800 us; the launch traced here: 790 us
  waiting for transfers between devices  354 us (44%)
  Pallas kernels  301 us (38%)
  starting transfers between devices  79.9 us (10%)
  local copies, waits for them, and re-layouts  49.7 us (6%)
    ppermute x118, waiting for transfers between devices, permute(): return lax.ppermute(values, AXES, pairs)  354 us
    pallas_call x66, Pallas kernels, whole_call(): pl.pallas_call(tied(body, len(specs), ties), out_shape=out_shape, in_spec...  143 us
    ppermute x118, starting transfers between devices, permute(): return lax.ppermute(values, AXES, pairs)  79.9 us
    pallas_call x2, Pallas kernels, ff_backward(): kernel_call(functools.partial(ff_backward_body, old is not None), (wide /...  61.1 us
    unnamed x242, local copies, waits for them, and re-layouts  48.8 us
    pallas_call x2, Pallas kernels, ff_forward(): kernel_call(ff_forward_body, (wide // TILE,), [full((size, width))] * 4 +...  46.3 us
    pallas_call x2, Pallas kernels, ff_weights(): kernel_call(functools.partial(ff_weights_body, split, old is not None), (...  29.8 us
    pallas_call x2, Pallas kernels, backward_loop(): pl.pallas_call(tied(attend_back_body, 10, ties), out_shape=[jax.ShapeDtyp...  20.8 us
  transfers between devices with their start and end apart: 118, of which 57 were waited for; matrix products, arithmetic and copies ran while one was open for 0% of the time, Pallas kernels for 27%

profile of v4, /device:TPU:0, one launch (start us, length us, event | category | flops | bytes accessed | tf_op | source)
XLA Modules:
  0.0 789.9 jit_solution(17213017848939919284)
XLA Ops:
  10.5 16.9 %collective-permute-done.1.refs_3_ = bf16[48,1920]{1,0:T(8,128)(2,1)S(1)} collective-permute-done((bf16[48,1920]{1,0:T(8,128)(2,1)S(1)}, bf16[48,1920]{1,0:T(8,128)(2,1)S(1)}, u32[]{:S(2)}, u32[]{:S(2)}) %collective-permute-start.1) | collective-permute-done | bytes 184352 | tf_op jit(solution)/shard_map/ppermute | solution.py:75
  31.0 14.9 %collective-permute-done.3.refs_3_ = bf16[2,48,1920]{2,1,0:T(8,128)(2,1)S(1)} collective-permute-done((bf16[2,48,1920]{2,1,0:T(8,128)(2,1)S(1)}, bf16[2,48,1920]{2,1,0:T(8,128)(2,1)S(1)}, u32[]{:S(2)}, u32[]{:S(2)}) %collective-permute-start.3) | collective-permute-done | bytes 368672 | tf_op jit(solution)/shard_map/ppermute | solution.py:75
  50.6 7.8 collective-permute-done.7.refs_3_
  58.4 5.4 collective-permute-done.8.refs_4_
  67.9 4.4 collective-permute-start.15
  72.4 28.5 %collective-permute-done.10.refs_3_ = bf16[2,2,2,48,1920]{4,3,2,1,0:T(8,128)(2,1)S(1)} collective-permute-done((bf16[2,2,2,48,1920]{4,3,2,1,0:T(8,128)(2,1)S(1)}, bf16[2,2,2,48,1920]{4,3,2,1,0:T(8,128)(2,1)S(1)}, u32[]{:S(2)}, u32[]{:S(2)}) %collective-permute-start.10) | collective-permute-done | bytes 1474592 | tf_op jit(solution)/shard_map/ppermute | solution.py:75
  108.6 6.9 collective-permute-done.15.refs_1_.refs_3_
  125.1 5.1 shard_map.212
  135.8 4.4 collective-permute-done.17.refs_3_
  148.8 10.3 %collective-permute-done.18.refs_1_ = bf16[256,512]{1,0:T(8,128)(2,1)S(1)} collective-permute-done((bf16[256,512]{1,0:T(8,128)(2,1)S(1)}, bf16[256,512]{1,0:T(8,128)(2,1)S(1)}, u32[]{:S(2)}, u32[]{:S(2)}) %collective-permute-start.18) | collective-permute-done | bytes 262176 | tf_op jit(solution)/shard_map/ppermute | solution.py:75
  169.4 8.3 %collective-permute-done.20.refs_1_ = bf16[2,256,512]{2,1,0:T(8,128)(2,1)} collective-permute-done((bf16[2,256,512]{2,1,0:T(8,128)(2,1)S(1)}, bf16[2,256,512]{2,1,0:T(8,128)(2,1)}, u32[]{:S(2)}, u32[]{:S(2)}) %collective-permute-start.20) | collective-permute-done | bytes 524320 | tf_op jit(solution)/shard_map/ppermute | solution.py:75
  192.2 6.4 shard_map.218
  204.7 21.5 %collective-permute-done.33.refs_3_ = bf16[2,224,512]{2,1,0:T(8,128)(2,1)} collective-permute-done((bf16[2,224,512]{2,1,0:T(8,128)(2,1)}, bf16[2,224,512]{2,1,0:T(8,128)(2,1)}, u32[]{:S(2)}, u32[]{:S(2)}) %collective-permute-start.33) | collective-permute-done | bytes 458784 | tf_op jit(solution)/shard_map/ppermute | solution.py:75
  230.4 4.7 shard_map.221
  236.0 4.2 shard_map.224.wu_ref.refs_7_
  246.2 4.8 collective-permute-done.35
  251.0 4.4 collective-permute-done.34
  255.5 4.2 shard_map.226.wd_ref.refs_8_
  259.7 23.6 %shard_map.227 = (f32[512,1152]{1,0:T(8,128)S(1)}, bf16[1024,1792]{1,0:T(8,128)(2,1)}, bf16[1024,1792]{1,0:T(8,128)(2,1)}, bf16[128,1152]{1,0:T(8,128)(2,1)S(1)}...) custom-call(bf16[256,1152]{1,0:T(8,128)(2,1)S(1)} %get-tuple-element.255.x0_ref.refs_1_, ...), custom_call_target="tpu_custom_call" | custom-call | flops 12683575296 | tf_op jit(solution)/shard_map/pallas_call | solution.py:242
  288.4 13.6 %collective-permute-done.41.refs_2_ = bf16[256,1152]{1,0:T(8,128)(2,1)S(1)} collective-permute-done((bf16[256,1152]{1,0:T(8,128)(2,1)S(1)}, bf16[256,1152]{1,0:T(8,128)(2,1)S(1)}, u32[]{:S(2)}, u32[]{:S(2)}) %collective-permute-start.41) | collective-permute-done | bytes 589856 | tf_op jit(solution)/shard_map/ppermute | solution.py:75
  310.1 6.7 collective-permute-done.44.refs_3_
  316.8 14.4 %collective-permute-done.43.refs_2_ = bf16[256,512]{1,0:T(8,128)(2,1)S(1)} collective-permute-done((bf16[256,512]{1,0:T(8,128)(2,1)S(1)}, bf16[256,512]{1,0:T(8,128)(2,1)S(1)}, u32[]{:S(2)}, u32[]{:S(2)}) %collective-permute-start.43) | collective-permute-done | bytes 262176 | tf_op jit(solution)/shard_map/ppermute | solution.py:75
  333.2 5.3 shard_map.231
  344.0 4.9 shard_map.233
  348.9 10.3 %collective-permute-done.49.refs_0_ = bf16[256,1152]{1,0:T(8,128)(2,1)S(1)} collective-permute-done((bf16[256,1152]{1,0:T(8,128)(2,1)S(1)}, bf16[256,1152]{1,0:T(8,128)(2,1)S(1)}, u32[]{:S(2)}, u32[]{:S(2)}) %collective-permute-start.49) | collective-permute-done | bytes 589856 | tf_op jit(solution)/shard_map/ppermute | solution.py:75
  361.3 22.7 %shard_map.235 = (f32[512,1152]{1,0:T(8,128)S(1)}, bf16[1024,1792]{1,0:T(8,128)(2,1)}, bf16[1024,1792]{1,0:T(8,128)(2,1)}, bf16[128,1152]{1,0:T(8,128)(2,1)S(1)}...) custom-call(bf16[256,1152]{1,0:T(8,128)(2,1)S(1)} %get-tuple-element.277.x0_ref.refs_0_, ...), custom_call_target="tpu_custom_call" | custom-call | flops 12683575296 | tf_op jit(solution)/shard_map/pallas_call | solution.py:242
  392.9 30.5 %shard_map.238 = (f32[512,1152]{1,0:T(8,128)}, bf16[1024,1792]{1,0:T(8,128)(2,1)}, bf16[1024,1792]{1,0:T(8,128)(2,1)}, bf16[1792,640]{1,0:T(8,128)(2,1)}, bf16[1...) custom-call(bf16[256,1152]{1,0:T(8,128)(2,1)S(1)} %copy-done.34, ...), custom_call_target="tpu_custom_call" | custom-call | tf_op jit(solution)/shard_map/pallas_call | solution.py:330
  432.2 13.7 %shard_map.240 = (bf16[1152,1792]{1,0:T(8,128)(2,1)}, bf16[1152,1792]{1,0:T(8,128)(2,1)}) custom-call(bf16[256,1152]{1,0:T(8,128)(2,1)S(1)} %get-tuple-element.277.x0_ref.refs_0_, bf16[256,1152]{1,0:T(8,128)(2,1)S(1)} %shard_map.234.x1_ref.refs_1_, bf16[256,1152]{1,0:T(8,128)(2,1)S(1)} %copy-done.101, bf16[256,1152]{1,0:T(8,128)(2,1)S(1)} %copy-done.103, ...), custom_call_target="tpu_custom_call" | custom-call | flops 8455716864 | tf_op jit(solution)/shard_map/pallas_call | solution.py:421
  446.0 4.2 shard_map.241
  451.2 9.9 %shard_map.242 = (bf16[4,256,512]{2,1,0:T(8,128)(2,1)S(1)}, bf16[4,256,512]{2,1,0:T(8,128)(2,1)S(1)}, bf16[256,1024]{1,0:T(8,128)(2,1)S(1)}) custom-call(bf16[256,1024]{1,0:T(8,128)(2,1)S(1)} %shard_map.230.q_ref, bf16[2048,512]{1,0:T(8,128)(2,1)} %copy-done.109, s32[256,1]{1,0:T(8,128)S(1)} %copy-done.85, s32[256,1]{1,0:T(8,128)S(1)} %copy-done.87, ...), custom_call_target="tpu_custom_call" | custom-call | flops 5368709120 | tf_op jit(solution)/shard_map/pallas_call | solution.py:1438
  466.8 11.9 %collective-permute-done.65.refs_1_ = bf16[2,256,512]{2,1,0:T(8,128)(2,1)S(1)} collective-permute-done((bf16[2,256,512]{2,1,0:T(8,128)(2,1)S(1)}, bf16[2,256,512]{2,1,0:T(8,128)(2,1)S(1)}, u32[]{:S(2)}, u32[]{:S(2)}) %collective-permute-start.65) | collective-permute-done | bytes 524320 | tf_op jit(solution)/shard_map/ppermute | solution.py:75
  486.6 6.8 collective-permute-done.66.refs_1_
  496.2 4.2 shard_map.248
  501.4 14.1 %collective-permute-done.72.refs_1_ = bf16[256,1152]{1,0:T(8,128)(2,1)S(1)} collective-permute-done((bf16[256,1152]{1,0:T(8,128)(2,1)S(1)}, bf16[256,1152]{1,0:T(8,128)(2,1)S(1)}, u32[]{:S(2)}, u32[]{:S(2)}) %collective-permute-start.72) | collective-permute-done | bytes 589856 | tf_op jit(solution)/shard_map/ppermute | solution.py:75
  517.5 30.7 %shard_map.249 = (f32[512,1152]{1,0:T(8,128)}, bf16[1024,1792]{1,0:T(8,128)(2,1)}, bf16[1024,1792]{1,0:T(8,128)(2,1)}, bf16[1792,640]{1,0:T(8,128)(2,1)}, bf16[1...) custom-call(bf16[256,1152]{1,0:T(8,128)(2,1)S(1)} %get-tuple-element, ...), custom_call_target="tpu_custom_call" | custom-call | tf_op jit(solution)/shard_map/pallas_call | solution.py:330
  558.5 16.0 %shard_map.252 = (bf16[2,2,144,1792]{3,2,1,0:T(8,128)(2,1)S(1)}, bf16[2,2,144,1792]{3,2,1,0:T(8,128)(2,1)}, bf16[2,2,144,1792]{3,2,1,0:T(8,128)(2,1)}, bf16[2,2,144,1792]{3,2,1,0:T(8,128)(2,1)}) custom-call(s32[5]{0:T(128)S(1)} %stack.23.refs_0_.coords_ref.refs_9_, bf16[256,1152]{1,0:T(8,128)(2,1)S(1)} %copy-done.99, ...), custom_call_target="tpu_custom_call" | custom-call | flops 8455716864 | tf_op jit(solution)/shard_map/pallas_call | solution.py:421
  583.4 10.9 %shard_map.255 = (bf16[4,256,512]{2,1,0:T(8,128)(2,1)S(1)}, bf16[4,256,512]{2,1,0:T(8,128)(2,1)}, bf16[256,1024]{1,0:T(8,128)(2,1)S(1)}) custom-call(bf16[256,1024]{1,0:T(8,128)(2,1)S(1)} %copy-done.41, bf16[2048,512]{1,0:T(8,128)(2,1)} %copy-done.108, s32[256,1]{1,0:T(8,128)S(1)} %copy-done.85, s32[256,1]{1,0:T(8,128)S(1)} %copy-done.87, ...), custom_call_target="tpu_custom_call" | custom-call | flops 5368709120 | tf_op jit(solution)/shard_map/pallas_call | solution.py:1438
  605.2 7.7 collective-permute-done.83.refs_1_
  622.0 4.5 shard_map.259
  635.4 5.6 shard_map.262
  644.9 5.2 shard_map.264
  659.8 12.6 %collective-permute-done.98.refs_1_ = bf16[224,640]{1,0:T(8,128)(2,1)S(1)} collective-permute-done((bf16[224,640]{1,0:T(8,128)(2,1)}, bf16[224,640]{1,0:T(8,128)(2,1)S(1)}, u32[]{:S(2)}, u32[]{:S(2)}) %collective-permute-start.98) | collective-permute-done | bytes 286752 | tf_op jit(solution)/shard_map/ppermute | solution.py:75
  674.2 17.4 %collective-permute-done.96.refs_2_ = bf16[2,144,1792]{2,1,0:T(8,128)(2,1)S(1)} collective-permute-done((bf16[2,144,1792]{2,1,0:T(8,128)(2,1)S(1)}, bf16[2,144,1792]{2,1,0:T(8,128)(2,1)S(1)}, u32[]{:S(2)}, u32[]{:S(2)}) %collective-permute-start.96) | collective-permute-done | bytes 1032224 | tf_op jit(solution)/shard_map/ppermute | solution.py:75
  705.0 28.3 %collective-permute-done.107.refs_2_ = bf16[144,1792]{1,0:T(8,128)(2,1)S(1)} collective-permute-done((bf16[144,1792]{1,0:T(8,128)(2,1)S(1)}, bf16[144,1792]{1,0:T(8,128)(2,1)S(1)}, u32[]{:S(2)}, u32[]{:S(2)}) %collective-permute-start.107) | collective-permute-done | bytes 516128 | tf_op jit(solution)/shard_map/ppermute | solution.py:75
  733.3 11.0 %collective-permute-done.108.refs_4_ = bf16[144,1792]{1,0:T(8,128)(2,1)S(1)} collective-permute-done((bf16[144,1792]{1,0:T(8,128)(2,1)S(1)}, bf16[144,1792]{1,0:T(8,128)(2,1)S(1)}, u32[]{:S(2)}, u32[]{:S(2)}) %collective-permute-start.108) | collective-permute-done | bytes 516128 | tf_op jit(solution)/shard_map/ppermute | solution.py:75
  750.5 16.2 %collective-permute-done.111.refs_5_ = bf16[2,56,768]{2,1,0:T(8,128)(2,1)S(1)} collective-permute-done((bf16[2,56,768]{2,1,0:T(8,128)(2,1)S(1)}, bf16[2,56,768]{2,1,0:T(8,128)(2,1)S(1)}, u32[]{:S(2)}, u32[]{:S(2)}) %collective-permute-start.111) | collective-permute-done | bytes 172064 | tf_op jit(solution)/shard_map/ppermute | solution.py:75
  771.2 8.9 %collective-permute-done.116.p2_ref = bf16[2,36,1792]{2,1,0:T(8,128)(2,1)S(1)} collective-permute-done((bf16[2,36,1792]{2,1,0:T(8,128)(2,1)S(1)}, bf16[2,36,1792]{2,1,0:T(8,128)(2,1)S(1)}, u32[]{:S(2)}, u32[]{:S(2)}) %collective-permute-start.116) | collective-permute-done | bytes 258080 | tf_op jit(solution)/shard_map/ppermute | solution.py:75
  780.1 4.3 collective-permute-done.117.p3_ref
  (512 shorter events, 248.5 us)
Async XLA Ops:
  6.4 21.1 %collective-permute-start = (bf16[48,2048]{1,0:T(8,128)(2,1)S(1)}, bf16[48,2048]{1,0:T(8,128)(2,1)S(1)}, u32[]{:S(2)}, u32[]{:S(2)}) collective-permute-start(bf16[48,2048]{1,0:T(8,128)(2,1)S(1)} %get-tuple-element.216.refs_0_), channel_id=1, source_target_pairs={{0,4},{1,5},{2,6},{3,7},{4,0},{5,1},{6,2},{7,3},{8,12},{9,13},{10,... | collective-permute-start | bytes 589832 | tf_op jit(solution)/shard_map/ppermute | solution.py:75
  66.0 36.7 %collective-permute-start.9 = (bf16[2,2,2,48,2048]{4,3,2,1,0:T(8,128)(2,1)}, bf16[2,2,2,48,2048]{4,3,2,1,0:T(8,128)(2,1)S(1)}, u32[]{:S(2)}, u32[]{:S(2)}) collective-permute-start(bf16[2,2,2,48,2048]{4,3,2,1,0:T(8,128)(2,1)} %get-tuple-element.226.refs_0_), channel_id=1, source_target_pairs={{0,16},{1,17},{2,18},{3,19},{4,20},{5,21},{6,22},{7,23},{8,24},{9,... | collective-permute-start | bytes 4718600 | tf_op jit(solution)/shard_map/ppermute | solution.py:75
  66.6 34.3 %collective-permute-start.10 = (bf16[2,2,2,48,1920]{4,3,2,1,0:T(8,128)(2,1)S(1)}, bf16[2,2,2,48,1920]{4,3,2,1,0:T(8,128)(2,1)S(1)}, u32[]{:S(2)}, u32[]{:S(2)}) collective-permute-start(bf16[2,2,2,48,1920]{4,3,2,1,0:T(8,128)(2,1)S(1)} %get-tuple-element.227.refs_2_), channel_id=1, source_target_pairs={{0,8},{1,9},{2,10},{3,11},{4,12},{5,13},{6,14},{7,15},{8,0},{9,1},... | collective-permute-start | bytes 4423688 | tf_op jit(solution)/shard_map/ppermute | solution.py:75
  67.9 47.5 %collective-permute-start.15 = (bf16[2,144,1792]{2,1,0:T(8,128)(2,1)S(1)}, bf16[2,144,1792]{2,1,0:T(8,128)(2,1)S(1)}, u32[]{:S(2)}, u32[]{:S(2)}) collective-permute-start(bf16[2,144,1792]{2,1,0:T(8,128)(2,1)S(1)} %shard_map.208.refs_4_.refs_0_.refs_2_), channel_id=1, source_target_pairs={{0,4},{1,5},{2,6},{3,7},{4,0},{5,1},{6,2},{7,3},{8,12},{9,13},{10,... | collective-permute-start | bytes 3096584 | tf_op jit(solution)/shard_map/ppermute | solution.py:75
  116.5 23.7 %collective-permute-start.17 = (bf16[2,144,1792]{2,1,0:T(8,128)(2,1)S(1)}, bf16[2,144,1792]{2,1,0:T(8,128)(2,1)}, u32[]{:S(2)}, u32[]{:S(2)}) collective-permute-start(bf16[2,144,1792]{2,1,0:T(8,128)(2,1)S(1)} %get-tuple-element.239.refs_2_), channel_id=1, source_target_pairs={{0,16},{1,17},{2,18},{3,19},{4,20},{5,21},{6,22},{7,23},{8,24},{9,... | collective-permute-start | bytes 3096584 | tf_op jit(solution)/shard_map/ppermute | solution.py:75
  117.9 23.4 %collective-permute-start.16 = (bf16[2,144,1792]{2,1,0:T(8,128)(2,1)S(1)}, bf16[2,144,1792]{2,1,0:T(8,128)(2,1)}, u32[]{:S(2)}, u32[]{:S(2)}) collective-permute-start(bf16[2,144,1792]{2,1,0:T(8,128)(2,1)S(1)} %get-tuple-element.232.refs_9_.refs_0_), channel_id=1, source_target_pairs={{0,8},{1,9},{2,10},{3,11},{4,12},{5,13},{6,14},{7,15},{8,0},{9,1},... | collective-permute-start | bytes 3096584 | tf_op jit(solution)/shard_map/ppermute | solution.py:75
  121.9 26.8 %collective-permute-start.19 = (bf16[224,1152]{1,0:T(8,128)(2,1)}, bf16[224,1152]{1,0:T(8,128)(2,1)S(1)}, u32[]{:S(2)}, u32[]{:S(2)}) collective-permute-start(bf16[224,1152]{1,0:T(8,128)(2,1)} %copy-done.80), channel_id=1, source_target_pairs={{0,4},{1,5},{2,6},{3,7},{4,0},{5,1},{6,2},{7,3},{8,12},{9,13},{10,... | collective-permute-start | bytes 1548296 | tf_op jit(solution)/shard_map/ppermute | solution.py:75
  122.6 43.7 %collective-permute-start.23 = (bf16[2,2,2,2,48,512]{5,4,3,2,1,0:T(8,128)(2,1)}, bf16[2,2,2,2,48,512]{5,4,3,2,1,0:T(8,128)(2,1)S(1)}, u32[]{:S(2)}, u32[]{:S(2)}) collective-permute-start(bf16[2,2,2,2,48,512]{5,4,3,2,1,0:T(8,128)(2,1)} %copy-done.66), channel_id=1, source_target_pairs={{0,1},{1,0},{2,3},{3,2},{4,5},{5,4},{6,7},{7,6},{8,9},{9,8},{10,11... | collective-permute-start | bytes 2359304 | tf_op jit(solution)/shard_map/ppermute | solution.py:75
  145.3 20.2 %collective-permute-start.26 = (bf16[2,2,2,2,48,256]{5,4,3,2,1,0:T(8,128)(2,1)}, bf16[2,2,2,2,48,256]{5,4,3,2,1,0:T(8,128)(2,1)S(1)}, u32[]{:S(2)}, u32[]{:S(2)}) collective-permute-start(bf16[2,2,2,2,48,256]{5,4,3,2,1,0:T(8,128)(2,1)} %get-tuple-element.249), channel_id=1, source_target_pairs={{0,1},{1,0},{2,3},{3,2},{4,5},{5,4},{6,7},{7,6},{8,9},{9,8},{10,11... | collective-permute-start | bytes 1179656 | tf_op jit(solution)/shard_map/ppermute | solution.py:75
  145.3 22.7 %collective-permute-start.25 = (bf16[2,2,2,2,48,512]{5,4,3,2,1,0:T(8,128)(2,1)S(1)}, bf16[2,2,2,2,48,512]{5,4,3,2,1,0:T(8,128)(2,1)S(1)}, u32[]{:S(2)}, u32[]{:S(2)}) collective-permute-start(bf16[2,2,2,2,48,512]{5,4,3,2,1,0:T(8,128)(2,1)S(1)} %copy-done.69), channel_id=1, source_target_pairs={{0,1},{1,0},{2,3},{3,2},{4,5},{5,4},{6,7},{7,6},{8,9},{9,8},{10,11... | collective-permute-start | bytes 2359304 | tf_op jit(solution)/shard_map/ppermute | solution.py:75
  148.8 29.0 %collective-permute-start.24 = (bf16[2,2,2,2,48,640]{5,4,3,2,1,0:T(8,128)(2,1)S(1)}, bf16[2,2,2,2,48,640]{5,4,3,2,1,0:T(8,128)(2,1)S(1)}, u32[]{:S(2)}, u32[]{:S(2)}) collective-permute-start(bf16[2,2,2,2,48,640]{5,4,3,2,1,0:T(8,128)(2,1)S(1)} %copy-done.54), channel_id=1, source_target_pairs={{0,1},{1,0},{2,3},{3,2},{4,5},{5,4},{6,7},{7,6},{8,9},{9,8},{10,11... | collective-permute-start | bytes 2949128 | tf_op jit(solution)/shard_map/ppermute | solution.py:75
  159.1 76.2 %collective-permute-start.31 = (bf16[2,2,144,1792]{3,2,1,0:T(8,128)(2,1)}, bf16[2,2,144,1792]{3,2,1,0:T(8,128)(2,1)}, u32[]{:S(2)}, u32[]{:S(2)}) collective-permute-start(bf16[2,2,144,1792]{3,2,1,0:T(8,128)(2,1)} %get-tuple-element.258), channel_id=1, source_target_pairs={{0,8},{1,9},{2,10},{3,11},{4,12},{5,13},{6,14},{7,15},{8,0},{9,1},... | collective-permute-start | bytes 6193160 | tf_op jit(solution)/shard_map/ppermute | solution.py:75
  168.9 71.3 %collective-permute-start.30 = (bf16[2,2,144,1792]{3,2,1,0:T(8,128)(2,1)S(1)}, bf16[2,2,144,1792]{3,2,1,0:T(8,128)(2,1)}, u32[]{:S(2)}, u32[]{:S(2)}) collective-permute-start(bf16[2,2,144,1792]{3,2,1,0:T(8,128)(2,1)S(1)} %copy-done.4), channel_id=1, source_target_pairs={{0,16},{1,17},{2,18},{3,19},{4,20},{5,21},{6,22},{7,23},{8,24},{9,... | collective-permute-start | bytes 6193160 | tf_op jit(solution)/shard_map/ppermute | solution.py:75
  177.8 48.4 %collective-permute-start.32 = (bf16[2,224,640]{2,1,0:T(8,128)(2,1)}, bf16[2,224,640]{2,1,0:T(8,128)(2,1)S(1)}, u32[]{:S(2)}, u32[]{:S(2)}) collective-permute-start(bf16[2,224,640]{2,1,0:T(8,128)(2,1)} %get-tuple-element.244.refs_2_.refs_0_), channel_id=1, source_target_pairs={{0,8},{1,9},{2,10},{3,11},{4,12},{5,13},{6,14},{7,15},{8,0},{9,1},... | collective-permute-start | bytes 1720328 | tf_op jit(solution)/shard_map/ppermute | solution.py:75
  180.4 45.8 %collective-permute-start.33 = (bf16[2,224,512]{2,1,0:T(8,128)(2,1)}, bf16[2,224,512]{2,1,0:T(8,128)(2,1)}, u32[]{:S(2)}, u32[]{:S(2)}) collective-permute-start(bf16[2,224,512]{2,1,0:T(8,128)(2,1)} %get-tuple-element.259.refs_2_), channel_id=1, source_target_pairs={{0,16},{1,17},{2,18},{3,19},{4,20},{5,21},{6,22},{7,23},{8,24},{9,... | collective-permute-start | bytes 1376264 | tf_op jit(solution)/shard_map/ppermute | solution.py:75
  204.4 30.7 %collective-permute-start.27 = (bf16[256,1152]{1,0:T(8,128)(2,1)S(1)}, bf16[256,1152]{1,0:T(8,128)(2,1)S(1)}, u32[]{:S(2)}, u32[]{:S(2)}) collective-permute-start(bf16[256,1152]{1,0:T(8,128)(2,1)S(1)} %get-tuple-element.255.x0_ref.refs_1_), channel_id=1, source_target_pairs={{0,2},{1,3},{2,0},{3,1},{4,6},{5,7},{6,4},{7,5},{8,10},{9,11},{10,... | collective-permute-start | bytes 1769480 | tf_op jit(solution)/shard_map/ppermute | solution.py:75
  228.4 27.0 %collective-permute-start.34 = (bf16[2,2,224,640]{3,2,1,0:T(8,128)(2,1)S(1)}, bf16[2,2,224,640]{3,2,1,0:T(8,128)(2,1)}, u32[]{:S(2)}, u32[]{:S(2)}) collective-permute-start(bf16[2,2,224,640]{3,2,1,0:T(8,128)(2,1)S(1)} %get-tuple-element.260), channel_id=1, source_target_pairs={{0,16},{1,17},{2,18},{3,19},{4,20},{5,21},{6,22},{7,23},{8,24},{9,... | collective-permute-start | bytes 3440648 | tf_op jit(solution)/shard_map/ppermute | solution.py:75
  229.0 22.0 %collective-permute-start.35 = (bf16[2,2,224,512]{3,2,1,0:T(8,128)(2,1)}, bf16[2,2,224,512]{3,2,1,0:T(8,128)(2,1)}, u32[]{:S(2)}, u32[]{:S(2)}) collective-permute-start(bf16[2,2,224,512]{3,2,1,0:T(8,128)(2,1)} %get-tuple-element.261), channel_id=1, source_target_pairs={{0,8},{1,9},{2,10},{3,11},{4,12},{5,13},{6,14},{7,15},{8,0},{9,1},... | collective-permute-start | bytes 2752520 | tf_op jit(solution)/shard_map/ppermute | solution.py:75
  235.1 24.6 %collective-permute-start.28 = (bf16[256,1152]{1,0:T(8,128)(2,1)S(1)}, bf16[256,1152]{1,0:T(8,128)(2,1)}, u32[]{:S(2)}, u32[]{:S(2)}) collective-permute-start(bf16[256,1152]{1,0:T(8,128)(2,1)S(1)} %get-tuple-element.255.x0_ref.refs_1_), channel_id=1, source_target_pairs={{0,1},{1,0},{2,3},{3,2},{4,5},{5,4},{6,7},{7,6},{8,9},{9,8},{10,11... | collective-permute-start | bytes 1769480 | tf_op jit(solution)/shard_map/ppermute | solution.py:75
  235.2 24.4 %collective-permute-start.29 = (bf16[256,1152]{1,0:T(8,128)(2,1)S(1)}, bf16[256,1152]{1,0:T(8,128)(2,1)}, u32[]{:S(2)}, u32[]{:S(2)}) collective-permute-start(bf16[256,1152]{1,0:T(8,128)(2,1)S(1)} %shard_map.222.x1_ref.refs_2_), channel_id=1, source_target_pairs={{0,1},{1,0},{2,3},{3,2},{4,5},{5,4},{6,7},{7,6},{8,9},{9,8},{10,11... | collective-permute-start | bytes 1769480 | tf_op jit(solution)/shard_map/ppermute | solution.py:75
  240.2 44.1 %collective-permute-start.40 = (bf16[256,1152]{1,0:T(8,128)(2,1)S(1)}, bf16[256,1152]{1,0:T(8,128)(2,1)S(1)}, u32[]{:S(2)}, u32[]{:S(2)}) collective-permute-start(bf16[256,1152]{1,0:T(8,128)(2,1)S(1)} %copy-done.33), channel_id=1, source_target_pairs={{0,2},{1,3},{2,0},{3,1},{4,6},{5,7},{6,4},{7,5},{8,10},{9,11},{10,... | collective-permute-start | bytes 1769480 | tf_op jit(solution)/shard_map/ppermute | solution.py:75
  306.9 24.4 %collective-permute-start.43 = (bf16[256,512]{1,0:T(8,128)(2,1)S(1)}, bf16[256,512]{1,0:T(8,128)(2,1)S(1)}, u32[]{:S(2)}, u32[]{:S(2)}) collective-permute-start(bf16[256,512]{1,0:T(8,128)(2,1)S(1)} %get-tuple-element.272.refs_0_), channel_id=1, source_target_pairs={{0,4},{1,5},{2,6},{3,7},{4,0},{5,1},{6,2},{7,3},{8,12},{9,13},{10,... | collective-permute-start | bytes 786440 | tf_op jit(solution)/shard_map/ppermute | solution.py:75
  308.9 22.4 %collective-permute-start.42 = (bf16[256,512]{1,0:T(8,128)(2,1)S(1)}, bf16[256,512]{1,0:T(8,128)(2,1)S(1)}, u32[]{:S(2)}, u32[]{:S(2)}) collective-permute-start(bf16[256,512]{1,0:T(8,128)(2,1)S(1)} %get-tuple-element.272.refs_0_), channel_id=1, source_target_pairs={{0,2},{1,3},{2,0},{3,1},{4,6},{5,7},{6,4},{7,5},{8,10},{9,11},{10,... | collective-permute-start | bytes 786440 | tf_op jit(solution)/shard_map/ppermute | solution.py:75
  310.1 22.7 %collective-permute-start.45 = (bf16[256,512]{1,0:T(8,128)(2,1)S(1)}, bf16[256,512]{1,0:T(8,128)(2,1)S(1)}, u32[]{:S(2)}, u32[]{:S(2)}) collective-permute-start(bf16[256,512]{1,0:T(8,128)(2,1)S(1)} %get-tuple-element.272.refs_0_), channel_id=1, source_target_pairs={{0,1},{1,0},{2,3},{3,2},{4,5},{5,4},{6,7},{7,6},{8,9},{9,8},{10,11... | collective-permute-start | bytes 786440 | tf_op jit(solution)/shard_map/ppermute | solution.py:75
  392.6 33.0 %collective-permute-start.56 = (bf16[256,1152]{1,0:T(8,128)(2,1)}, bf16[256,1152]{1,0:T(8,128)(2,1)S(1)}, u32[]{:S(2)}, u32[]{:S(2)}) collective-permute-start(bf16[256,1152]{1,0:T(8,128)(2,1)} %get-tuple-element.286), channel_id=1, source_target_pairs={{0,2},{1,3},{2,0},{3,1},{4,6},{5,7},{6,4},{7,5},{8,10},{9,11},{10,... | collective-permute-start | bytes 1769480 | tf_op jit(solution)/shard_map/ppermute | solution.py:75
  461.6 24.9 %collective-permute-start.71 = (bf16[256,1664]{1,0:T(8,128)(2,1)S(1)}, bf16[256,1664]{1,0:T(8,128)(2,1)S(1)}, u32[]{:S(2)}, u32[]{:S(2)}) collective-permute-start(bf16[256,1664]{1,0:T(8,128)(2,1)S(1)} %copy-done.60), channel_id=1, source_target_pairs={{0,1},{1,0},{2,3},{3,2},{4,5},{5,4},{6,7},{7,6},{8,9},{9,8},{10,11... | collective-permute-start | bytes 2555912 | tf_op jit(solution)/shard_map/ppermute | solution.py:75
  551.6 29.6 %collective-permute-start.80 = (bf16[2,2,224,640]{3,2,1,0:T(8,128)(2,1)}, bf16[2,2,224,640]{3,2,1,0:T(8,128)(2,1)}, u32[]{:S(2)}, u32[]{:S(2)}) collective-permute-start(bf16[2,2,224,640]{3,2,1,0:T(8,128)(2,1)} %get-tuple-element.340), channel_id=1, source_target_pairs={{0,8},{1,9},{2,10},{3,11},{4,12},{5,13},{6,14},{7,15},{8,0},{9,1},... | collective-permute-start | bytes 3440648 | tf_op jit(solution)/shard_map/ppermute | solution.py:75
  553.6 27.6 %collective-permute-start.81 = (bf16[2,2,224,512]{3,2,1,0:T(8,128)(2,1)}, bf16[2,2,224,512]{3,2,1,0:T(8,128)(2,1)}, u32[]{:S(2)}, u32[]{:S(2)}) collective-permute-start(bf16[2,2,224,512]{3,2,1,0:T(8,128)(2,1)} %get-tuple-element.342), channel_id=1, source_target_pairs={{0,16},{1,17},{2,18},{3,19},{4,20},{5,21},{6,22},{7,23},{8,24},{9,... | collective-permute-start | bytes 2752520 | tf_op jit(solution)/shard_map/ppermute | solution.py:75
  575.8 59.6 %collective-permute-start.85 = (bf16[2,2,144,1792]{3,2,1,0:T(8,128)(2,1)}, bf16[2,2,144,1792]{3,2,1,0:T(8,128)(2,1)}, u32[]{:S(2)}, u32[]{:S(2)}) collective-permute-start(bf16[2,2,144,1792]{3,2,1,0:T(8,128)(2,1)} %get-tuple-element.351), channel_id=1, source_target_pairs={{0,8},{1,9},{2,10},{3,11},{4,12},{5,13},{6,14},{7,15},{8,0},{9,1},... | collective-permute-start | bytes 6193160 | tf_op jit(solution)/shard_map/ppermute | solution.py:75
  576.4 58.9 %collective-permute-start.86 = (bf16[2,2,144,1792]{3,2,1,0:T(8,128)(2,1)}, bf16[2,2,144,1792]{3,2,1,0:T(8,128)(2,1)}, u32[]{:S(2)}, u32[]{:S(2)}) collective-permute-start(bf16[2,2,144,1792]{3,2,1,0:T(8,128)(2,1)} %get-tuple-element.353), channel_id=1, source_target_pairs={{0,16},{1,17},{2,18},{3,19},{4,20},{5,21},{6,22},{7,23},{8,24},{9,... | collective-permute-start | bytes 6193160 | tf_op jit(solution)/shard_map/ppermute | solution.py:75
  603.8 31.6 %collective-permute-start.87 = (bf16[2,224,640]{2,1,0:T(8,128)(2,1)S(1)}, bf16[2,224,640]{2,1,0:T(8,128)(2,1)S(1)}, u32[]{:S(2)}, u32[]{:S(2)}) collective-permute-start(bf16[2,224,640]{2,1,0:T(8,128)(2,1)S(1)} %get-tuple-element.354), channel_id=1, source_target_pairs={{0,16},{1,17},{2,18},{3,19},{4,20},{5,21},{6,22},{7,23},{8,24},{9,... | collective-permute-start | bytes 1720328 | tf_op jit(solution)/shard_map/ppermute | solution.py:75
  613.0 20.4 %collective-permute-start.88 = (bf16[2,224,512]{2,1,0:T(8,128)(2,1)}, bf16[2,224,512]{2,1,0:T(8,128)(2,1)S(1)}, u32[]{:S(2)}, u32[]{:S(2)}) collective-permute-start(bf16[2,224,512]{2,1,0:T(8,128)(2,1)} %copy-done.106), channel_id=1, source_target_pairs={{0,8},{1,9},{2,10},{3,11},{4,12},{5,13},{6,14},{7,15},{8,0},{9,1},... | collective-permute-start | bytes 1376264 | tf_op jit(solution)/shard_map/ppermute | solution.py:75
  615.0 29.3 %collective-permute-start.84 = (bf16[256,512]{1,0:T(8,128)(2,1)S(1)}, bf16[256,512]{1,0:T(8,128)(2,1)S(1)}, u32[]{:S(2)}, u32[]{:S(2)}) collective-permute-start(bf16[256,512]{1,0:T(8,128)(2,1)S(1)} %get-tuple-element.349), channel_id=1, source_target_pairs={{0,4},{1,5},{2,6},{3,7},{4,0},{5,1},{6,2},{7,3},{8,12},{9,13},{10,... | collective-permute-start | bytes 786440 | tf_op jit(solution)/shard_map/ppermute | solution.py:75
  633.4 62.1 %collective-permute-start.94 = (bf16[2,2,2,48,1664]{4,3,2,1,0:T(8,128)(2,1)}, bf16[2,2,2,48,1664]{4,3,2,1,0:T(8,128)(2,1)}, u32[]{:S(2)}, u32[]{:S(2)}) collective-permute-start(bf16[2,2,2,48,1664]{4,3,2,1,0:T(8,128)(2,1)} %get-tuple-element.372), channel_id=1, source_target_pairs={{0,8},{1,9},{2,10},{3,11},{4,12},{5,13},{6,14},{7,15},{8,0},{9,1},... | collective-permute-start | bytes 3833864 | tf_op jit(solution)/shard_map/ppermute | solution.py:75
  643.8 51.8 %collective-permute-start.95 = (bf16[2,2,2,56,1280]{4,3,2,1,0:T(8,128)(2,1)}, bf16[2,2,2,56,1280]{4,3,2,1,0:T(8,128)(2,1)S(1)}, u32[]{:S(2)}, u32[]{:S(2)}) collective-permute-start(bf16[2,2,2,56,1280]{4,3,2,1,0:T(8,128)(2,1)} %copy-done.95), channel_id=1, source_target_pairs={{0,16},{1,17},{2,18},{3,19},{4,20},{5,21},{6,22},{7,23},{8,24},{9,... | collective-permute-start | bytes 3440648 | tf_op jit(solution)/shard_map/ppermute | solution.py:75
  654.1 37.5 %collective-permute-start.96 = (bf16[2,144,1792]{2,1,0:T(8,128)(2,1)S(1)}, bf16[2,144,1792]{2,1,0:T(8,128)(2,1)S(1)}, u32[]{:S(2)}, u32[]{:S(2)}) collective-permute-start(bf16[2,144,1792]{2,1,0:T(8,128)(2,1)S(1)} %copy-done.97), channel_id=1, source_target_pairs={{0,16},{1,17},{2,18},{3,19},{4,20},{5,21},{6,22},{7,23},{8,24},{9,... | collective-permute-start | bytes 3096584 | tf_op jit(solution)/shard_map/ppermute | solution.py:75
  654.6 37.0 %collective-permute-start.97 = (bf16[2,144,1792]{2,1,0:T(8,128)(2,1)S(1)}, bf16[2,144,1792]{2,1,0:T(8,128)(2,1)S(1)}, u32[]{:S(2)}, u32[]{:S(2)}) collective-permute-start(bf16[2,144,1792]{2,1,0:T(8,128)(2,1)S(1)} %copy-done.119), channel_id=1, source_target_pairs={{0,8},{1,9},{2,10},{3,11},{4,12},{5,13},{6,14},{7,15},{8,0},{9,1},... | collective-permute-start | bytes 3096584 | tf_op jit(solution)/shard_map/ppermute | solution.py:75
  672.5 30.2 %collective-permute-start.105 = (bf16[2,2,2,56,768]{4,3,2,1,0:T(8,128)(2,1)S(1)}, bf16[2,2,2,56,768]{4,3,2,1,0:T(8,128)(2,1)S(1)}, u32[]{:S(2)}, u32[]{:S(2)}) collective-permute-start(bf16[2,2,2,56,768]{4,3,2,1,0:T(8,128)(2,1)S(1)} %get-tuple-element.392), channel_id=1, source_target_pairs={{0,8},{1,9},{2,10},{3,11},{4,12},{5,13},{6,14},{7,15},{8,0},{9,1},... | collective-permute-start | bytes 2064392 | tf_op jit(solution)/shard_map/ppermute | solution.py:75
  697.8 47.6 %collective-permute-start.103 = (bf16[2,2,48,1664]{3,2,1,0:T(8,128)(2,1)S(1)}, bf16[2,2,48,1664]{3,2,1,0:T(8,128)(2,1)S(1)}, u32[]{:S(2)}, u32[]{:S(2)}) collective-permute-start(bf16[2,2,48,1664]{3,2,1,0:T(8,128)(2,1)S(1)} %get-tuple-element.389), channel_id=1, source_target_pairs={{0,16},{1,17},{2,18},{3,19},{4,20},{5,21},{6,22},{7,23},{8,24},{9,... | collective-permute-start | bytes 1916936 | tf_op jit(solution)/shard_map/ppermute | solution.py:75
  698.4 47.0 %collective-permute-start.104 = (bf16[2,2,56,1280]{3,2,1,0:T(8,128)(2,1)S(1)}, bf16[2,2,56,1280]{3,2,1,0:T(8,128)(2,1)S(1)}, u32[]{:S(2)}, u32[]{:S(2)}) collective-permute-start(bf16[2,2,56,1280]{3,2,1,0:T(8,128)(2,1)S(1)} %get-tuple-element.391), channel_id=1, source_target_pairs={{0,8},{1,9},{2,10},{3,11},{4,12},{5,13},{6,14},{7,15},{8,0},{9,1},... | collective-permute-start | bytes 1720328 | tf_op jit(solution)/shard_map/ppermute | solution.py:75
  699.8 33.5 %collective-permute-start.107 = (bf16[144,1792]{1,0:T(8,128)(2,1)S(1)}, bf16[144,1792]{1,0:T(8,128)(2,1)S(1)}, u32[]{:S(2)}, u32[]{:S(2)}) collective-permute-start(bf16[144,1792]{1,0:T(8,128)(2,1)S(1)} %get-tuple-element.395), channel_id=1, source_target_pairs={{0,4},{1,5},{2,6},{3,7},{4,0},{5,1},{6,2},{7,3},{8,12},{9,13},{10,... | collective-permute-start | bytes 1548296 | tf_op jit(solution)/shard_map/ppermute | solution.py:75
  701.0 43.2 %collective-permute-start.108 = (bf16[144,1792]{1,0:T(8,128)(2,1)S(1)}, bf16[144,1792]{1,0:T(8,128)(2,1)S(1)}, u32[]{:S(2)}, u32[]{:S(2)}) collective-permute-start(bf16[144,1792]{1,0:T(8,128)(2,1)S(1)} %get-tuple-element.397), channel_id=1, source_target_pairs={{0,4},{1,5},{2,6},{3,7},{4,0},{5,1},{6,2},{7,3},{8,12},{9,13},{10,... | collective-permute-start | bytes 1548296 | tf_op jit(solution)/shard_map/ppermute | solution.py:75
  703.4 42.0 %collective-permute-start.106 = (bf16[2,2,56,768]{3,2,1,0:T(8,128)(2,1)S(1)}, bf16[2,2,56,768]{3,2,1,0:T(8,128)(2,1)S(1)}, u32[]{:S(2)}, u32[]{:S(2)}) collective-permute-start(bf16[2,2,56,768]{3,2,1,0:T(8,128)(2,1)S(1)} %get-tuple-element.394), channel_id=1, source_target_pairs={{0,16},{1,17},{2,18},{3,19},{4,20},{5,21},{6,22},{7,23},{8,24},{9,... | collective-permute-start | bytes 1032200 | tf_op jit(solution)/shard_map/ppermute | solution.py:75
  746.3 20.3 %collective-permute-start.109 = (bf16[2,48,1664]{2,1,0:T(8,128)(2,1)S(1)}, bf16[2,48,1664]{2,1,0:T(8,128)(2,1)S(1)}, u32[]{:S(2)}, u32[]{:S(2)}) collective-permute-start(bf16[2,48,1664]{2,1,0:T(8,128)(2,1)S(1)} %get-tuple-element.400), channel_id=1, source_target_pairs={{0,2},{1,3},{2,0},{3,1},{4,6},{5,7},{6,4},{7,5},{8,10},{9,11},{10,... | collective-permute-start | bytes 958472 | tf_op jit(solution)/shard_map/ppermute | solution.py:75
  746.4 20.2 %collective-permute-start.110 = (bf16[2,56,1280]{2,1,0:T(8,128)(2,1)S(1)}, bf16[2,56,1280]{2,1,0:T(8,128)(2,1)S(1)}, u32[]{:S(2)}, u32[]{:S(2)}) collective-permute-start(bf16[2,56,1280]{2,1,0:T(8,128)(2,1)S(1)} %get-tuple-element.402), channel_id=1, source_target_pairs={{0,2},{1,3},{2,0},{3,1},{4,6},{5,7},{6,4},{7,5},{8,10},{9,11},{10,... | collective-permute-start | bytes 860168 | tf_op jit(solution)/shard_map/ppermute | solution.py:75
  748.5 21.9 %collective-permute-start.115 = (bf16[2,36,1792]{2,1,0:T(8,128)(2,1)S(1)}, bf16[2,36,1792]{2,1,0:T(8,128)(2,1)S(1)}, u32[]{:S(2)}, u32[]{:S(2)}) collective-permute-start(bf16[2,36,1792]{2,1,0:T(8,128)(2,1)S(1)} %get-tuple-element.414), channel_id=1, source_target_pairs={{0,1},{1,0},{2,3},{3,2},{4,5},{5,4},{6,7},{7,6},{8,9},{9,8},{10,11... | collective-permute-start | bytes 774152 | tf_op jit(solution)/shard_map/ppermute | solution.py:75
  748.5 31.6 %collective-permute-start.116 = (bf16[2,36,1792]{2,1,0:T(8,128)(2,1)S(1)}, bf16[2,36,1792]{2,1,0:T(8,128)(2,1)S(1)}, u32[]{:S(2)}, u32[]{:S(2)}) collective-permute-start(bf16[2,36,1792]{2,1,0:T(8,128)(2,1)S(1)} %get-tuple-element.415), channel_id=1, source_target_pairs={{0,2},{1,3},{2,0},{3,1},{4,6},{5,7},{6,4},{7,5},{8,10},{9,11},{10,... | collective-permute-start | bytes 774152 | tf_op jit(solution)/shard_map/ppermute | solution.py:75
  767.4 20.6 %collective-permute-start.112 = (bf16[48,1664]{1,0:T(8,128)(2,1)S(1)}, bf16[48,1664]{1,0:T(8,128)(2,1)S(1)}, u32[]{:S(2)}, u32[]{:S(2)}) collective-permute-start(bf16[48,1664]{1,0:T(8,128)(2,1)S(1)} %get-tuple-element.406), channel_id=1, source_target_pairs={{0,4},{1,5},{2,6},{3,7},{4,0},{5,1},{6,2},{7,3},{8,12},{9,13},{10,... | collective-permute-start | bytes 479240 | tf_op jit(solution)/shard_map/ppermute | solution.py:75
  (190 other events, 1675.5 us)

commit v5 on v4

--- a/solution.py
+++ b/solution.py
@@ -125,7 +125,6 @@
 COST_WEIGHTS = 4
 COST_ATTEND = 4
 COST_ATTEND_BACK = 10
-COST_OUTER = 0
 COST_LEAVE = 2
 COST_ENTER = 2
 LIGHT = pl.CostEstimate(flops=0, bytes_accessed=0, transcendentals=0)
@@ -919,24 +918,25 @@
 
 def enter_back_body(
     first_loop, own_ref, other_ref, result_ref, middle_ref, gain_ref, w_ref, ol_ref, od_ref,
-    grad_ref, branch_ref, side_ref, mixed_ref, gain_grad_ref,
+    grad_ref, branch_ref, mixed_ref, gain_grad_ref,
 ):
-    rank = side_ref.shape[1]
+    width = grad_ref.shape[1]
+    rank = branch_ref.shape[1] - width
     grad_normed = own_ref[...] + other_ref[...].astype(F32)
     back, gain_grad = norm_back(middle_ref[...], gain_ref[1:2], grad_normed)
     gain_grad_ref[...] = jnp.broadcast_to(gain_grad, gain_grad_ref.shape)
     grad = result_ref[...].astype(F32) + back
     grad_ref[...] = grad
     branch = rounded(grad)
-    branch_ref[...] = branch
+    branch_ref[:, :width] = branch
     side = rounded(matmul_nt(branch, ol_ref[...]))
-    side_ref[...] = side
+    branch_ref[:, width:] = side
     down = od_ref[:, :rank] if first_loop else od_ref[:, rank:]
     mixed_ref[...] = rounded(matmul_nt(branch, w_ref[...]) + matmul_nt(side, down))
 
 
 def rope_back_body(count, *refs):
-    gq_ref, ql_ref, cos_ref, sin_ref, out_ref, low_ref = refs[count:]
+    gq_ref, ql_ref, cos_ref, sin_ref, out_ref = refs[count:]
     width_q = gq_ref.shape[1]
     kv = refs[0][...].astype(F32)
     for ref in refs[1:count]:
@@ -944,8 +944,8 @@
     keys = rounded(rotate(kv[:, :HD], cos_ref[...], -sin_ref[...]))
     values = rounded(kv[:, HD:])
     out_ref[:, :HD] = keys
-    out_ref[:, HD:] = values
-    low_ref[...] = rounded(
+    out_ref[:, HD : 2 * HD] = values
+    out_ref[:, 2 * HD :] = rounded(
         matmul_nt(gq_ref[...], ql_ref[:, :width_q])
         + matmul_nt(keys, ql_ref[:, width_q : width_q + HD])
         + matmul_nt(values, ql_ref[:, width_q + HD :])
@@ -953,17 +953,17 @@
 
 
 def leave_back_body(
-    first_loop, kv_ref, gq_ref, low_ref, w_ref, qd_ref, residual_ref, gain_ref, grad_ref,
+    first_loop, in_ref, gq_ref, w_ref, qd_ref, residual_ref, gain_ref, grad_ref,
     other_gain_ref, *refs,
 ):
     out_ref, out_b_ref, gain_grad_ref = refs[-3:]
-    rank = low_ref.shape[1]
+    rank = in_ref.shape[1] - 2 * HD
     width_q = gq_ref.shape[1]
     down = qd_ref[:, :rank] if first_loop else qd_ref[:, rank:]
     grad_normed = (
         matmul_nt(gq_ref[...], w_ref[:, :width_q])
-        + matmul_nt(kv_ref[...], w_ref[:, width_q:])
-        + matmul_nt(low_ref[...], down)
+        + matmul_nt(in_ref[:, : 2 * HD], w_ref[:, width_q:])
+        + matmul_nt(in_ref[:, 2 * HD :], down)
     )
     back, gain_grad = norm_back(residual_ref[...], gain_ref[0:1], grad_normed)
     gain_grad_ref[0:1] = gain_grad
@@ -1038,31 +1038,36 @@
         ol_ref[loop] = outs[at : at + last_rows, :width]
 
 
-def outer_body(columns, rights, olds, own_ref, came_ref, *refs):
-    out_refs = refs[2 * rights + olds :]
+def outer_body(columns, pieces, olds, own_ref, came_ref, right_ref, right_came_ref, *refs):
+    out_refs = refs[olds:]
     own, came = own_ref[:, columns], came_ref[:, columns]
-    for number in range(rights):
-        right_ref, right_came_ref = refs[2 * number], refs[2 * number + 1]
-        out_ref = out_refs[number]
-        cols = out_ref.shape[1]
+    for number, piece in enumerate(pieces):
+        cols = piece.stop - piece.start
         step = 512 if cols % 512 == 0 else 384 if cols % 384 == 0 else cols
         for start in range(0, cols, step):
             part = slice(start, start + step)
-            total = matmul_tn(own, right_ref[:, part]) + matmul_tn(came, right_came_ref[:, part])
+            from_right = slice(piece.start + start, piece.start + start + step)
+            total = matmul_tn(own, right_ref[:, from_right]) + matmul_tn(
+                came, right_came_ref[:, from_right]
+            )
             if number < olds:
-                total = total + refs[2 * rights + number][:, part].astype(F32)
-            out_ref[:, part] = rounded(total)
-
-
-def outer(left, columns, rights, olds=(), ties=()):
+                total = total + refs[number][:, part].astype(F32)
+            out_refs[number][:, part] = rounded(total)
+
+
+def outer(left, columns, right, widths, olds=(), ties=()):
     rows = columns.stop - columns.start
+    pieces = []
+    at = 0
+    for cols in widths:
+        pieces.append(slice(at, at + cols))
+        at += cols
     return whole_call(
-        functools.partial(outer_body, columns, len(rights), len(olds)),
-        [shape(rows, right[0].shape[1]) for right in rights],
+        functools.partial(outer_body, columns, pieces, len(olds)),
+        [shape(rows, cols) for cols in widths],
         None,
-        [*left, *[value for right in rights for value in right], *olds],
+        [*left, *right, *olds],
         ties,
-        flops=int(COST_OUTER * rows * columns.stop * sum(value[0].shape[1] for value in rights)),
     )
 
 
@@ -1415,11 +1420,11 @@
                 d_up = (("y", "p"), [pair[2], grid.permute(pair[3], {"x": 1})])
         else:
             d_gate, d_up = pair
-        grad_middle, grad_branch_b, grad_side_b, grad_mixed_b, gain_grad_ff = whole_call(
+        grad_middle, grad_branch_b, grad_mixed_b, gain_grad_ff = whole_call(
             functools.partial(enter_back_body, loop == 0),
             [
-                shape(tokens, width, F32), shape(tokens, width), shape(tokens, rank),
-                shape(tokens, width_q), shape(8, width, F32),
+                shape(tokens, width, F32), shape(tokens, width + rank), shape(tokens, width_q),
+                shape(8, width, F32),
             ],
             None,
             [own, other, grad_result, middle, gains, w_out, ol, od],
@@ -1453,14 +1458,20 @@
         grad_kv = (("p", "h"), [kv_own, grid.permute(kv_sent, {"c": 1})])
         (grad_kv,) = step([(grad_kv, "h")])
         (grad_kv,) = step([(grad_kv, "p")])
-        branch, side = with_core(grad_branch_b), with_core(grad_side_b)
+        branch = with_core(grad_branch_b)
         d_out, d_od = outer(
-            spreads, mixed_columns, [branch, side], [old["out"]] if last else [], [grad_kv[1][0]]
+            spreads,
+            mixed_columns,
+            branch,
+            [width, rank],
+            [old["out"]] if last else [],
+            [grad_kv[1][0]],
         )
         (d_queries,) = outer(
             spreads,
             joined_columns,
-            [with_core(grad_queries_b)],
+            with_core(grad_queries_b),
+            [width_q],
             [old["queries"]] if last else [],
             [d_out],
         )
@@ -1494,9 +1505,9 @@
         else:
             sums["gate"], sums["up"] = d_gate, d_up
         sums["down"] = down
-        grad_kv_b, grad_low_rank_b = whole_call(
+        grad_in_b = whole_call(
             functools.partial(rope_back_body, len(grad_kv[1])),
-            [shape(tokens, 2 * HD), shape(tokens, rank)],
+            shape(tokens, 2 * HD + rank),
             None,
             [*grad_kv[1], grad_queries_b, ql, *tables],
             ties,
@@ -1504,7 +1515,8 @@
         sums["kv"], sums["qd"] = outer(
             spreads,
             joined_columns,
-            [with_core(grad_kv_b), with_core(grad_low_rank_b)],
+            with_core(grad_in_b),
+            [2 * HD, rank],
             [old["kv"]] if last else [],
         )
         following, following_b, gain_grads = whole_call(
@@ -1512,8 +1524,7 @@
             [shape(tokens, width, F32), shape(tokens, width), shape(8, width, F32)],
             None,
             [
-                grad_kv_b, grad_queries_b, grad_low_rank_b, w_qkv, qd, residual, gains,
-                grad_middle, gain_grad_ff,
+                grad_in_b, grad_queries_b, w_qkv, qd, residual, gains, grad_middle, gain_grad_ff,
             ]
             + ([old["gains"]] if last else []),
         )

time: 800 us -> 812 us (1.015)
  local copies, waits for them, and re-layouts: 49.7 us -> 68.2 us
  waiting for transfers between devices: 354 us -> 342 us
    unnamed x242 -> x294, local copies, waits for them, and re-layouts: 48.8 us -> 67.3 us
    ppermute x118 -> x114, waiting for transfers between devices: 354 us -> 342 us  [permute(): return lax.ppermute(values, AXES, pairs)]
    ppermute x118 -> x114, starting transfers between devices: 79.9 us -> 79.9 us  [permute(): return lax.ppermute(values, AXES, pairs)]
  transfers between devices with their start and end apart: 118 -> 114, of which waited for: 57 -> 51; matrix products, arithmetic and copies ran while one was open for 0% -> 0% of each run, Pallas kernels for 27% -> 27%
where the time goes in v5:
time: 812 us; the launch traced here: 801 us
  waiting for transfers between devices  342 us (42%)
  Pallas kernels  305 us (38%)
  starting transfers between devices  79.9 us (10%)
  local copies, waits for them, and re-layouts  68.2 us (8%)
    ppermute x114, waiting for transfers between devices, permute(): return lax.ppermute(values, AXES, pairs)  342 us
    pallas_call x66, Pallas kernels, whole_call(): pl.pallas_call(tied(body, len(specs), ties), out_shape=out_shape, in_spec...  149 us
    ppermute x114, starting transfers between devices, permute(): return lax.ppermute(values, AXES, pairs)  79.9 us
    unnamed x294, local copies, waits for them, and re-layouts  67.3 us
    pallas_call x2, Pallas kernels, ff_backward(): kernel_call(functools.partial(ff_backward_body, old is not None), (wide /...  61 us
    pallas_call x2, Pallas kernels, ff_forward(): kernel_call(ff_forward_body, (wide // TILE,), [full((size, width))] * 4 +...  45.6 us
    pallas_call x2, Pallas kernels, ff_weights(): kernel_call(functools.partial(ff_weights_body, split, old is not None), (...  29.8 us
    pallas_call x2, Pallas kernels, backward_loop(): pl.pallas_call(tied(attend_back_body, 10, ties), out_shape=[jax.ShapeDtyp...  19.8 us
  transfers between devices with their start and end apart: 114, of which 51 were waited for; matrix products, arithmetic and copies ran while one was open for 0% of the time, Pallas kernels for 27%

profile of v5, /device:TPU:0, one launch (start us, length us, event | category | flops | bytes accessed | tf_op | source)
XLA Modules:
  0.0 801.1 jit_solution(12521108629671330940)
XLA Ops:
  10.5 16.9 %collective-permute-done.1.refs_3_ = bf16[48,1920]{1,0:T(8,128)(2,1)S(1)} collective-permute-done((bf16[48,1920]{1,0:T(8,128)(2,1)S(1)}, bf16[48,1920]{1,0:T(8,128)(2,1)S(1)}, u32[]{:S(2)}, u32[]{:S(2)}) %collective-permute-start.1) | collective-permute-done | bytes 184352 | tf_op jit(solution)/shard_map/ppermute | solution.py:75
  31.0 14.9 %collective-permute-done.3.refs_3_ = bf16[2,48,1920]{2,1,0:T(8,128)(2,1)S(1)} collective-permute-done((bf16[2,48,1920]{2,1,0:T(8,128)(2,1)S(1)}, bf16[2,48,1920]{2,1,0:T(8,128)(2,1)S(1)}, u32[]{:S(2)}, u32[]{:S(2)}) %collective-permute-start.3) | collective-permute-done | bytes 368672 | tf_op jit(solution)/shard_map/ppermute | solution.py:75
  50.6 7.8 collective-permute-done.7.refs_3_
  58.4 5.4 collective-permute-done.8.refs_4_
  67.9 4.4 collective-permute-start.15
  72.4 28.5 %collective-permute-done.10.refs_3_ = bf16[2,2,2,48,1920]{4,3,2,1,0:T(8,128)(2,1)S(1)} collective-permute-done((bf16[2,2,2,48,1920]{4,3,2,1,0:T(8,128)(2,1)S(1)}, bf16[2,2,2,48,1920]{4,3,2,1,0:T(8,128)(2,1)S(1)}, u32[]{:S(2)}, u32[]{:S(2)}) %collective-permute-start.10) | collective-permute-done | bytes 1474592 | tf_op jit(solution)/shard_map/ppermute | solution.py:75
  110.9 4.5 collective-permute-done.15.refs_1_.refs_3_
  127.3 4.9 shard_map.212
  141.5 4.2 shard_map.214
  146.1 9.7 %collective-permute-done.19.refs_1_ = bf16[224,1152]{1,0:T(8,128)(2,1)S(1)} collective-permute-done((bf16[224,1152]{1,0:T(8,128)(2,1)}, bf16[224,1152]{1,0:T(8,128)(2,1)S(1)}, u32[]{:S(2)}, u32[]{:S(2)}) %collective-permute-start.19) | collective-permute-done | bytes 516128 | tf_op jit(solution)/shard_map/ppermute | solution.py:75
  155.8 4.7 collective-permute-done.18.refs_1_
  171.1 9.1 %collective-permute-done.20.refs_1_ = bf16[2,256,512]{2,1,0:T(8,128)(2,1)} collective-permute-done((bf16[2,256,512]{2,1,0:T(8,128)(2,1)S(1)}, bf16[2,256,512]{2,1,0:T(8,128)(2,1)}, u32[]{:S(2)}, u32[]{:S(2)}) %collective-permute-start.20) | collective-permute-done | bytes 524320 | tf_op jit(solution)/shard_map/ppermute | solution.py:75
  195.7 6.7 shard_map.218
  208.4 19.2 %collective-permute-done.33.refs_3_ = bf16[2,224,512]{2,1,0:T(8,128)(2,1)} collective-permute-done((bf16[2,224,512]{2,1,0:T(8,128)(2,1)}, bf16[2,224,512]{2,1,0:T(8,128)(2,1)}, u32[]{:S(2)}, u32[]{:S(2)}) %collective-permute-start.33) | collective-permute-done | bytes 458784 | tf_op jit(solution)/shard_map/ppermute | solution.py:75
  232.3 5.6 shard_map.221
  240.1 4.3 shard_map.224.wu_ref.refs_7_
  252.8 4.2 collective-permute-done.34
  257.1 4.3 shard_map.226.wd_ref.refs_8_
  261.4 23.1 %shard_map.227 = (f32[512,1152]{1,0:T(8,128)S(1)}, bf16[1024,1792]{1,0:T(8,128)(2,1)}, bf16[1024,1792]{1,0:T(8,128)(2,1)}, bf16[128,1152]{1,0:T(8,128)(2,1)S(1)}...) custom-call(bf16[256,1152]{1,0:T(8,128)(2,1)S(1)} %copy-done.121, ...), custom_call_target="tpu_custom_call" | custom-call | flops 12683575296 | tf_op jit(solution)/shard_map/pallas_call | solution.py:241
  289.8 13.6 %collective-permute-done.41.refs_2_ = bf16[256,1152]{1,0:T(8,128)(2,1)S(1)} collective-permute-done((bf16[256,1152]{1,0:T(8,128)(2,1)S(1)}, bf16[256,1152]{1,0:T(8,128)(2,1)S(1)}, u32[]{:S(2)}, u32[]{:S(2)}) %collective-permute-start.41) | collective-permute-done | bytes 589856 | tf_op jit(solution)/shard_map/ppermute | solution.py:75
  311.4 6.7 collective-permute-done.44.refs_3_
  318.2 14.4 %collective-permute-done.43.refs_2_ = bf16[256,512]{1,0:T(8,128)(2,1)S(1)} collective-permute-done((bf16[256,512]{1,0:T(8,128)(2,1)S(1)}, bf16[256,512]{1,0:T(8,128)(2,1)S(1)}, u32[]{:S(2)}, u32[]{:S(2)}) %collective-permute-start.43) | collective-permute-done | bytes 262176 | tf_op jit(solution)/shard_map/ppermute | solution.py:75
  334.5 5.3 shard_map.231
  344.2 4.9 shard_map.233
  349.1 10.3 %collective-permute-done.49.refs_0_ = bf16[256,1152]{1,0:T(8,128)(2,1)S(1)} collective-permute-done((bf16[256,1152]{1,0:T(8,128)(2,1)S(1)}, bf16[256,1152]{1,0:T(8,128)(2,1)S(1)}, u32[]{:S(2)}, u32[]{:S(2)}) %collective-permute-start.49) | collective-permute-done | bytes 589856 | tf_op jit(solution)/shard_map/ppermute | solution.py:75
  361.5 22.5 %shard_map.235 = (f32[512,1152]{1,0:T(8,128)S(1)}, bf16[1024,1792]{1,0:T(8,128)(2,1)}, bf16[1024,1792]{1,0:T(8,128)(2,1)}, bf16[128,1152]{1,0:T(8,128)(2,1)S(1)}...) custom-call(bf16[256,1152]{1,0:T(8,128)(2,1)S(1)} %get-tuple-element.271.x0_ref.refs_0_, ...), custom_call_target="tpu_custom_call" | custom-call | flops 12683575296 | tf_op jit(solution)/shard_map/pallas_call | solution.py:241
  393.0 30.4 %shard_map.238 = (f32[512,1152]{1,0:T(8,128)}, bf16[1024,1792]{1,0:T(8,128)(2,1)}, bf16[1024,1792]{1,0:T(8,128)(2,1)}, bf16[1792,640]{1,0:T(8,128)(2,1)}, bf16[1...) custom-call(bf16[256,1152]{1,0:T(8,128)(2,1)S(1)} %copy-done.36, ...), custom_call_target="tpu_custom_call" | custom-call | tf_op jit(solution)/shard_map/pallas_call | solution.py:329
  432.2 13.7 %shard_map.240 = (bf16[1152,1792]{1,0:T(8,128)(2,1)}, bf16[1152,1792]{1,0:T(8,128)(2,1)}) custom-call(bf16[256,1152]{1,0:T(8,128)(2,1)S(1)} %copy-done.124, bf16[256,1152]{1,0:T(8,128)(2,1)S(1)} %copy-done.87, bf16[256,1152]{1,0:T(8,128)(2,1)S(1)} %copy-done.126, bf16[256,1152]{1,0:T(8,128)(2,1)S(1)} %copy-done.128, ...), custom_call_target="tpu_custom_call" | custom-call | flops 8455716864 | tf_op jit(solution)/shard_map/pallas_call | solution.py:420
  446.0 4.2 shard_map.241
  451.2 9.8 %shard_map.242 = (bf16[4,256,512]{2,1,0:T(8,128)(2,1)S(1)}, bf16[4,256,512]{2,1,0:T(8,128)(2,1)S(1)}, bf16[256,1024]{1,0:T(8,128)(2,1)S(1)}) custom-call(bf16[256,1024]{1,0:T(8,128)(2,1)S(1)} %copy-done.91, bf16[2048,512]{1,0:T(8,128)(2,1)} %copy-done.136, s32[256,1]{1,0:T(8,128)S(1)} %copy-done.105, s32[256,1]{1,0:T(8,128)S(1)} %copy-done.108, ...), custom_call_target="tpu_custom_call" | custom-call | flops 5368709120 | tf_op jit(solution)/shard_map/pallas_call | solution.py:1443
  466.9 11.8 %collective-permute-done.65.refs_1_ = bf16[2,256,512]{2,1,0:T(8,128)(2,1)S(1)} collective-permute-done((bf16[2,256,512]{2,1,0:T(8,128)(2,1)S(1)}, bf16[2,256,512]{2,1,0:T(8,128)(2,1)S(1)}, u32[]{:S(2)}, u32[]{:S(2)}) %collective-permute-start.65) | collective-permute-done | bytes 524320 | tf_op jit(solution)/shard_map/ppermute | solution.py:75
  485.3 8.1 %collective-permute-done.66.refs_1_ = bf16[256,512]{1,0:T(8,128)(2,1)S(1)} collective-permute-done((bf16[256,512]{1,0:T(8,128)(2,1)S(1)}, bf16[256,512]{1,0:T(8,128)(2,1)S(1)}, u32[]{:S(2)}, u32[]{:S(2)}) %collective-permute-start.66) | collective-permute-done | bytes 262176 | tf_op jit(solution)/shard_map/ppermute | solution.py:75
  496.2 4.2 shard_map.248
  501.4 14.0 %collective-permute-done.71.refs_1_ = bf16[256,1152]{1,0:T(8,128)(2,1)S(1)} collective-permute-done((bf16[256,1152]{1,0:T(8,128)(2,1)S(1)}, bf16[256,1152]{1,0:T(8,128)(2,1)S(1)}, u32[]{:S(2)}, u32[]{:S(2)}) %collective-permute-start.71) | collective-permute-done | bytes 589856 | tf_op jit(solution)/shard_map/ppermute | solution.py:75
  517.4 30.6 %shard_map.249 = (f32[512,1152]{1,0:T(8,128)}, bf16[1024,1792]{1,0:T(8,128)(2,1)}, bf16[1024,1792]{1,0:T(8,128)(2,1)}, bf16[1792,640]{1,0:T(8,128)(2,1)}, bf16[1...) custom-call(bf16[256,1152]{1,0:T(8,128)(2,1)S(1)} %get-tuple-element, ...), custom_call_target="tpu_custom_call" | custom-call | tf_op jit(solution)/shard_map/pallas_call | solution.py:329
  566.2 16.1 %shard_map.252 = (bf16[2,2,144,1792]{3,2,1,0:T(8,128)(2,1)S(1)}, bf16[2,2,144,1792]{3,2,1,0:T(8,128)(2,1)}, bf16[2,2,144,1792]{3,2,1,0:T(8,128)(2,1)}, bf16[2,2,144,1792]{3,2,1,0:T(8,128)(2,1)}) custom-call(s32[5]{0:T(128)S(1)} %stack.23.refs_0_.coords_ref.refs_9_, bf16[256,1152]{1,0:T(8,128)(2,1)S(1)} %copy-done.122, bf16[256,1152]{1,0:T(8,128)(2,1)S(1)} %copy-done.85, ...), custom_call_target="tpu_custom_call" | custom-call | flops 8455716864 | tf_op jit(solution)/shard_map/pallas_call | solution.py:420
  597.7 10.0 %shard_map.255 = (bf16[4,256,512]{2,1,0:T(8,128)(2,1)S(1)}, bf16[4,256,512]{2,1,0:T(8,128)(2,1)S(1)}, bf16[256,1024]{1,0:T(8,128)(2,1)S(1)}) custom-call(bf16[256,1024]{1,0:T(8,128)(2,1)S(1)} %copy-done.43, bf16[2048,512]{1,0:T(8,128)(2,1)} %copy-done.135, s32[256,1]{1,0:T(8,128)S(1)} %copy-done.106, s32[256,1]{1,0:T(8,128)S(1)} %copy-done.109, ...), custom_call_target="tpu_custom_call" | custom-call | flops 5368709120 | tf_op jit(solution)/shard_map/pallas_call | solution.py:1443
  616.2 9.1 %collective-permute-done.82.refs_1_ = bf16[2,256,512]{2,1,0:T(8,128)(2,1)S(1)} collective-permute-done((bf16[2,256,512]{2,1,0:T(8,128)(2,1)S(1)}, bf16[2,256,512]{2,1,0:T(8,128)(2,1)S(1)}, u32[]{:S(2)}, u32[]{:S(2)}) %collective-permute-start.82) | collective-permute-done | bytes 524320 | tf_op jit(solution)/shard_map/ppermute | solution.py:75
  635.0 4.5 shard_map.259
  645.2 5.6 shard_map.262
  657.5 5.2 shard_map.264
  670.0 12.4 %collective-permute-done.95.refs_1_ = bf16[224,640]{1,0:T(8,128)(2,1)S(1)} collective-permute-done((bf16[224,640]{1,0:T(8,128)(2,1)S(1)}, bf16[224,640]{1,0:T(8,128)(2,1)S(1)}, u32[]{:S(2)}, u32[]{:S(2)}) %collective-permute-start.95) | collective-permute-done | bytes 286752 | tf_op jit(solution)/shard_map/ppermute | solution.py:75
  684.7 18.0 %collective-permute-done.93.refs_2_ = bf16[2,144,1792]{2,1,0:T(8,128)(2,1)S(1)} collective-permute-done((bf16[2,144,1792]{2,1,0:T(8,128)(2,1)S(1)}, bf16[2,144,1792]{2,1,0:T(8,128)(2,1)S(1)}, u32[]{:S(2)}, u32[]{:S(2)}) %collective-permute-start.93) | collective-permute-done | bytes 1032224 | tf_op jit(solution)/shard_map/ppermute | solution.py:75
  715.5 30.4 %collective-permute-done.103.refs_2_ = bf16[144,1792]{1,0:T(8,128)(2,1)S(1)} collective-permute-done((bf16[144,1792]{1,0:T(8,128)(2,1)S(1)}, bf16[144,1792]{1,0:T(8,128)(2,1)S(1)}, u32[]{:S(2)}, u32[]{:S(2)}) %collective-permute-start.103) | collective-permute-done | bytes 516128 | tf_op jit(solution)/shard_map/ppermute | solution.py:75
  745.9 9.7 %collective-permute-done.104.refs_4_ = bf16[144,1792]{1,0:T(8,128)(2,1)S(1)} collective-permute-done((bf16[144,1792]{1,0:T(8,128)(2,1)S(1)}, bf16[144,1792]{1,0:T(8,128)(2,1)S(1)}, u32[]{:S(2)}, u32[]{:S(2)}) %collective-permute-start.104) | collective-permute-done | bytes 516128 | tf_op jit(solution)/shard_map/ppermute | solution.py:75
  761.8 16.2 %collective-permute-done.107.refs_5_ = bf16[2,56,768]{2,1,0:T(8,128)(2,1)S(1)} collective-permute-done((bf16[2,56,768]{2,1,0:T(8,128)(2,1)S(1)}, bf16[2,56,768]{2,1,0:T(8,128)(2,1)S(1)}, u32[]{:S(2)}, u32[]{:S(2)}) %collective-permute-start.107) | collective-permute-done | bytes 172064 | tf_op jit(solution)/shard_map/ppermute | solution.py:75
  782.0 5.4 collective-permute-done.112.p2_ref
  787.4 5.4 collective-permute-done.113.p3_ref
  (556 shorter events, 263.9 us)
Async XLA Ops:
  6.4 21.1 %collective-permute-start = (bf16[48,2048]{1,0:T(8,128)(2,1)S(1)}, bf16[48,2048]{1,0:T(8,128)(2,1)S(1)}, u32[]{:S(2)}, u32[]{:S(2)}) collective-permute-start(bf16[48,2048]{1,0:T(8,128)(2,1)S(1)} %get-tuple-element.210.refs_0_), channel_id=1, source_target_pairs={{0,4},{1,5},{2,6},{3,7},{4,0},{5,1},{6,2},{7,3},{8,12},{9,13},{10,... | collective-permute-start | bytes 589832 | tf_op jit(solution)/shard_map/ppermute | solution.py:75
  65.9 36.7 %collective-permute-start.9 = (bf16[2,2,2,48,2048]{4,3,2,1,0:T(8,128)(2,1)}, bf16[2,2,2,48,2048]{4,3,2,1,0:T(8,128)(2,1)S(1)}, u32[]{:S(2)}, u32[]{:S(2)}) collective-permute-start(bf16[2,2,2,48,2048]{4,3,2,1,0:T(8,128)(2,1)} %get-tuple-element.220.refs_0_), channel_id=1, source_target_pairs={{0,16},{1,17},{2,18},{3,19},{4,20},{5,21},{6,22},{7,23},{8,24},{9,... | collective-permute-start | bytes 4718600 | tf_op jit(solution)/shard_map/ppermute | solution.py:75
  66.6 34.3 %collective-permute-start.10 = (bf16[2,2,2,48,1920]{4,3,2,1,0:T(8,128)(2,1)S(1)}, bf16[2,2,2,48,1920]{4,3,2,1,0:T(8,128)(2,1)S(1)}, u32[]{:S(2)}, u32[]{:S(2)}) collective-permute-start(bf16[2,2,2,48,1920]{4,3,2,1,0:T(8,128)(2,1)S(1)} %get-tuple-element.221.refs_2_), channel_id=1, source_target_pairs={{0,8},{1,9},{2,10},{3,11},{4,12},{5,13},{6,14},{7,15},{8,0},{9,1},... | collective-permute-start | bytes 4423688 | tf_op jit(solution)/shard_map/ppermute | solution.py:75
  67.9 47.5 %collective-permute-start.15 = (bf16[2,144,1792]{2,1,0:T(8,128)(2,1)S(1)}, bf16[2,144,1792]{2,1,0:T(8,128)(2,1)S(1)}, u32[]{:S(2)}, u32[]{:S(2)}) collective-permute-start(bf16[2,144,1792]{2,1,0:T(8,128)(2,1)S(1)} %shard_map.208.refs_4_.refs_0_.refs_2_), channel_id=1, source_target_pairs={{0,4},{1,5},{2,6},{3,7},{4,0},{5,1},{6,2},{7,3},{8,12},{9,13},{10,... | collective-permute-start | bytes 3096584 | tf_op jit(solution)/shard_map/ppermute | solution.py:75
  116.6 23.9 %collective-permute-start.17 = (bf16[2,144,1792]{2,1,0:T(8,128)(2,1)}, bf16[2,144,1792]{2,1,0:T(8,128)(2,1)}, u32[]{:S(2)}, u32[]{:S(2)}) collective-permute-start(bf16[2,144,1792]{2,1,0:T(8,128)(2,1)} %get-tuple-element.233.refs_2_), channel_id=1, source_target_pairs={{0,16},{1,17},{2,18},{3,19},{4,20},{5,21},{6,22},{7,23},{8,24},{9,... | collective-permute-start | bytes 3096584 | tf_op jit(solution)/shard_map/ppermute | solution.py:75
  118.0 23.4 %collective-permute-start.16 = (bf16[2,144,1792]{2,1,0:T(8,128)(2,1)S(1)}, bf16[2,144,1792]{2,1,0:T(8,128)(2,1)}, u32[]{:S(2)}, u32[]{:S(2)}) collective-permute-start(bf16[2,144,1792]{2,1,0:T(8,128)(2,1)S(1)} %get-tuple-element.226.refs_9_.refs_0_), channel_id=1, source_target_pairs={{0,8},{1,9},{2,10},{3,11},{4,12},{5,13},{6,14},{7,15},{8,0},{9,1},... | collective-permute-start | bytes 3096584 | tf_op jit(solution)/shard_map/ppermute | solution.py:75
  123.4 32.4 %collective-permute-start.19 = (bf16[224,1152]{1,0:T(8,128)(2,1)}, bf16[224,1152]{1,0:T(8,128)(2,1)S(1)}, u32[]{:S(2)}, u32[]{:S(2)}) collective-permute-start(bf16[224,1152]{1,0:T(8,128)(2,1)} %copy-done.94), channel_id=1, source_target_pairs={{0,4},{1,5},{2,6},{3,7},{4,0},{5,1},{6,2},{7,3},{8,12},{9,13},{10,... | collective-permute-start | bytes 1548296 | tf_op jit(solution)/shard_map/ppermute | solution.py:75
  124.0 43.6 %collective-permute-start.23 = (bf16[2,2,2,2,48,512]{5,4,3,2,1,0:T(8,128)(2,1)}, bf16[2,2,2,2,48,512]{5,4,3,2,1,0:T(8,128)(2,1)S(1)}, u32[]{:S(2)}, u32[]{:S(2)}) collective-permute-start(bf16[2,2,2,2,48,512]{5,4,3,2,1,0:T(8,128)(2,1)} %copy-done.70), channel_id=1, source_target_pairs={{0,1},{1,0},{2,3},{3,2},{4,5},{5,4},{6,7},{7,6},{8,9},{9,8},{10,11... | collective-permute-start | bytes 2359304 | tf_op jit(solution)/shard_map/ppermute | solution.py:75
  145.6 21.2 %collective-permute-start.26 = (bf16[2,2,2,2,48,256]{5,4,3,2,1,0:T(8,128)(2,1)S(1)}, bf16[2,2,2,2,48,256]{5,4,3,2,1,0:T(8,128)(2,1)S(1)}, u32[]{:S(2)}, u32[]{:S(2)}) collective-permute-start(bf16[2,2,2,2,48,256]{5,4,3,2,1,0:T(8,128)(2,1)S(1)} %copy-done.100), channel_id=1, source_target_pairs={{0,1},{1,0},{2,3},{3,2},{4,5},{5,4},{6,7},{7,6},{8,9},{9,8},{10,11... | collective-permute-start | bytes 1179656 | tf_op jit(solution)/shard_map/ppermute | solution.py:75
  145.6 23.7 %collective-permute-start.25 = (bf16[2,2,2,2,48,512]{5,4,3,2,1,0:T(8,128)(2,1)S(1)}, bf16[2,2,2,2,48,512]{5,4,3,2,1,0:T(8,128)(2,1)S(1)}, u32[]{:S(2)}, u32[]{:S(2)}) collective-permute-start(bf16[2,2,2,2,48,512]{5,4,3,2,1,0:T(8,128)(2,1)S(1)} %copy-done.73), channel_id=1, source_target_pairs={{0,1},{1,0},{2,3},{3,2},{4,5},{5,4},{6,7},{7,6},{8,9},{9,8},{10,11... | collective-permute-start | bytes 2359304 | tf_op jit(solution)/shard_map/ppermute | solution.py:75
  155.8 24.3 %collective-permute-start.24 = (bf16[2,2,2,2,48,640]{5,4,3,2,1,0:T(8,128)(2,1)S(1)}, bf16[2,2,2,2,48,640]{5,4,3,2,1,0:T(8,128)(2,1)S(1)}, u32[]{:S(2)}, u32[]{:S(2)}) collective-permute-start(bf16[2,2,2,2,48,640]{5,4,3,2,1,0:T(8,128)(2,1)S(1)} %copy-done.61), channel_id=1, source_target_pairs={{0,1},{1,0},{2,3},{3,2},{4,5},{5,4},{6,7},{7,6},{8,9},{9,8},{10,11... | collective-permute-start | bytes 2949128 | tf_op jit(solution)/shard_map/ppermute | solution.py:75
  160.5 77.5 %collective-permute-start.31 = (bf16[2,2,144,1792]{3,2,1,0:T(8,128)(2,1)}, bf16[2,2,144,1792]{3,2,1,0:T(8,128)(2,1)}, u32[]{:S(2)}, u32[]{:S(2)}) collective-permute-start(bf16[2,2,144,1792]{3,2,1,0:T(8,128)(2,1)} %get-tuple-element.252), channel_id=1, source_target_pairs={{0,8},{1,9},{2,10},{3,11},{4,12},{5,13},{6,14},{7,15},{8,0},{9,1},... | collective-permute-start | bytes 6193160 | tf_op jit(solution)/shard_map/ppermute | solution.py:75
  170.3 74.1 %collective-permute-start.30 = (bf16[2,2,144,1792]{3,2,1,0:T(8,128)(2,1)S(1)}, bf16[2,2,144,1792]{3,2,1,0:T(8,128)(2,1)}, u32[]{:S(2)}, u32[]{:S(2)}) collective-permute-start(bf16[2,2,144,1792]{3,2,1,0:T(8,128)(2,1)S(1)} %copy-done.4), channel_id=1, source_target_pairs={{0,16},{1,17},{2,18},{3,19},{4,20},{5,21},{6,22},{7,23},{8,24},{9,... | collective-permute-start | bytes 6193160 | tf_op jit(solution)/shard_map/ppermute | solution.py:75
  180.2 47.4 %collective-permute-start.32 = (bf16[2,224,640]{2,1,0:T(8,128)(2,1)}, bf16[2,224,640]{2,1,0:T(8,128)(2,1)}, u32[]{:S(2)}, u32[]{:S(2)}) collective-permute-start(bf16[2,224,640]{2,1,0:T(8,128)(2,1)} %get-tuple-element.238.refs_2_.refs_0_), channel_id=1, source_target_pairs={{0,8},{1,9},{2,10},{3,11},{4,12},{5,13},{6,14},{7,15},{8,0},{9,1},... | collective-permute-start | bytes 1720328 | tf_op jit(solution)/shard_map/ppermute | solution.py:75
  182.8 44.8 %collective-permute-start.33 = (bf16[2,224,512]{2,1,0:T(8,128)(2,1)}, bf16[2,224,512]{2,1,0:T(8,128)(2,1)}, u32[]{:S(2)}, u32[]{:S(2)}) collective-permute-start(bf16[2,224,512]{2,1,0:T(8,128)(2,1)} %get-tuple-element.253.refs_2_), channel_id=1, source_target_pairs={{0,16},{1,17},{2,18},{3,19},{4,20},{5,21},{6,22},{7,23},{8,24},{9,... | collective-permute-start | bytes 1376264 | tf_op jit(solution)/shard_map/ppermute | solution.py:75
  208.1 29.8 %collective-permute-start.27 = (bf16[256,1152]{1,0:T(8,128)(2,1)S(1)}, bf16[256,1152]{1,0:T(8,128)(2,1)S(1)}, u32[]{:S(2)}, u32[]{:S(2)}) collective-permute-start(bf16[256,1152]{1,0:T(8,128)(2,1)S(1)} %get-tuple-element.249.x0_ref.refs_1_), channel_id=1, source_target_pairs={{0,2},{1,3},{2,0},{3,1},{4,6},{5,7},{6,4},{7,5},{8,10},{9,11},{10,... | collective-permute-start | bytes 1769480 | tf_op jit(solution)/shard_map/ppermute | solution.py:75
  230.0 27.0 %collective-permute-start.34 = (bf16[2,2,224,640]{3,2,1,0:T(8,128)(2,1)S(1)}, bf16[2,2,224,640]{3,2,1,0:T(8,128)(2,1)}, u32[]{:S(2)}, u32[]{:S(2)}) collective-permute-start(bf16[2,2,224,640]{3,2,1,0:T(8,128)(2,1)S(1)} %get-tuple-element.254), channel_id=1, source_target_pairs={{0,16},{1,17},{2,18},{3,19},{4,20},{5,21},{6,22},{7,23},{8,24},{9,... | collective-permute-start | bytes 3440648 | tf_op jit(solution)/shard_map/ppermute | solution.py:75
  230.8 22.0 %collective-permute-start.35 = (bf16[2,2,224,512]{3,2,1,0:T(8,128)(2,1)}, bf16[2,2,224,512]{3,2,1,0:T(8,128)(2,1)}, u32[]{:S(2)}, u32[]{:S(2)}) collective-permute-start(bf16[2,2,224,512]{3,2,1,0:T(8,128)(2,1)} %get-tuple-element.255), channel_id=1, source_target_pairs={{0,8},{1,9},{2,10},{3,11},{4,12},{5,13},{6,14},{7,15},{8,0},{9,1},... | collective-permute-start | bytes 2752520 | tf_op jit(solution)/shard_map/ppermute | solution.py:75
  237.9 23.5 %collective-permute-start.28 = (bf16[256,1152]{1,0:T(8,128)(2,1)S(1)}, bf16[256,1152]{1,0:T(8,128)(2,1)}, u32[]{:S(2)}, u32[]{:S(2)}) collective-permute-start(bf16[256,1152]{1,0:T(8,128)(2,1)S(1)} %get-tuple-element.249.x0_ref.refs_1_), channel_id=1, source_target_pairs={{0,1},{1,0},{2,3},{3,2},{4,5},{5,4},{6,7},{7,6},{8,9},{9,8},{10,11... | collective-permute-start | bytes 1769480 | tf_op jit(solution)/shard_map/ppermute | solution.py:75
  238.0 23.4 %collective-permute-start.29 = (bf16[256,1152]{1,0:T(8,128)(2,1)S(1)}, bf16[256,1152]{1,0:T(8,128)(2,1)}, u32[]{:S(2)}, u32[]{:S(2)}) collective-permute-start(bf16[256,1152]{1,0:T(8,128)(2,1)S(1)} %shard_map.222.x1_ref.refs_2_), channel_id=1, source_target_pairs={{0,1},{1,0},{2,3},{3,2},{4,5},{5,4},{6,7},{7,6},{8,9},{9,8},{10,11... | collective-permute-start | bytes 1769480 | tf_op jit(solution)/shard_map/ppermute | solution.py:75
  244.4 41.1 %collective-permute-start.40 = (bf16[256,1152]{1,0:T(8,128)(2,1)S(1)}, bf16[256,1152]{1,0:T(8,128)(2,1)S(1)}, u32[]{:S(2)}, u32[]{:S(2)}) collective-permute-start(bf16[256,1152]{1,0:T(8,128)(2,1)S(1)} %copy-done.35), channel_id=1, source_target_pairs={{0,2},{1,3},{2,0},{3,1},{4,6},{5,7},{6,4},{7,5},{8,10},{9,11},{10,... | collective-permute-start | bytes 1769480 | tf_op jit(solution)/shard_map/ppermute | solution.py:75
  308.2 24.4 %collective-permute-start.43 = (bf16[256,512]{1,0:T(8,128)(2,1)S(1)}, bf16[256,512]{1,0:T(8,128)(2,1)S(1)}, u32[]{:S(2)}, u32[]{:S(2)}) collective-permute-start(bf16[256,512]{1,0:T(8,128)(2,1)S(1)} %get-tuple-element.266.refs_0_), channel_id=1, source_target_pairs={{0,4},{1,5},{2,6},{3,7},{4,0},{5,1},{6,2},{7,3},{8,12},{9,13},{10,... | collective-permute-start | bytes 786440 | tf_op jit(solution)/shard_map/ppermute | solution.py:75
  310.3 22.4 %collective-permute-start.42 = (bf16[256,512]{1,0:T(8,128)(2,1)S(1)}, bf16[256,512]{1,0:T(8,128)(2,1)S(1)}, u32[]{:S(2)}, u32[]{:S(2)}) collective-permute-start(bf16[256,512]{1,0:T(8,128)(2,1)S(1)} %get-tuple-element.266.refs_0_), channel_id=1, source_target_pairs={{0,2},{1,3},{2,0},{3,1},{4,6},{5,7},{6,4},{7,5},{8,10},{9,11},{10,... | collective-permute-start | bytes 786440 | tf_op jit(solution)/shard_map/ppermute | solution.py:75
  311.4 22.7 %collective-permute-start.45 = (bf16[256,512]{1,0:T(8,128)(2,1)S(1)}, bf16[256,512]{1,0:T(8,128)(2,1)S(1)}, u32[]{:S(2)}, u32[]{:S(2)}) collective-permute-start(bf16[256,512]{1,0:T(8,128)(2,1)S(1)} %get-tuple-element.266.refs_0_), channel_id=1, source_target_pairs={{0,1},{1,0},{2,3},{3,2},{4,5},{5,4},{6,7},{7,6},{8,9},{9,8},{10,11... | collective-permute-start | bytes 786440 | tf_op jit(solution)/shard_map/ppermute | solution.py:75
  392.6 33.0 %collective-permute-start.56 = (bf16[256,1152]{1,0:T(8,128)(2,1)}, bf16[256,1152]{1,0:T(8,128)(2,1)S(1)}, u32[]{:S(2)}, u32[]{:S(2)}) collective-permute-start(bf16[256,1152]{1,0:T(8,128)(2,1)} %get-tuple-element.280), channel_id=1, source_target_pairs={{0,2},{1,3},{2,0},{3,1},{4,6},{5,7},{6,4},{7,5},{8,10},{9,11},{10,... | collective-permute-start | bytes 1769480 | tf_op jit(solution)/shard_map/ppermute | solution.py:75
  461.6 23.7 %collective-permute-start.70 = (bf16[256,1664]{1,0:T(8,128)(2,1)}, bf16[256,1664]{1,0:T(8,128)(2,1)S(1)}, u32[]{:S(2)}, u32[]{:S(2)}) collective-permute-start(bf16[256,1664]{1,0:T(8,128)(2,1)} %get-tuple-element.251.refs_1_), channel_id=1, source_target_pairs={{0,1},{1,0},{2,3},{3,2},{4,5},{5,4},{6,7},{7,6},{8,9},{9,8},{10,11... | collective-permute-start | bytes 2555912 | tf_op jit(solution)/shard_map/ppermute | solution.py:75
  554.9 39.1 %collective-permute-start.79 = (bf16[2,2,224,640]{3,2,1,0:T(8,128)(2,1)}, bf16[2,2,224,640]{3,2,1,0:T(8,128)(2,1)}, u32[]{:S(2)}, u32[]{:S(2)}) collective-permute-start(bf16[2,2,224,640]{3,2,1,0:T(8,128)(2,1)} %get-tuple-element.331), channel_id=1, source_target_pairs={{0,8},{1,9},{2,10},{3,11},{4,12},{5,13},{6,14},{7,15},{8,0},{9,1},... | collective-permute-start | bytes 3440648 | tf_op jit(solution)/shard_map/ppermute | solution.py:75
  557.0 37.0 %collective-permute-start.80 = (bf16[2,2,224,512]{3,2,1,0:T(8,128)(2,1)}, bf16[2,2,224,512]{3,2,1,0:T(8,128)(2,1)}, u32[]{:S(2)}, u32[]{:S(2)}) collective-permute-start(bf16[2,2,224,512]{3,2,1,0:T(8,128)(2,1)} %get-tuple-element.333), channel_id=1, source_target_pairs={{0,16},{1,17},{2,18},{3,19},{4,20},{5,21},{6,22},{7,23},{8,24},{9,... | collective-permute-start | bytes 2752520 | tf_op jit(solution)/shard_map/ppermute | solution.py:75
  562.5 22.4 %collective-permute-start.78 = (bf16[256,1152]{1,0:T(8,128)(2,1)}, bf16[256,1152]{1,0:T(8,128)(2,1)S(1)}, u32[]{:S(2)}, u32[]{:S(2)}) collective-permute-start(bf16[256,1152]{1,0:T(8,128)(2,1)} %get-tuple-element.324), channel_id=1, source_target_pairs={{0,2},{1,3},{2,0},{3,1},{4,6},{5,7},{6,4},{7,5},{8,10},{9,11},{10,... | collective-permute-start | bytes 1769480 | tf_op jit(solution)/shard_map/ppermute | solution.py:75
  583.6 61.3 %collective-permute-start.84 = (bf16[2,2,144,1792]{3,2,1,0:T(8,128)(2,1)}, bf16[2,2,144,1792]{3,2,1,0:T(8,128)(2,1)}, u32[]{:S(2)}, u32[]{:S(2)}) collective-permute-start(bf16[2,2,144,1792]{3,2,1,0:T(8,128)(2,1)} %get-tuple-element.342), channel_id=1, source_target_pairs={{0,8},{1,9},{2,10},{3,11},{4,12},{5,13},{6,14},{7,15},{8,0},{9,1},... | collective-permute-start | bytes 6193160 | tf_op jit(solution)/shard_map/ppermute | solution.py:75
  584.1 60.8 %collective-permute-start.85 = (bf16[2,2,144,1792]{3,2,1,0:T(8,128)(2,1)}, bf16[2,2,144,1792]{3,2,1,0:T(8,128)(2,1)}, u32[]{:S(2)}, u32[]{:S(2)}) collective-permute-start(bf16[2,2,144,1792]{3,2,1,0:T(8,128)(2,1)} %get-tuple-element.344), channel_id=1, source_target_pairs={{0,16},{1,17},{2,18},{3,19},{4,20},{5,21},{6,22},{7,23},{8,24},{9,... | collective-permute-start | bytes 6193160 | tf_op jit(solution)/shard_map/ppermute | solution.py:75
  614.9 30.0 %collective-permute-start.86 = (bf16[2,224,640]{2,1,0:T(8,128)(2,1)}, bf16[2,224,640]{2,1,0:T(8,128)(2,1)S(1)}, u32[]{:S(2)}, u32[]{:S(2)}) collective-permute-start(bf16[2,224,640]{2,1,0:T(8,128)(2,1)} %get-tuple-element.345), channel_id=1, source_target_pairs={{0,16},{1,17},{2,18},{3,19},{4,20},{5,21},{6,22},{7,23},{8,24},{9,... | collective-permute-start | bytes 1720328 | tf_op jit(solution)/shard_map/ppermute | solution.py:75
  628.0 28.0 %collective-permute-start.83 = (bf16[256,512]{1,0:T(8,128)(2,1)}, bf16[256,512]{1,0:T(8,128)(2,1)}, u32[]{:S(2)}, u32[]{:S(2)}) collective-permute-start(bf16[256,512]{1,0:T(8,128)(2,1)} %get-tuple-element.340), channel_id=1, source_target_pairs={{0,4},{1,5},{2,6},{3,7},{4,0},{5,1},{6,2},{7,3},{8,12},{9,13},{10,... | collective-permute-start | bytes 786440 | tf_op jit(solution)/shard_map/ppermute | solution.py:75
  644.2 62.5 %collective-permute-start.91 = (bf16[2,2,2,48,1664]{4,3,2,1,0:T(8,128)(2,1)}, bf16[2,2,2,48,1664]{4,3,2,1,0:T(8,128)(2,1)}, u32[]{:S(2)}, u32[]{:S(2)}) collective-permute-start(bf16[2,2,2,48,1664]{4,3,2,1,0:T(8,128)(2,1)} %get-tuple-element.360), channel_id=1, source_target_pairs={{0,8},{1,9},{2,10},{3,11},{4,12},{5,13},{6,14},{7,15},{8,0},{9,1},... | collective-permute-start | bytes 3833864 | tf_op jit(solution)/shard_map/ppermute | solution.py:75
  654.6 52.0 %collective-permute-start.92 = (bf16[2,2,2,56,1280]{4,3,2,1,0:T(8,128)(2,1)}, bf16[2,2,2,56,1280]{4,3,2,1,0:T(8,128)(2,1)S(1)}, u32[]{:S(2)}, u32[]{:S(2)}) collective-permute-start(bf16[2,2,2,56,1280]{4,3,2,1,0:T(8,128)(2,1)} %copy-done.117), channel_id=1, source_target_pairs={{0,16},{1,17},{2,18},{3,19},{4,20},{5,21},{6,22},{7,23},{8,24},{9,... | collective-permute-start | bytes 3440648 | tf_op jit(solution)/shard_map/ppermute | solution.py:75
  665.5 37.3 %collective-permute-start.93 = (bf16[2,144,1792]{2,1,0:T(8,128)(2,1)S(1)}, bf16[2,144,1792]{2,1,0:T(8,128)(2,1)S(1)}, u32[]{:S(2)}, u32[]{:S(2)}) collective-permute-start(bf16[2,144,1792]{2,1,0:T(8,128)(2,1)S(1)} %copy-done.119), channel_id=1, source_target_pairs={{0,16},{1,17},{2,18},{3,19},{4,20},{5,21},{6,22},{7,23},{8,24},{9,... | collective-permute-start | bytes 3096584 | tf_op jit(solution)/shard_map/ppermute | solution.py:75
  666.9 35.8 %collective-permute-start.94 = (bf16[2,144,1792]{2,1,0:T(8,128)(2,1)}, bf16[2,144,1792]{2,1,0:T(8,128)(2,1)S(1)}, u32[]{:S(2)}, u32[]{:S(2)}) collective-permute-start(bf16[2,144,1792]{2,1,0:T(8,128)(2,1)} %get-tuple-element.365), channel_id=1, source_target_pairs={{0,8},{1,9},{2,10},{3,11},{4,12},{5,13},{6,14},{7,15},{8,0},{9,1},... | collective-permute-start | bytes 3096584 | tf_op jit(solution)/shard_map/ppermute | solution.py:75
  682.4 31.6 %collective-permute-start.101 = (bf16[2,2,2,56,768]{4,3,2,1,0:T(8,128)(2,1)S(1)}, bf16[2,2,2,56,768]{4,3,2,1,0:T(8,128)(2,1)S(1)}, u32[]{:S(2)}, u32[]{:S(2)}) collective-permute-start(bf16[2,2,2,56,768]{4,3,2,1,0:T(8,128)(2,1)S(1)} %get-tuple-element.380), channel_id=1, source_target_pairs={{0,8},{1,9},{2,10},{3,11},{4,12},{5,13},{6,14},{7,15},{8,0},{9,1},... | collective-permute-start | bytes 2064392 | tf_op jit(solution)/shard_map/ppermute | solution.py:75
  708.9 47.9 %collective-permute-start.99 = (bf16[2,2,48,1664]{3,2,1,0:T(8,128)(2,1)S(1)}, bf16[2,2,48,1664]{3,2,1,0:T(8,128)(2,1)S(1)}, u32[]{:S(2)}, u32[]{:S(2)}) collective-permute-start(bf16[2,2,48,1664]{3,2,1,0:T(8,128)(2,1)S(1)} %get-tuple-element.377), channel_id=1, source_target_pairs={{0,16},{1,17},{2,18},{3,19},{4,20},{5,21},{6,22},{7,23},{8,24},{9,... | collective-permute-start | bytes 1916936 | tf_op jit(solution)/shard_map/ppermute | solution.py:75
  710.3 46.5 %collective-permute-start.100 = (bf16[2,2,56,1280]{3,2,1,0:T(8,128)(2,1)S(1)}, bf16[2,2,56,1280]{3,2,1,0:T(8,128)(2,1)S(1)}, u32[]{:S(2)}, u32[]{:S(2)}) collective-permute-start(bf16[2,2,56,1280]{3,2,1,0:T(8,128)(2,1)S(1)} %get-tuple-element.379), channel_id=1, source_target_pairs={{0,8},{1,9},{2,10},{3,11},{4,12},{5,13},{6,14},{7,15},{8,0},{9,1},... | collective-permute-start | bytes 1720328 | tf_op jit(solution)/shard_map/ppermute | solution.py:75
  711.1 34.8 %collective-permute-start.103 = (bf16[144,1792]{1,0:T(8,128)(2,1)S(1)}, bf16[144,1792]{1,0:T(8,128)(2,1)S(1)}, u32[]{:S(2)}, u32[]{:S(2)}) collective-permute-start(bf16[144,1792]{1,0:T(8,128)(2,1)S(1)} %get-tuple-element.383), channel_id=1, source_target_pairs={{0,4},{1,5},{2,6},{3,7},{4,0},{5,1},{6,2},{7,3},{8,12},{9,13},{10,... | collective-permute-start | bytes 1548296 | tf_op jit(solution)/shard_map/ppermute | solution.py:75
  713.0 42.6 %collective-permute-start.104 = (bf16[144,1792]{1,0:T(8,128)(2,1)S(1)}, bf16[144,1792]{1,0:T(8,128)(2,1)S(1)}, u32[]{:S(2)}, u32[]{:S(2)}) collective-permute-start(bf16[144,1792]{1,0:T(8,128)(2,1)S(1)} %get-tuple-element.385), channel_id=1, source_target_pairs={{0,4},{1,5},{2,6},{3,7},{4,0},{5,1},{6,2},{7,3},{8,12},{9,13},{10,... | collective-permute-start | bytes 1548296 | tf_op jit(solution)/shard_map/ppermute | solution.py:75
  714.7 42.0 %collective-permute-start.102 = (bf16[2,2,56,768]{3,2,1,0:T(8,128)(2,1)S(1)}, bf16[2,2,56,768]{3,2,1,0:T(8,128)(2,1)S(1)}, u32[]{:S(2)}, u32[]{:S(2)}) collective-permute-start(bf16[2,2,56,768]{3,2,1,0:T(8,128)(2,1)S(1)} %get-tuple-element.382), channel_id=1, source_target_pairs={{0,16},{1,17},{2,18},{3,19},{4,20},{5,21},{6,22},{7,23},{8,24},{9,... | collective-permute-start | bytes 1032200 | tf_op jit(solution)/shard_map/ppermute | solution.py:75
  757.7 20.4 %collective-permute-start.105 = (bf16[2,48,1664]{2,1,0:T(8,128)(2,1)S(1)}, bf16[2,48,1664]{2,1,0:T(8,128)(2,1)S(1)}, u32[]{:S(2)}, u32[]{:S(2)}) collective-permute-start(bf16[2,48,1664]{2,1,0:T(8,128)(2,1)S(1)} %get-tuple-element.388), channel_id=1, source_target_pairs={{0,2},{1,3},{2,0},{3,1},{4,6},{5,7},{6,4},{7,5},{8,10},{9,11},{10,... | collective-permute-start | bytes 958472 | tf_op jit(solution)/shard_map/ppermute | solution.py:75
  757.8 20.3 %collective-permute-start.106 = (bf16[2,56,1280]{2,1,0:T(8,128)(2,1)S(1)}, bf16[2,56,1280]{2,1,0:T(8,128)(2,1)S(1)}, u32[]{:S(2)}, u32[]{:S(2)}) collective-permute-start(bf16[2,56,1280]{2,1,0:T(8,128)(2,1)S(1)} %get-tuple-element.390), channel_id=1, source_target_pairs={{0,2},{1,3},{2,0},{3,1},{4,6},{5,7},{6,4},{7,5},{8,10},{9,11},{10,... | collective-permute-start | bytes 860168 | tf_op jit(solution)/shard_map/ppermute | solution.py:75
  759.9 21.9 %collective-permute-start.111 = (bf16[2,36,1792]{2,1,0:T(8,128)(2,1)S(1)}, bf16[2,36,1792]{2,1,0:T(8,128)(2,1)S(1)}, u32[]{:S(2)}, u32[]{:S(2)}) collective-permute-start(bf16[2,36,1792]{2,1,0:T(8,128)(2,1)S(1)} %get-tuple-element.402), channel_id=1, source_target_pairs={{0,1},{1,0},{2,3},{3,2},{4,5},{5,4},{6,7},{7,6},{8,9},{9,8},{10,11... | collective-permute-start | bytes 774152 | tf_op jit(solution)/shard_map/ppermute | solution.py:75
  759.9 27.5 %collective-permute-start.112 = (bf16[2,36,1792]{2,1,0:T(8,128)(2,1)S(1)}, bf16[2,36,1792]{2,1,0:T(8,128)(2,1)S(1)}, u32[]{:S(2)}, u32[]{:S(2)}) collective-permute-start(bf16[2,36,1792]{2,1,0:T(8,128)(2,1)S(1)} %get-tuple-element.403), channel_id=1, source_target_pairs={{0,2},{1,3},{2,0},{3,1},{4,6},{5,7},{6,4},{7,5},{8,10},{9,11},{10,... | collective-permute-start | bytes 774152 | tf_op jit(solution)/shard_map/ppermute | solution.py:75
  778.8 20.4 %collective-permute-start.108 = (bf16[48,1664]{1,0:T(8,128)(2,1)S(1)}, bf16[48,1664]{1,0:T(8,128)(2,1)S(1)}, u32[]{:S(2)}, u32[]{:S(2)}) collective-permute-start(bf16[48,1664]{1,0:T(8,128)(2,1)S(1)} %get-tuple-element.394), channel_id=1, source_target_pairs={{0,4},{1,5},{2,6},{3,7},{4,0},{5,1},{6,2},{7,3},{8,12},{9,13},{10,... | collective-permute-start | bytes 479240 | tf_op jit(solution)/shard_map/ppermute | solution.py:75
  (212 other events, 1821.0 us)
